TPU v7x, 32 devices: a whole 2x2x4 slice. The times are simulated.
32 devices in a mesh: fsdp: 2 (over core), ctx: 16 (over z, y, x).
Axes of the slice: x: 2, y: 2, z: 4, core: 2. Of those that a mesh axis runs over, the one named last changes fastest.
Arguments:
- token_ids: int32 [2, 2048], P('fsdp', 'ctx'), may hold values from 0 to 511
- embedding: bfloat16 [512, 4096], P(None, 'fsdp'), may hold values from -5 to 5
- conv_taps: float32 [3, 3, 4096], replicated, may hold values from -2.5 to 2.5
- residues: float32 [4096, 16], replicated, may hold values from -1.2 to 1.2
- decays: float32 [4096, 16], replicated, may hold values from 9.765625e-06 to 0.05
- filter_seed: int32 [4096, 16], replicated, may hold values from 0 to 4095
- skip_gain: float32 [4096], replicated, may hold values from 0.5 to 1.5
- cotangent: float32 [2, 4096, 2048], P('fsdp', None, 'ctx'), may hold values from -6 to 6
Outputs:
- mixer_out: float32 [2, 4096, 2048], P('fsdp', None, 'ctx')
- embed_grad: float32 [512, 4096], P(None, 'fsdp')
All inputs are finite; a program needn't handle non-finite values.
Results may differ from a plain program's by a relative error of at most 0.0006.
Values may be sent and summed in bfloat16 or wider, within the bound.
No kernel may reach another device: no remote copies, remote signals or barrier semaphores. Data moves between devices by JAX's collectives and lax.ppermute only.
A program may use at most 320 MiB of HBM per device.

v0:
```python
import math

import jax
import jax.numpy as jnp
from jax import lax
from jax.sharding import PartitionSpec as P

PERIOD = 4096


HIGHEST = lax.Precision.HIGHEST
TWO_PI = 2.0 * math.pi


def from_behind(value, axis, steps):
    count = lax.axis_size(axis)
    leading, last = (max(0, -steps), min(count, count - steps))
    return lax.ppermute(value, axis, [(source, source + steps) for source in range(leading, last)])


def dft_tables(half_blocks, tok_block):
    full_blocks = 2 * half_blocks
    total_len = full_blocks * tok_block
    outer = (
        jnp.arange(half_blocks, dtype=jnp.int32)[:, None]
        * jnp.arange(full_blocks, dtype=jnp.int32)[None, :]
        % full_blocks
    )
    outer_angle = TWO_PI / full_blocks * outer.astype(jnp.float32)
    twist = (
        jnp.arange(full_blocks, dtype=jnp.int32)[:, None]
        * jnp.arange(tok_block, dtype=jnp.int32)[None, :]
        % total_len
    )
    twist_angle = TWO_PI / total_len * twist.astype(jnp.float32)
    inner = (
        jnp.arange(tok_block, dtype=jnp.int32)[:, None]
        * jnp.arange(tok_block, dtype=jnp.int32)[None, :]
        % tok_block
    )
    inner_angle = TWO_PI / tok_block * inner.astype(jnp.float32)
    return (
        jnp.cos(outer_angle),
        jnp.sin(outer_angle),
        jnp.cos(twist_angle),
        jnp.sin(twist_angle),
        jnp.cos(inner_angle),
        jnp.sin(inner_angle),
    )


def forward_dft(blocks, tables):
    outer_cos, outer_sin, twist_cos, twist_sin, inner_cos, inner_sin = tables
    part_real = jnp.einsum("bcst,sk->bckt", blocks, outer_cos, precision=HIGHEST)
    part_imag = -jnp.einsum("bcst,sk->bckt", blocks, outer_sin, precision=HIGHEST)
    turned_real = part_real * twist_cos + part_imag * twist_sin
    turned_imag = part_imag * twist_cos - part_real * twist_sin
    spec_real = jnp.einsum("bckt,tm->bckm", turned_real, inner_cos, precision=HIGHEST) + jnp.einsum(
        "bckt,tm->bckm", turned_imag, inner_sin, precision=HIGHEST
    )
    spec_imag = jnp.einsum("bckt,tm->bckm", turned_imag, inner_cos, precision=HIGHEST) - jnp.einsum(
        "bckt,tm->bckm", turned_real, inner_sin, precision=HIGHEST
    )
    return (spec_real, spec_imag)


def inverse_dft(prod_real, prod_imag, tables):
    outer_cos, outer_sin, twist_cos, twist_sin, inner_cos, inner_sin = tables
    total_len = outer_cos.shape[1] * inner_cos.shape[0]
    back_real = jnp.einsum("bckm,tm->bckt", prod_real, inner_cos, precision=HIGHEST) - jnp.einsum(
        "bckm,tm->bckt", prod_imag, inner_sin, precision=HIGHEST
    )
    back_imag = jnp.einsum("bckm,tm->bckt", prod_imag, inner_cos, precision=HIGHEST) + jnp.einsum(
        "bckm,tm->bckt", prod_real, inner_sin, precision=HIGHEST
    )
    turned_real = back_real * twist_cos - back_imag * twist_sin
    turned_imag = back_imag * twist_cos + back_real * twist_sin
    signal = jnp.einsum("bckt,sk->bcst", turned_real, outer_cos, precision=HIGHEST) - jnp.einsum(
        "bckt,sk->bcst", turned_imag, outer_sin, precision=HIGHEST
    )
    return signal / total_len


def apply_filter(spread, kernel_real, kernel_imag, tables, adjoint_sign):
    batch_rows = spread.shape[0]
    slab_size = spread.shape[1]
    half_blocks = tables[0].shape[0]
    tok_block = tables[4].shape[0]
    spec_real, spec_imag = forward_dft(
        spread.reshape(batch_rows, slab_size, half_blocks, tok_block), tables
    )
    prod_real = kernel_real * spec_real - adjoint_sign * kernel_imag * spec_imag
    prod_imag = kernel_real * spec_imag + adjoint_sign * kernel_imag * spec_real
    return inverse_dft(prod_real, prod_imag, tables).reshape(spread.shape)


def body(token_ids, embedding, conv_taps, residues, decays, filter_seed, skip_gain, cotangent):
    ctx_size = lax.axis_size("ctx")
    ctx_rank = lax.axis_index("ctx")
    model_width = conv_taps.shape[2]
    vocab_size = embedding.shape[0]
    tok_block = token_ids.shape[1]
    full_table = lax.all_gather(embedding, "fsdp", axis=1, tiled=True)
    gain_local = skip_gain[:, None]
    signal = jnp.swapaxes(jnp.take(full_table, token_ids, axis=0), 1, 2)
    before = from_behind(signal[:, :, tok_block - 2 :], "ctx", 1)
    extended = jnp.concatenate([before, signal], axis=2).astype(jnp.float32)

    def causal_mix(tap_set):
        return (
            tap_set[0][:, None] * extended[:, :, 2:]
            + tap_set[1][:, None] * extended[:, :, 1 : tok_block + 1]
            + tap_set[2][:, None] * extended[:, :, :tok_block]
        )

    query_stream = causal_mix(conv_taps[0])
    key_stream = causal_mix(conv_taps[1])
    value_stream = causal_mix(conv_taps[2])
    mixed_in = key_stream * value_stream
    grad_long = cotangent * query_stream
    seq_len = tok_block * ctx_size
    slab_size = model_width // ctx_size
    slab_start = ctx_rank * slab_size
    positions = jnp.arange(seq_len, dtype=jnp.int32)
    decay_rate = lax.dynamic_slice_in_dim(decays, slab_start, slab_size, 0)[:, :, None]
    seed_part = lax.dynamic_slice_in_dim(filter_seed, slab_start, slab_size, 0)[:, :, None]
    residue_part = lax.dynamic_slice_in_dim(residues, slab_start, slab_size, 0)[:, :, None]
    phase_int = seed_part * positions[None, None, :] % PERIOD
    weight = residue_part * jnp.sqrt(decay_rate + 1.0 / seq_len)
    kernel = jnp.sum(
        weight
        * jnp.exp(-decay_rate * positions.astype(jnp.float32)[None, None, :])
        * jnp.cos(TWO_PI / PERIOD * phase_int.astype(jnp.float32)),
        axis=1,
    )
    tables = dft_tables(ctx_size, tok_block)
    kernel_real, kernel_imag = forward_dft(
        kernel.reshape(1, slab_size, ctx_size, tok_block), tables
    )
    spread_mix, spread_grad = (
        lax.all_to_all(mixed_in, "ctx", split_axis=1, concat_axis=2, tiled=True),
        lax.all_to_all(grad_long, "ctx", split_axis=1, concat_axis=2, tiled=True),
    )
    conv_part = apply_filter(spread_mix, kernel_real, kernel_imag, tables, 1.0)
    corr_part = apply_filter(spread_grad, kernel_real, kernel_imag, tables, -1.0)
    conv_out, correlated = (
        lax.all_to_all(conv_part, "ctx", split_axis=2, concat_axis=1, tiled=True),
        lax.all_to_all(corr_part, "ctx", split_axis=2, concat_axis=1, tiled=True),
    )
    long_out = conv_out + gain_local * mixed_in
    mixer_local = query_stream * long_out
    grad_query = cotangent * long_out
    grad_mixed = correlated + gain_local * grad_long
    grad_key = grad_mixed * value_stream
    grad_value = grad_mixed * key_stream

    def tap_term(tap_index):
        return (
            conv_taps[0][tap_index][:, None] * grad_query
            + conv_taps[1][tap_index][:, None] * grad_key
            + conv_taps[2][tap_index][:, None] * grad_value
        )

    first_term = tap_term(0)
    second_term = tap_term(1)
    third_term = tap_term(2)
    next_rows = from_behind(jnp.stack([second_term[:, :, :2], third_term[:, :, :2]]), "ctx", -1)
    grad_signal = (
        first_term
        + jnp.concatenate([second_term, next_rows[0]], axis=2)[:, :, 1 : tok_block + 1]
        + jnp.concatenate([third_term, next_rows[1]], axis=2)[:, :, 2 : tok_block + 2]
    )
    one_hot = (
        token_ids[:, :, None] == jnp.arange(vocab_size, dtype=jnp.int32)[None, None, :]
    ).astype(jnp.float32)
    partial_grad = jnp.einsum("btv,bct->vc", one_hot, grad_signal, precision=HIGHEST)
    half_grad = lax.psum_scatter(partial_grad, "fsdp", scatter_dimension=1, tiled=True)
    embed_grad = lax.psum(half_grad, "ctx")
    return (mixer_local, embed_grad)


def solution(mesh):
    placed = (P("fsdp", "ctx"), P(None, "fsdp"), P(), P(), P(), P(), P(), P("fsdp", None, "ctx"))
    return jax.shard_map(
        body,
        mesh=mesh,
        in_specs=placed,
        out_specs=(P("fsdp", None, "ctx"), P(None, "fsdp")),
        check_vma=False,
    )
```

profile of v0, /device:TPU:0, one launch (start us, length us, event | category | flops | bytes accessed | tf_op | source)
XLA Modules:
  0.0 807.3 jit_solution(14465913909398879539)
XLA Ops:
  9.2 16.7 %all-gather.2.cloned.1.call-done = bf16[512,4096]{1,0:T(8,128)(2,1)} async-done(((bf16[512,2048]{1,0:T(8,128)(2,1)}), bf16[512,4096]{1,0:T(8,128)(2,1)}) %all-gather.2.cloned.1.call-update) | async-done | bytes 4194320 | tf_op jit(solution)/shard_map/all_gather | solution.py:103
  26.0 4.9 gather_fusion
  31.7 4.2 collective-permute-start
  36.0 1.9 copy.109
  38.0 1.1 maximum_convert_fusion
  39.0 4.8 fusion.327
  43.8 5.6 copy.111
  49.5 6.4 all-to-all-start.2
  57.0 5.7 copy.97
  62.6 35.9 %all-to-all-done.2 = f32[1,4096,128]{2,0,1:T(1,128)S(1)} async-done(((f32[1,4096,128]{2,0,1:T(1,128)}), f32[1,4096,128]{2,0,1:T(1,128)S(1)}, u32[]{:S(2)}, u32[]{:S(2)}) %all-to-all-start.2) | async-done | bytes 2097184 | tf_op jit(solution)/shard_map/all_to_all | solution.py:142
  98.5 10.3 %all-to-all-start = ((f32[1,4096,128]{2,0,1:T(1,128)}), f32[1,4096,128]{2,0,1:T(1,128)}, u32[]{:S(2)}, u32[]{:S(2)}) async-start(f32[1,4096,128]{2,0,1:T(1,128)} %copy.97), calls=%async_computation | async-start | bytes 4194304 | tf_op jit(solution)/shard_map/all_to_all | solution.py:141
  108.9 135.0 %fusion.5 = f32[256,2048]{1,0:T(8,128)S(1)} fusion(s32[256,16]{1,0:T(8,128)S(1)} %copy.94, f32[2048]{0:T(1024)S(1)} %iota_convert_fusion, f32[256,16]{1,0:T(8,128)S(1)} %copy.93, f32[256,16]{1,0:T(8,128)S(1)} %copy.92), kind=kLoop, calls=%fused_computation.9 | loop fusion | flops 150470656 | bytes 2154496 | tf_op jit(solution)/shard_map/reduce_sum | solution.py:130
  244.4 5.2 fusion.176
  249.6 6.7 fusion.79
  256.3 6.8 fusion.81
  263.1 7.4 fusion.83
  270.5 7.5 fusion.85
  278.0 14.0 %fusion.10 = (f32[256,32,128]{2,1,0:T(8,128)}, f32[256,32,128]{2,1,0:T(8,128)}, f32[256,32,128]{2,1,0:T(8,128)}, f32[256,32,128]{2,1,0:T(8,128)}, f32[256,32,128]{2,1,0:T(8,128)}, /*index=5*/f32[256,32,128]{2,1,0:T(8,128)S(1)}) fusion(f32[32,256,128]{2,0,1:T(8,128)} %fusion.81, f32[32,256,128]{2,0,1:T(8,128)} %fusion.79, ...), kind=kOutput, calls=%fused_computation.16 | convolution fusion | flops 223353856 | bytes 48267264 | tf_op jit(solution)/shard_map/bcst,sk->bckt/dot_general | solution.py:54
  292.0 9.2 %fusion.29 = f32[256,32,128]{2,0,1:T(8,128)S(1)} fusion(f32[256,32,128]{2,1,0:T(8,128)} %get-tuple-element.26), kind=kOutput, calls=%fused_computation.53 | convolution fusion | flops 1610842112 | bytes 8388608 | tf_op jit(solution)/shard_map/bckt,tm->bckm/dot_general | solution.py:61
  301.2 8.8 %fusion.31 = f32[256,32,128]{2,0,1:T(8,128)} fusion(f32[256,32,128]{2,1,0:T(8,128)S(1)} %copy-done.5), kind=kOutput, calls=%fused_computation.55 | convolution fusion | flops 1610842112 | bytes 8388608 | tf_op jit(solution)/shard_map/bckt,tm->bckm/dot_general | solution.py:58
  310.0 7.0 fusion.37
  317.0 7.2 fusion.39
  324.3 7.0 fusion.45
  331.3 7.4 fusion.47
  338.7 8.5 %fusion.59 = f32[256,32,128]{2,0,1:T(8,128)} fusion(f32[256,32,128]{2,0,1:T(8,128)S(1)} %fusion.39, f32[256,32,128]{2,1,0:T(8,128)S(1)} %copy-done.2), kind=kOutput, calls=%fused_computation.79 | convolution fusion | flops 1611890688 | bytes 12582912 | tf_op jit(solution)/shard_map/bckt,tm->bckm/dot_general | solution.py:58
  347.2 8.5 %fusion.62 = f32[256,32,128]{2,0,1:T(8,128)} fusion(f32[256,32,128]{2,0,1:T(8,128)S(1)} %fusion.37, f32[256,32,128]{2,1,0:T(8,128)S(1)} %copy-done.2), kind=kOutput, calls=%fused_computation.80 | convolution fusion | flops 1611890688 | bytes 12582912 | tf_op jit(solution)/shard_map/bckt,tm->bckm/dot_general | solution.py:61
  355.7 8.6 %fusion.53 = f32[256,32,128]{2,0,1:T(8,128)} fusion(f32[256,32,128]{2,0,1:T(8,128)S(1)} %fusion.47, f32[256,32,128]{2,1,0:T(8,128)S(1)} %get-tuple-element.56), kind=kOutput, calls=%fused_computation.77 | convolution fusion | flops 1611890688 | bytes 12582912 | tf_op jit(solution)/shard_map/bckt,tm->bckm/dot_general | solution.py:58
  364.3 8.5 %fusion.56 = f32[256,32,128]{2,0,1:T(8,128)} fusion(f32[256,32,128]{2,0,1:T(8,128)S(1)} %fusion.45, f32[256,32,128]{2,1,0:T(8,128)S(1)} %get-tuple-element.56), kind=kOutput, calls=%fused_computation.78 | convolution fusion | flops 1611890688 | bytes 12582912 | tf_op jit(solution)/shard_map/bckt,tm->bckm/dot_general | solution.py:61
  372.8 8.5 %fusion.68 = f32[256,32,128]{2,0,1:T(8,128)} fusion(f32[256,32,128]{2,0,1:T(8,128)S(1)} %fusion.29, f32[256,32,128]{2,1,0:T(8,128)S(1)} %copy-done.6), kind=kOutput, calls=%fused_computation.82 | convolution fusion | flops 1611890688 | bytes 12582912 | tf_op jit(solution)/shard_map/bckt,tm->bckm/dot_general | solution.py:61
  381.4 16.6 %multiply_add_fusion.1 = (f32[256,32,128]{2,0,1:T(8,128)}, f32[256,32,128]{2,0,1:T(8,128)}, f32[256,32,128]{2,0,1:T(8,128)}, f32[256,32,128]{2,0,1:T(8,128)}) fusion(f32[256,32,128]{2,0,1:T(8,128)} %fusion.53, f32[256,32,128]{2,0,1:T(8,128)} %fusion.68, f32[256,32,128]{2,0,1:T(8,128)} %fusion.56, f32[256,32,128]{2,0,1:T(8,128)} %fusion.62, ...), kind=kOutput, calls=%fused_computation.47 | convolution fusion | flops 1625522176 | bytes 46137344 | tf_op jit(solution)/shard_map/bckt,tm->bckm/dot_general | solution.py:58
  398.0 7.6 fusion.124
  405.6 3.8 fusion.126
  409.4 3.8 convolution_subtract_fusion
  413.2 3.8 fusion.132
  417.0 4.0 fusion.130
  421.0 3.8 convolution_subtract_fusion.1
  424.8 5.5 convolution_add_fusion.1
  430.3 11.7 %multiply_subtract_fusion = (f32[256,32,128]{2,0,1:T(8,128)}, f32[256,32,128]{2,0,1:T(8,128)}, f32[256,32,128]{2,0,1:T(8,128)}, f32[256,32,128]{2,0,1:T(8,128)}) fusion(f32[256,32,128]{2,0,1:T(8,128)S(1)} %convolution_subtract_fusion, f32[32,128]{1,0:T(8,128)S(1)} %get-tuple-element.57, f32[32,128]{1,0:T(8,128)S(1)} %get-tuple-element.58, ...), kind=kOutput, calls=%fused_computation.46 | convolution fusion | flops 1624473600 | bytes 37781504 | tf_op jit(solution)/shard_map/bckm,tm->bckt/dot_general | solution.py:73
  442.0 7.0 fusion.21
  449.0 5.9 multiply_bitcast_fusion
  454.9 1.7 reshape.388
  456.6 3.6 copy.119
  460.3 7.4 all-to-all-start.3
  467.7 7.0 fusion.25
  474.7 5.9 multiply_bitcast_fusion.1
  480.6 2.7 reshape.384
  483.3 6.0 copy.107
  489.3 20.3 %all-to-all-done.3 = f32[1,256,2048]{1,0,2:T(1,128)S(1)} async-done(((f32[1,256,2048]{1,0,2:T(1,128)}), f32[1,256,2048]{1,0,2:T(1,128)S(1)}, u32[]{:S(2)}, u32[]{:S(2)}) %all-to-all-start.3) | async-done | bytes 2097184 | tf_op jit(solution)/shard_map/all_to_all | solution.py:148
  509.6 9.8 %all-to-all-start.1 = ((f32[1,256,2048]{1,0,2:T(1,128)}), f32[1,256,2048]{1,0,2:T(1,128)}, u32[]{:S(2)}, u32[]{:S(2)}) async-start(f32[1,256,2048]{1,0,2:T(1,128)} %copy.107), calls=%async_computation.1 | async-start | bytes 4194304 | tf_op jit(solution)/shard_map/all_to_all | solution.py:147
  519.4 2.5 copy.191
  522.0 2.9 all_to_all.61
  524.8 37.2 %all-to-all-done.1 = f32[1,256,2048]{1,0,2:T(1,128)} async-done(((f32[1,256,2048]{1,0,2:T(1,128)}), f32[1,256,2048]{1,0,2:T(1,128)}, u32[]{:S(2)}, u32[]{:S(2)}) %all-to-all-start.1) | async-done | bytes 2097184 | tf_op jit(solution)/shard_map/all_to_all | solution.py:147
  562.1 4.3 copy.192
  566.3 2.8 all_to_all.54
  569.1 10.8 %multiply_add_fusion.5 = (f32[1,4096,128]{1,2,0:T(8,128)}, f32[1,4096,128]{1,2,0:T(8,128)}, f32[1,4096,128]{1,2,0:T(8,128)}, f32[1,4096,128]{1,2,0:T(8,128)}, f32[1,4096,128]{1,2,0:T(8,128)}) fusion(f32[4096]{0:T(1024)S(1)} %bitcast.263, f32[4096]{0:T(1024)S(1)} %bitcast.259, f32[4096]{0:T(1024)S(1)} %bitcast.261, f32[1,4096,128]{1,2,0:T(8,128)S(1)} %copy-done.15, ...), kind=kLoop, calls=%fused_computation.106 | loop fusion | flops 6815744 | bytes 27328512 | tf_op jit(solution)/shard_map/add | solution.py:159
  579.9 0.9 slice_bitcast_fusion.3
  580.9 3.5 multiply_add_fusion.4
  584.5 1.4 collective-permute-start.1
  585.9 4.9 collective-permute-done.1
  590.8 6.4 fusion.73
  597.3 22.5 %reduce-scatter.2.cloned.1.call-done = f32[512,2048]{1,0:T(8,128)} async-done(((f32[512,4096]{1,0:T(8,128)}), f32[512,2048]{1,0:T(8,128)}) %reduce-scatter.2.cloned.1.call-update) | async-done | bytes 4194320 | tf_op jit(solution)/shard_map/reduce_scatter | solution.py:177
  619.8 1.8 copy.121
  621.7 174.2 %all-reduce.2.cloned.1.call-done = f32[512,2048]{1,0:T(8,128)} async-done(((f32[512,2048]{1,0:T(8,128)}), f32[512,2048]{1,0:T(8,128)}) %all-reduce.2.cloned.1.call-update) | async-done | bytes 4194320 | tf_op jit(solution)/shard_map/psum | solution.py:178
  795.9 4.7 copy.194
  (77 shorter events, 4.8 us)
Async XLA Ops:
  7.2 49.6 %copy-start = (s32[4096,16]{0,1:T(8,128)S(1)}, s32[4096,16]{0,1:T(8,128)}, u32[]{:S(2)}) copy-start(s32[4096,16]{0,1:T(8,128)} %param.13) | copy-start | bytes 786436
  7.2 18.8 %all-gather.2.cloned.1.call-start = ((), (), s32[]{:S(2)}) async-start(), calls=%async_computation.5 | async-start | bytes 6291456 | tf_op jit(solution)/shard_map/all_gather | solution.py:103
  9.2 26.7 %copy-start.23 = (f32[3,3,4096]{2,1,0:T(4,128)S(1)}, f32[3,3,4096]{2,1,0:T(4,128)}, u32[]{:S(2)}) copy-start(f32[3,3,4096]{2,1,0:T(4,128)} %param.10) | copy-start | bytes 442372
  31.7 6.3 collective-permute-start
  38.0 5.9 copy-start.14
  49.5 49.1 %all-to-all-start.2 = ((f32[1,4096,128]{2,0,1:T(1,128)}), f32[1,4096,128]{2,0,1:T(1,128)S(1)}, u32[]{:S(2)}, u32[]{:S(2)}) async-start(f32[1,4096,128]{2,0,1:T(1,128)} %copy.111), calls=%async_computation.2 | async-start | bytes 4194304 | tf_op jit(solution)/shard_map/all_to_all | solution.py:142
  98.5 164.6 %all-to-all-start = ((f32[1,4096,128]{2,0,1:T(1,128)}), f32[1,4096,128]{2,0,1:T(1,128)}, u32[]{:S(2)}, u32[]{:S(2)}) async-start(f32[1,4096,128]{2,0,1:T(1,128)} %copy.97), calls=%async_computation | async-start | bytes 4194304 | tf_op jit(solution)/shard_map/all_to_all | solution.py:141
  244.3 12.0 %copy-start.12 = (f32[32,8,16,128]{3,2,1,0:T(8,128)}, f32[32,8,16,128]{3,2,1,0:T(8,128)S(1)}, u32[]{:S(2)}) copy-start(f32[32,8,16,128]{3,2,1,0:T(8,128)S(1)} %copy.122) | copy-start | bytes 6291460
  270.5 7.5 copy-start.13
  292.0 9.2 %copy-start.5 = (f32[256,32,128]{2,1,0:T(8,128)S(1)}, f32[256,32,128]{2,1,0:T(8,128)}, u32[]{:S(2)}) copy-start(f32[256,32,128]{2,1,0:T(8,128)} %get-tuple-element.26) | copy-start | bytes 12582916
  301.2 8.8 %copy-start.4 = (f32[256,32,128]{2,1,0:T(8,128)S(1)}, f32[256,32,128]{2,1,0:T(8,128)}, u32[]{:S(2)}) copy-start(f32[256,32,128]{2,1,0:T(8,128)} %get-tuple-element.53) | copy-start | bytes 12582916
  317.0 7.3 copy-start.3
  331.3 7.5 copy-start.2
  364.3 8.5 %copy-start.6 = (f32[256,32,128]{2,1,0:T(8,128)S(1)}, f32[256,32,128]{2,1,0:T(8,128)}, u32[]{:S(2)}) copy-start(f32[256,32,128]{2,1,0:T(8,128)} %get-tuple-element.25) | copy-start | bytes 12582916
  372.8 8.5 %copy-start.7 = (f32[256,32,128]{2,1,0:T(8,128)S(1)}, f32[256,32,128]{2,1,0:T(8,128)}, u32[]{:S(2)}) copy-start(f32[256,32,128]{2,1,0:T(8,128)} %get-tuple-element.25) | copy-start | bytes 12582916
  398.0 7.6 copy-start.11
  405.5 3.8 copy-start.10
  409.4 3.8 copy-start.8
  413.2 3.8 copy-start.9
  442.0 7.0 copy-start.20
  460.3 49.3 %all-to-all-start.3 = ((f32[1,256,2048]{1,0,2:T(1,128)}), f32[1,256,2048]{1,0,2:T(1,128)S(1)}, u32[]{:S(2)}, u32[]{:S(2)}) async-start(f32[1,256,2048]{1,0,2:T(1,128)} %copy.119), calls=%async_computation.3 | async-start | bytes 4194304 | tf_op jit(solution)/shard_map/all_to_all | solution.py:148
  467.7 7.0 copy-start.19
  509.6 52.5 %all-to-all-start.1 = ((f32[1,256,2048]{1,0,2:T(1,128)}), f32[1,256,2048]{1,0,2:T(1,128)}, u32[]{:S(2)}, u32[]{:S(2)}) async-start(f32[1,256,2048]{1,0,2:T(1,128)} %copy.107), calls=%async_computation.1 | async-start | bytes 4194304 | tf_op jit(solution)/shard_map/all_to_all | solution.py:147
  519.4 100.4 %reduce-scatter.2.cloned.1.call-start = ((), (), s32[]{:S(2)}) async-start(), calls=%async_computation.6 | async-start | bytes 12582912 | tf_op jit(solution)/shard_map/reduce_scatter | solution.py:177
  562.1 7.0 copy-start.15
  562.1 7.0 copy-start.24
  580.9 9.9 %copy-start.16 = (f32[1,4096,128]{1,2,0:T(8,128)S(1)}, f32[1,4096,128]{1,2,0:T(8,128)}, u32[]{:S(2)}) copy-start(f32[1,4096,128]{1,2,0:T(8,128)} %get-tuple-element.11) | copy-start | bytes 6291460
  580.9 9.9 %copy-start.17 = (f32[1,4096,128]{1,2,0:T(8,128)S(1)}, f32[1,4096,128]{1,2,0:T(8,128)}, u32[]{:S(2)}) copy-start(f32[1,4096,128]{1,2,0:T(8,128)} %get-tuple-element.12) | copy-start | bytes 6291460
  580.9 9.9 %copy-start.18 = (f32[1,4096,128]{1,2,0:T(8,128)S(1)}, f32[1,4096,128]{1,2,0:T(8,128)}, u32[]{:S(2)}) copy-start(f32[1,4096,128]{1,2,0:T(8,128)} %get-tuple-element.13) | copy-start | bytes 6291460
  580.9 9.9 %copy-start.21 = (f32[1,4096,128]{1,2,0:T(8,128)S(1)}, f32[1,4096,128]{1,2,0:T(8,128)}, u32[]{:S(2)}) copy-start(f32[1,4096,128]{1,2,0:T(8,128)} %get-tuple-element.10) | copy-start | bytes 6291460
  580.9 9.9 %copy-start.25 = (s32[1,128]{1,0:T(1,128)S(1)}, s32[1,128]{1,0:T(1,128)}, u32[]{:S(2)}) copy-start(s32[1,128]{1,0:T(1,128)} %param.8) | copy-start | bytes 1540
  584.5 6.3 collective-permute-start.1
  597.2 22.6 %copy-start.22 = (f32[1,4096,128]{1,2,0:T(8,128)S(1)}, f32[1,4096,128]{1,2,0:T(8,128)}, u32[]{:S(2)}) copy-start(f32[1,4096,128]{1,2,0:T(8,128)} %get-tuple-element.35) | copy-start | bytes 6291460
  597.2 198.6 %all-reduce.2.cloned.1.call-start = ((), (), s32[]{:S(2)}) async-start(), calls=%async_computation.7 | async-start | bytes 8388608 | tf_op jit(solution)/shard_map/psum | solution.py:178
  619.8 180.7 %copy-start.1 = (s32[4096,16]{0,1:T(8,128)S(1)}, s32[4096,16]{0,1:T(8,128)}, u32[]{:S(2)}) copy-start(s32[4096,16]{0,1:T(8,128)} %param.13) | copy-start | bytes 786436
Sparse Core Ops, SparseCore 0:
  9.6 16.3 all-gather.1
  597.4 22.4 reduce-scatter.1
  626.4 169.4 all-reduce.1
where the time goes:
time: 813 us; the launch traced here: 807 us
  waiting for transfers between devices  312 us (38%)
  matrix products  230 us (28%)
  other arithmetic  158 us (19%)
  local copies, waits for them, and re-layouts  53.7 us (7%)
  starting transfers between devices  39.7 us (5%)
  between operations  14.5 us (2%)
    psum x1, waiting for transfers between devices, body(): embed_grad = lax.psum(half_grad, 'ctx')  174 us
    reduce_sum x1, other arithmetic, body(): jnp.sum(weight * jnp.exp(-decay_rate * positions.astype(jnp.float32)[None...  135 us
    all_to_all x1, waiting for transfers between devices, body(): lax.all_to_all(conv_part, 'ctx', split_axis=2, concat_axis=1, tiled=True)  37.2 us
    all_to_all x1, waiting for transfers between devices, body(): lax.all_to_all(grad_long, 'ctx', split_axis=1, concat_axis=2, tiled=True)  35.9 us
    dot_general x3, matrix products, forward_dft(): jnp.einsum('bckt,tm->bckm', turned_real, inner_cos, precision=HIGHEST)  33.7 us
    dot_general x3, matrix products, forward_dft(): jnp.einsum('bcst,sk->bckt', blocks, outer_cos, precision=HIGHEST)  28.3 us
    dot_general x3, matrix products, forward_dft(): jnp.einsum('bckt,tm->bckm', turned_real, inner_sin, precision=HIGHEST)  25.5 us
    dot_general x3, matrix products, forward_dft(): jnp.einsum('bckt,tm->bckm', turned_imag, inner_sin, precision=HIGHEST)  23.5 us
  transfers between devices with their start and end apart: 9, of which 7 were waited for; matrix products, arithmetic and copies ran while one was open for 24% of the time, Pallas kernels for 0%

commit v1 on v0

v1 whole, which is shorter than its diff:
```python
import math

import jax
import jax.numpy as jnp
import ml_dtypes
import numpy as np
from jax import lax
from jax.experimental import pallas as pl
from jax.experimental.pallas import tpu as pltpu
from jax.sharding import PartitionSpec as P

PERIOD = 4096
LANES = 128
SUBLANES = 8
FULL = 32000.0
TINY = 2.0**-110
CODE = 1024.0
VMEM_BYTES = 56 * 1024 * 1024
F32 = jnp.float32
BF16 = jnp.bfloat16


def pack_pair(upper, lower):
    top = jnp.max(jnp.maximum(jnp.abs(upper), jnp.abs(lower)), axis=0, keepdims=True)
    code = jnp.ceil(jnp.log2(jnp.maximum(top, TINY)) * CODE)
    gain = FULL * jnp.exp2(code * (-1.0 / CODE))
    high = jnp.round(upper * gain).astype(jnp.int32)
    low = jnp.round(lower * gain).astype(jnp.int32)
    words = (high << 16) | (low & 0xFFFF)
    return words, jnp.broadcast_to(code.astype(jnp.int32), (SUBLANES, upper.shape[1]))


def unpack_pair(words, code):
    step = jnp.exp2(code.astype(F32) * (1.0 / CODE)) * (1.0 / FULL)
    return (
        (words >> 16).astype(F32) * step,
        ((words << 16) >> 16).astype(F32) * step,
    )


def plus(a, b):
    return b if a is None else a if b is None else a + b


def minus(a, b):
    return a if b is None else -b if a is None else a - b


def turn(re, im, top, bottom):
    top %= bottom
    if 8 * top % bottom == 0:
        eighth = 8 * top // bottom
        if eighth == 0:
            return re, im
        if eighth == 4:
            return -re, -im
        if eighth == 2:
            return im, -re
        if eighth == 6:
            return -im, re
        half = math.sqrt(0.5)
        if eighth == 1:
            return (re + im) * half, (im - re) * half
        if eighth == 5:
            return (re + im) * -half, (re - im) * half
        if eighth == 3:
            return (im - re) * half, (re + im) * -half
        return (re - im) * half, (re + im) * half
    angle = 2.0 * math.pi * top / bottom
    c, s = math.cos(angle), math.sin(angle)
    return re * c + im * s, im * c - re * s


def complex_dft(points):
    n = len(points)
    if n == 1:
        return points
    even, odd = complex_dft(points[::2]), complex_dft(points[1::2])
    out = [None] * n
    for k in range(n // 2):
        re, im = turn(*odd[k], k, n)
        out[k] = (even[k][0] + re, even[k][1] + im)
        out[k + n // 2] = (even[k][0] - re, even[k][1] - im)
    return out


def odd_part(diff, n):
    quarter = n // 4
    return complex_dft([turn(diff[s], -diff[s + quarter], s, n) for s in range(quarter)])


def place_odd(out, odd, n):
    for index, (re, im) in enumerate(odd):
        k = 4 * index + 1
        if k <= n // 2:
            out[k] = (re, im)
        else:
            out[n - k] = (re, -im)


def real_dft(x):
    n = len(x)
    if n == 1:
        return [(x[0], None)]
    if n == 2:
        return [(x[0] + x[1], None), (x[0] - x[1], None)]
    half = n // 2
    out = [None] * (half + 1)
    out[::2] = real_dft([x[s] + x[s + half] for s in range(half)])
    place_odd(out, odd_part([x[s] - x[s + half] for s in range(half)], n), n)
    return out


def padded_real_dft(x):
    n = 2 * len(x)
    out = [None] * (len(x) + 1)
    out[::2] = real_dft(x)
    place_odd(out, odd_part(x, n), n)
    return out


def odd_back(spectrum, n):
    quarter = n // 4
    points = []
    for index in range(quarter):
        k = 4 * index + 1
        re, im = spectrum[k] if k <= n // 2 else spectrum[n - k]
        points.append((im if k <= n // 2 else -im, re))
    waves = [(re, im) for im, re in complex_dft(points)]
    first, second = [], []
    for s, (re, im) in enumerate(waves):
        im, re = turn(im, re, s, n)
        first.append(re)
        second.append(-im)
    return first + second


def real_back(spectrum):
    n = 2 * (len(spectrum) - 1)
    if n == 2:
        a, b = spectrum[0][0], spectrum[1][0]
        return [a + b, a - b]
    even = real_back(spectrum[::2])
    odd = odd_back(spectrum, n)
    return [a + b for a, b in zip(even, odd)] + [a - b for a, b in zip(even, odd)]


def padded_real_back(spectrum):
    n = 2 * (len(spectrum) - 1)
    even = real_back(spectrum[::2])
    return [a + b for a, b in zip(even, odd_back(spectrum, n))]


def stacked(matrix):
    high = matrix.astype(ml_dtypes.bfloat16)
    low = (matrix - high.astype(np.float64)).astype(ml_dtypes.bfloat16)
    return np.concatenate([high, high, low], axis=0)


def transform_tables(blocks):
    total = 2 * blocks * LANES
    inner = np.arange(LANES)[:, None] * np.arange(LANES)[None, :] % LANES
    angle = 2.0 * np.pi / LANES * inner
    c, s = np.cos(angle), np.sin(angle)
    ahead = np.block([[c, -s], [s, c]])
    back = np.block([[c, s], [-s, c]]) * (2.0 / total)
    turns = np.arange(blocks + 1)[:, None] * np.arange(LANES)[None, :] % total
    angle = 2.0 * np.pi / total * turns
    weight = np.ones((blocks + 1, 1))
    weight[0] = weight[-1] = 0.5
    twist = np.stack([np.cos(angle), np.sin(angle), np.cos(angle) * weight, np.sin(angle) * weight], axis=1)
    return (
        jnp.asarray(stacked(ahead)),
        jnp.asarray(stacked(back)),
        jnp.asarray(np.pad(twist, ((0, 0), (0, 4), (0, 0))), F32),
    )


def split_dot(value, table):
    high = value.astype(BF16)
    low = (value - high.astype(F32)).astype(BF16)
    return jnp.dot(jnp.concatenate([high, low, high], axis=1), table, preferred_element_type=F32)


def inner_ahead(value, twist, table):
    re, im = value[:, :LANES], value[:, LANES:]
    c, s = twist[0:1], twist[1:2]
    turned = jnp.concatenate([re * c + im * s, im * c - re * s], axis=1)
    return split_dot(turned, table)


def inner_back(value, twist, table):
    out = split_dot(value, table)
    re, im = out[:, :LANES], out[:, LANES:]
    c, s = twist[2:3], twist[3:4]
    return jnp.concatenate([re * c - im * s, im * c + re * s], axis=1)


def store_spectrum(ref, rows, spectrum):
    for k, (re, im) in enumerate(spectrum):
        ref[k, rows, :LANES] = re
        ref[k, rows, LANES:] = jnp.zeros_like(re) if im is None else im


def load_spectrum(ref, rows, count):
    return [(ref[k, rows, :LANES], ref[k, rows, LANES:]) for k in range(count)]


def later(previous, current, steps, lane):
    moved = pltpu.roll(current, steps, 1)
    if previous is None:
        return jnp.where(lane < steps, 0.0, moved), moved
    return jnp.where(lane < steps, previous, moved), moved


def earlier(following, current, steps, lane):
    moved = pltpu.roll(current, LANES - steps, 1)
    kept = lane < LANES - steps
    if following is None:
        return jnp.where(kept, moved, 0.0), moved
    return jnp.where(kept, moved, following), moved


def shifted_blocks(x_ref, rows, blocks, lane):
    one = two = None
    for block in range(blocks):
        x = x_ref[block, rows, :]
        back_one, one = later(one, x, 1, lane)
        back_two, two = later(two, x, 2, lane)
        yield block, (x, back_one, back_two)


def column(values, index):
    return values[:, index : index + 1]


def mix(taps, stream, terms):
    return sum(taps[3 * stream + j] * terms[j] for j in range(3))


def wide_taps(tap_ref, rows):
    taps = tap_ref[rows, :]
    return [jnp.broadcast_to(column(taps, i), (SUBLANES, LANES)) for i in range(9)]


def for_tiles(channels, step):
    def run(tile, carry):
        step(pl.ds(pl.multiple_of(tile * SUBLANES, SUBLANES), SUBLANES))
        return carry

    lax.fori_loop(0, channels // SUBLANES, run, 0)


def unit_turn(phase):
    phase = phase & (PERIOD - 1)
    quadrant = (phase + PERIOD // 8) >> 10
    angle = (phase - (quadrant << 10)).astype(F32) * (2.0 * math.pi / PERIOD)
    square = angle * angle
    sin = angle * (1.0 + square * (-1.0 / 6 + square * (1.0 / 120 + square * (-1.0 / 5040 + square * (1.0 / 362880)))))
    cos = 1.0 + square * (-0.5 + square * (1.0 / 24 + square * (-1.0 / 720 + square * (1.0 / 40320))))
    swap = (quadrant & 1) == 1
    c = jnp.where(swap, sin, cos)
    s = jnp.where(swap, cos, sin)
    c = jnp.where(((quadrant + 1) & 2) == 2, -c, c)
    s = jnp.where((quadrant & 2) == 2, -s, s)
    return c, s


RESTART = 16


def filter_blocks(weights, decays, seeds, blocks, modes):
    position = lax.broadcasted_iota(jnp.int32, (SUBLANES, LANES), 1)
    time = position.astype(F32)
    leap_decay = jnp.exp(decays * (-1.0 * LANES))
    leap_cos, leap_sin = unit_turn(seeds * LANES)
    leap_re, leap_im = leap_decay * leap_cos, leap_decay * leap_sin
    twice, size = 2.0 * leap_re, leap_decay * leap_decay
    starts = []
    for start in range(0, blocks, RESTART):
        if start == 0:
            starts.append((weights, None))
        else:
            fall = weights * jnp.exp(decays * (-1.0 * LANES * start))
            c, s = unit_turn(seeds * (LANES * start))
            starts.append((fall * c, fall * s))
    total = [None] * blocks
    for mode in range(modes):
        c, s = unit_turn(column(seeds, mode) * position)
        fall = jnp.exp(-column(decays, mode) * time)
        base_re, base_im = fall * c, fall * s
        wide = lambda v: jnp.broadcast_to(column(v, mode), (SUBLANES, LANES))
        jump_re, jump_im, ahead, behind = wide(leap_re), wide(leap_im), wide(twice), wide(size)
        for index, (start_re, start_im) in enumerate(starts):
            first = index * RESTART
            re, im = base_re, base_im
            if start_im is None:
                w = wide(start_re)
                re, im = w * re, w * im
            else:
                a, b = wide(start_re), wide(start_im)
                re, im = a * re - b * im, a * im + b * re
            old, new = re, jump_re * re - jump_im * im
            total[first] = plus(total[first], old)
            for block in range(first + 1, min(first + RESTART, blocks)):
                total[block] = plus(total[block], new)
                old, new = new, ahead * new - behind * old
    return total


def encode_kernel(value_ref, out_ref):
    height = value_ref.shape[2]
    words, code = pack_pair(value_ref[0, 0], value_ref[1, 0])
    out_ref[0, :height, :] = words
    out_ref[0, height:, :] = code


def decode_kernel(words_ref, out_ref):
    height = out_ref.shape[2]
    out_ref[0, 0], out_ref[1, 0] = unpack_pair(words_ref[0, :height, :], words_ref[0, height : height + 1, :])


def encode(value, blocks):
    half = value.shape[0] // 2 // blocks
    return pl.pallas_call(
        encode_kernel,
        grid=(blocks,),
        in_specs=[pl.BlockSpec((2, 1, half, LANES), lambda i: (0, i, 0, 0))],
        out_specs=pl.BlockSpec((1, half + SUBLANES, LANES), lambda i: (i, 0, 0)),
        out_shape=jax.ShapeDtypeStruct((blocks, half + SUBLANES, LANES), jnp.int32),
        name="encode_cotangent",
    )(value.reshape(2, blocks, half, LANES))


def decode(words, blocks):
    half = words.shape[1] - SUBLANES
    out = pl.pallas_call(
        decode_kernel,
        grid=(blocks,),
        in_specs=[pl.BlockSpec((1, half + SUBLANES, LANES), lambda i: (i, 0, 0))],
        out_specs=pl.BlockSpec((2, 1, half, LANES), lambda i: (0, i, 0, 0)),
        out_shape=jax.ShapeDtypeStruct((2, blocks, half, LANES), F32),
        name="decode_mixer",
    )(words)
    return out.reshape(2 * blocks * half, LANES)


def pack_table_kernel(mine_ref, other_ref, out_ref):
    total = mine_ref[...] + other_ref[...]
    half = total.shape[0] // 2
    words, code = pack_pair(total[:half], total[half:])
    out_ref[:half, :] = words
    out_ref[half:, :] = code


def unpack_table_kernel(words_ref, out_ref):
    half = out_ref.shape[0] // 2
    upper, lower = unpack_pair(words_ref[0, :half, :], words_ref[0, half : half + 1, :])
    out_ref[:half, :] = upper
    out_ref[half:, :] = lower


def one_hot_block(token_ref, block, vocab):
    wanted = token_ref[pl.ds(block, 1), :]
    entry = lax.broadcasted_iota(jnp.int32, (vocab, LANES), 0)
    return (entry == wanted).astype(F32).astype(BF16)


def forward_kernel(
    table_ref, token_ref, tap_ref, residue_ref, decay_ref, seed_ref, gain_ref, ahead_ref, back_ref, twist_ref,
    words_ref, response_ref, long_ref, x_ref,
    work_ref, mixed_ref, query_ref,
):
    blocks, channels, _ = x_ref.shape
    half = channels // 2
    vocab = table_ref.shape[1]
    modes = residue_ref.shape[1]
    tall = jnp.concatenate([table_ref[0].astype(F32).T, table_ref[1].astype(F32).T], axis=0).astype(BF16)

    @pl.loop(0, blocks // 2)
    def _(pair):
        hot = jnp.concatenate([one_hot_block(token_ref, 2 * pair + i, vocab) for i in range(2)], axis=1)
        found = jnp.dot(tall, hot, preferred_element_type=F32)
        x_ref[2 * pair] = found[:, :LANES]
        x_ref[2 * pair + 1] = found[:, LANES:]

    def filters(rows):
        decays = decay_ref[rows, :]
        weights = residue_ref[rows, :] * jnp.sqrt(decays + 1.0 / (blocks * LANES))
        taken = filter_blocks(weights, decays, seed_ref[rows, :], blocks, modes)
        store_spectrum(response_ref, rows, padded_real_dft(taken))

    def streams(rows):
        lane = lax.broadcasted_iota(jnp.int32, (SUBLANES, LANES), 1)
        taps = wide_taps(tap_ref, rows)
        mixed = []
        for block, terms in shifted_blocks(x_ref, rows, blocks, lane):
            query_ref[block, rows, :] = mix(taps, 0, terms)
            mixed.append(mix(taps, 1, terms) * mix(taps, 2, terms))
            mixed_ref[block, rows, :] = mixed[-1]
        store_spectrum(work_ref, rows, padded_real_dft(mixed))

    for_tiles(channels, filters)
    for_tiles(channels, streams)

    @pl.loop(0, blocks + 1)
    def _(k):
        twist = twist_ref[k]
        response = inner_ahead(response_ref[k], twist, ahead_ref[...])
        response_ref[k] = response
        spectrum = inner_ahead(work_ref[k], twist, ahead_ref[...])
        a, b = response[:, :LANES], response[:, LANES:]
        c, d = spectrum[:, :LANES], spectrum[:, LANES:]
        product = jnp.concatenate([a * c - b * d, a * d + b * c], axis=1)
        work_ref[k] = inner_back(product, twist, back_ref[...])

    def results(rows):
        conv = padded_real_back(load_spectrum(work_ref, rows, blocks + 1))
        gain = jnp.broadcast_to(gain_ref[rows, :], (SUBLANES, LANES))
        for block in range(blocks):
            long_out = conv[block] + gain * mixed_ref[block, rows, :]
            long_ref[block, rows, :] = long_out
            query_ref[block, rows, :] = query_ref[block, rows, :] * long_out

    for_tiles(channels, results)

    @pl.loop(0, blocks)
    def _(block):
        words, code = pack_pair(query_ref[block, :half, :], query_ref[block, half:, :])
        words_ref[block, :half, :] = words
        words_ref[block, half:, :] = code


def backward_kernel(
    words_ref, x_ref, long_ref, response_ref, token_ref, tap_ref, gain_ref, ahead_ref, back_ref, twist_ref,
    grad_ref,
    work_ref, cot_ref, late_ref,
):
    blocks, channels, _ = x_ref.shape
    half = channels // 2
    vocab = grad_ref.shape[1]

    @pl.loop(0, blocks)
    def _(block):
        upper, lower = unpack_pair(words_ref[block, :half, :], words_ref[block, half : half + 1, :])
        cot_ref[block, :half, :] = upper
        cot_ref[block, half:, :] = lower

    def streams(rows):
        lane = lax.broadcasted_iota(jnp.int32, (SUBLANES, LANES), 1)
        taps = wide_taps(tap_ref, rows)
        long_grad = []
        for block, terms in shifted_blocks(x_ref, rows, blocks, lane):
            long_grad.append(cot_ref[block, rows, :] * mix(taps, 0, terms))
            late_ref[block, rows, :] = long_grad[-1]
        store_spectrum(work_ref, rows, padded_real_dft(long_grad))

    for_tiles(channels, streams)

    @pl.loop(0, blocks + 1)
    def _(k):
        twist = twist_ref[k]
        spectrum = inner_ahead(work_ref[k], twist, ahead_ref[...])
        a, b = response_ref[k, :, :LANES], response_ref[k, :, LANES:]
        c, d = spectrum[:, :LANES], spectrum[:, LANES:]
        product = jnp.concatenate([a * c + b * d, a * d - b * c], axis=1)
        work_ref[k] = inner_back(product, twist, back_ref[...])

    def results(rows):
        lane = lax.broadcasted_iota(jnp.int32, (SUBLANES, LANES), 1)
        taps = wide_taps(tap_ref, rows)
        gain = jnp.broadcast_to(gain_ref[rows, :], (SUBLANES, LANES))
        correlated = padded_real_back(load_spectrum(work_ref, rows, blocks + 1))
        for block in range(blocks):
            late_ref[block, rows, :] = correlated[block] + gain * late_ref[block, rows, :]
        held = None
        for block, terms in shifted_blocks(x_ref, rows, blocks, lane):
            mixed_grad = late_ref[block, rows, :]
            grads = (
                cot_ref[block, rows, :] * long_ref[block, rows, :],
                mixed_grad * mix(taps, 2, terms),
                mixed_grad * mix(taps, 1, terms),
            )
            now, next_one, next_two = (sum(taps[3 * s + j] * grads[s] for s in range(3)) for j in range(3))
            next_one = pltpu.roll(next_one, LANES - 1, 1)
            next_two = pltpu.roll(next_two, LANES - 2, 1)
            if held is not None:
                base, one, two = held
                late_ref[block - 1, rows, :] = (
                    base + jnp.where(lane < LANES - 1, one, next_one) + jnp.where(lane < LANES - 2, two, next_two)
                )
            held = (now, next_one, next_two)
        base, one, two = held
        late_ref[blocks - 1, rows, :] = (
            base + jnp.where(lane < LANES - 1, one, 0.0) + jnp.where(lane < LANES - 2, two, 0.0)
        )

    for_tiles(channels, results)

    def gather(block, total):
        hot = one_hot_block(token_ref, block, vocab)
        value = late_ref[block]
        high = value.astype(BF16)
        low = (value - high.astype(F32)).astype(BF16)
        return total + lax.dot_general(
            jnp.concatenate([hot, hot], axis=1),
            jnp.concatenate([high, low], axis=1),
            (((1,), (1,)), ((), ())),
            preferred_element_type=F32,
        )

    total = lax.fori_loop(0, blocks, gather, jnp.zeros((vocab, channels), F32))
    grad_ref[0] = total[:, :half]
    grad_ref[1] = total[:, half:]


def in_vmem(count):
    return [pl.BlockSpec(memory_space=pltpu.VMEM)] * count


def body(token_ids, embedding, conv_taps, residues, decays, filter_seed, skip_gain, cotangent):
    blocks = lax.axis_size("ctx")
    rank = lax.axis_index("ctx")
    side = lax.axis_index("fsdp")
    width = conv_taps.shape[2]
    vocab = embedding.shape[0]
    half = width // 2 // blocks
    channels = 2 * half
    modes = residues.shape[1]

    cot_words = lax.all_to_all(encode(cotangent[0], blocks), "ctx", split_axis=0, concat_axis=0, tiled=True)

    tokens = lax.all_gather(token_ids, "ctx", axis=0, tiled=True)
    own_columns = lax.dynamic_slice_in_dim(embedding, rank * half, half, 1)
    other_columns = lax.ppermute(own_columns, "fsdp", [(0, 1), (1, 0)])
    table = jnp.where(
        side == 0, jnp.stack([own_columns, other_columns]), jnp.stack([other_columns, own_columns])
    )

    def slab(value):
        parts = value.reshape(2, blocks, half, value.shape[1])
        return lax.dynamic_index_in_dim(parts, rank, 1, keepdims=False).reshape(channels, value.shape[1])

    taps = lax.dynamic_index_in_dim(conv_taps.reshape(9, 2, blocks, half), rank, 2, keepdims=False)
    taps = jnp.pad(taps.reshape(9, channels).T, ((0, 0), (0, 7)))
    gain = slab(skip_gain[:, None])
    ahead, back, twist = transform_tables(blocks)
    slots = blocks + 1
    stack = jax.ShapeDtypeStruct((blocks, channels, LANES), F32)
    params = pltpu.CompilerParams(vmem_limit_bytes=VMEM_BYTES)
    work = pltpu.VMEM((slots, channels, 2 * LANES), F32)
    buffer = pltpu.VMEM((blocks, channels, LANES), F32)

    mixer_words, response, long_out, x = pl.pallas_call(
        forward_kernel,
        in_specs=in_vmem(10),
        out_specs=tuple(in_vmem(4)),
        out_shape=(
            jax.ShapeDtypeStruct((blocks, half + SUBLANES, LANES), jnp.int32),
            jax.ShapeDtypeStruct((slots, channels, 2 * LANES), F32),
            stack,
            stack,
        ),
        scratch_shapes=[work, buffer, buffer],
        compiler_params=params,
        name="forward",
    )(table, tokens, taps, slab(residues), slab(decays), slab(filter_seed), gain, ahead, back, twist)

    mixer_words = lax.all_to_all(mixer_words, "ctx", split_axis=0, concat_axis=0, tiled=True)

    grads = pl.pallas_call(
        backward_kernel,
        in_specs=in_vmem(10),
        out_specs=in_vmem(1)[0],
        out_shape=jax.ShapeDtypeStruct((2, vocab, half), F32),
        scratch_shapes=[work, buffer, buffer],
        compiler_params=params,
        name="backward",
    )(cot_words, x, long_out, response, tokens, taps, gain, ahead, back, twist)

    mine = lax.dynamic_index_in_dim(grads, side, 0, keepdims=False)
    theirs = lax.dynamic_index_in_dim(grads, 1 - side, 0, keepdims=False)
    theirs = lax.ppermute(theirs, "fsdp", [(0, 1), (1, 0)])
    tall = vocab // 2 + SUBLANES
    grad_words = pl.pallas_call(
        pack_table_kernel,
        out_shape=jax.ShapeDtypeStruct((tall, half), jnp.int32),
        name="pack_table",
    )(mine, theirs)
    grad_words = lax.all_gather(grad_words, "ctx", axis=0, tiled=False)
    group = max(1, LANES // half)
    if group > 1:
        grad_words = grad_words.reshape(blocks // group, group, tall, half)
        grad_words = jnp.swapaxes(grad_words, 1, 2).reshape(blocks // group, tall, group * half)
    embed_grad = pl.pallas_call(
        unpack_table_kernel,
        grid=(blocks // group,),
        in_specs=[pl.BlockSpec((1, tall, group * half), lambda i: (i, 0, 0))],
        out_specs=pl.BlockSpec((vocab, group * half), lambda i: (0, i)),
        out_shape=jax.ShapeDtypeStruct((vocab, blocks * half), F32),
        name="unpack_table",
    )(grad_words)
    mixer_out = decode(mixer_words, blocks)
    return mixer_out[None], embed_grad


def solution(mesh):
    placed = (P("fsdp", "ctx"), P(None, "fsdp"), P(), P(), P(), P(), P(), P("fsdp", None, "ctx"))
    return jax.shard_map(
        body,
        mesh=mesh,
        in_specs=placed,
        out_specs=(P("fsdp", None, "ctx"), P(None, "fsdp")),
        check_vma=False,
    )
```

time: 813 us -> 241 us (0.30)
  waiting for transfers between devices: 312 us -> 13.6 us
  matrix products: 230 us -> 0 us
  other arithmetic: 158 us -> 1.7 us
  Pallas kernels: 0 us -> 102 us
  blocking collectives: 0 us -> 82.4 us
  local copies, waits for them, and re-layouts: 53.7 us -> 16.8 us
  starting transfers between devices: 39.7 us -> 8.36 us
    dot_general x31 -> x0, matrix products: 230 us -> none  [the longest x3 33.7 us: forward_dft(): jnp.einsum('bckt,tm->bckm', turned_real, inner_cos, precision=HIGHEST)]
    psum x1 -> x0, waiting for transfers between devices: 174 us -> none  [body(): embed_grad = lax.psum(half_grad, 'ctx')]
    reduce_sum x1 -> x0, other arithmetic: 135 us -> none  [body(): jnp.sum(weight * jnp.exp(-decay_rate * positions.astype(jnp.float32)[None...]
    pallas_call x0 -> x6, Pallas kernels: none -> 102 us  [the longest x1 38.9 us: body(): pl.pallas_call(forward_kernel, in_specs=in_vmem(10), out_specs=tuple(in_v...]
    all_to_all x4 -> x1, waiting for transfers between devices: 93.4 us -> 0.01 us  [body(): lax.all_to_all(encode(cotangent[0], blocks), 'ctx', split_axis=0, concat_...]
    all_gather x0 -> x1, blocking collectives: none -> 41.4 us  [body(): tokens = lax.all_gather(token_ids, 'ctx', axis=0, tiled=True)]
    all_to_all x0 -> x1, blocking collectives: none -> 41 us  [body(): lax.all_to_all(mixer_words, 'ctx', split_axis=0, concat_axis=0, tiled=True)]
    all_to_all x4 -> x1, starting transfers between devices: 33.9 us -> 8.31 us  [body(): lax.all_to_all(encode(cotangent[0], blocks), 'ctx', split_axis=0, concat_...]
  transfers between devices with their start and end apart: 9 -> 4, of which waited for: 7 -> 2; matrix products, arithmetic and copies ran while one was open for 24% -> 6% of each run, Pallas kernels for 0% -> 20%
where the time goes in v1:
time: 241 us; the launch traced here: 239 us
  Pallas kernels  102 us (42%)
  blocking collectives  82.4 us (34%)
  local copies, waits for them, and re-layouts  16.8 us (7%)
  between operations  14.1 us (6%)
  waiting for transfers between devices  13.6 us (6%)
  starting transfers between devices  8.36 us (3%)
    all_gather x1, blocking collectives, body(): tokens = lax.all_gather(token_ids, 'ctx', axis=0, tiled=True)  41.4 us
    all_to_all x1, blocking collectives, body(): lax.all_to_all(mixer_words, 'ctx', split_axis=0, concat_axis=0, tiled=True)  41 us
    pallas_call x1, Pallas kernels, body(): pl.pallas_call(forward_kernel, in_specs=in_vmem(10), out_specs=tuple(in_v...  38.9 us
    pallas_call x1, Pallas kernels, body(): pl.pallas_call(backward_kernel, in_specs=in_vmem(10), out_specs=in_vmem(1...  32.3 us
    all_gather x1, waiting for transfers between devices, body(): grad_words = lax.all_gather(grad_words, 'ctx', axis=0, tiled=False)  12 us
    pallas_call x1, Pallas kernels, body(): pl.pallas_call(unpack_table_kernel, grid=(blocks // group,), in_specs=[pl...  9.91 us
    pallas_call x1, Pallas kernels, encode(): pl.pallas_call(encode_kernel, grid=(blocks,), in_specs=[pl.BlockSpec((2,...  9.68 us
    pallas_call x1, Pallas kernels, decode(): pl.pallas_call(decode_kernel, grid=(blocks,), in_specs=[pl.BlockSpec((1,...  9.4 us
  transfers between devices with their start and end apart: 4, of which 2 were waited for; matrix products, arithmetic and copies ran while one was open for 6% of the time, Pallas kernels for 20%

profile of v1, /device:TPU:0, one launch (start us, length us, event | category | flops | bytes accessed | tf_op | source)
XLA Modules:
  0.0 239.0 jit_solution(12813655256749408482)
XLA Ops:
  7.2 0.0 copy-start
  7.2 0.0 copy-start.4
  7.2 9.7 %encode_cotangent.1 = s32[16,136,128]{2,1,0:T(8,128)} custom-call(f32[2,16,128,128]{3,2,1,0:T(8,128)} %bitcast.37), custom_call_target="tpu_custom_call" | custom-call | tf_op jit(solution)/shard_map/encode_cotangent/pallas_call | solution.py:325
  16.9 8.3 %all-to-all-start.1 = ((s32[16,136,128]{2,1,0:T(8,128)}), s32[16,136,128]{2,1,0:T(8,128)S(1)}, u32[]{:S(2)}, u32[]{:S(2)}) async-start(s32[16,136,128]{2,1,0:T(8,128)} %encode_cotangent.1), calls=%async_computation.1 | async-start | bytes 2228224 | tf_op jit(solution)/shard_map/all_to_all | solution.py:531
  25.2 0.0 copy-start.5
  25.2 0.0 all-gather.4.cloned.1.call-start
  25.3 0.0 copy-done
  25.3 0.7 constant_dynamic-slice_fusion.5
  26.0 0.0 collective-permute-start
  26.0 0.0 copy-done.4
  26.0 0.8 reshape.36
  26.7 1.0 copy.35
  27.7 1.7 copy.36
  29.4 1.7 copy.37
  31.1 0.9 constant_dynamic-slice_fusion.4
  32.0 0.9 constant_dynamic-slice_fusion.1
  33.0 0.9 constant_dynamic-slice_fusion.2
  33.9 0.7 fusion
  34.6 0.8 copy.29.gain_ref
  35.4 0.1 copy.31
  35.5 0.8 copy.33
  36.3 0.8 copy.32
  37.1 0.8 copy.34
  37.8 0.6 pad.4.tap_ref
  38.5 0.0 copy-done.5
  38.5 41.4 %all-gather.1 = s32[16,1,128]{2,1,0:T(1,128)} all-gather(s32[1,1,128]{2,1,0:T(1,128)S(1)} %bitcast.51), channel_id=1, replica_groups=mesh['fsdp'=2,'ctx'=16] {'ctx'}, dimensions={0}, use_global_device_ids=true | all-gather | bytes 8704 | tf_op jit(solution)/shard_map/all_gather | solution.py:533
  79.9 0.0 collective-permute-done
  79.9 1.7 maximum_select_fusion.table_ref
  81.6 38.9 %forward.1 = (s32[16,136,128]{2,1,0:T(8,128)}, f32[17,256,256]{2,1,0:T(8,128)}, f32[16,256,128]{2,1,0:T(8,128)}, f32[16,256,128]{2,1,0:T(8,128)}) custom-call(bf16[2,512,128]{2,1,0:T(8,128)(2,1)} %maximum_select_fusion.table_ref, s32[16,128]{1,0:T(8,128)} %bitcast.49, f32[256,16]{1,0:T(8,128)} %pad.4.tap_ref, f32[256,16]{1,0:T(8,128)} %bitcast.40, ...), custom_call_target="tpu_custom_call" | custom-call | tf_op jit(solution)/shard_map/forward/pallas_call | solution.py:554
  120.6 0.0 all-to-all-done.1.words_ref
  120.6 0.0 copy-start.1
  120.6 1.0 copy-done.1
  121.6 32.3 %backward.1 = f32[2,512,128]{2,1,0:T(8,128)} custom-call(s32[16,136,128]{2,1,0:T(8,128)} %copy-done.1, f32[16,256,128]{2,1,0:T(8,128)} %get-tuple-element.7.x_ref, f32[16,256,128]{2,1,0:T(8,128)} %get-tuple-element.8.long_ref, f32[17,256,256]{2,1,0:T(8,128)} %get-tuple-element.9.response_ref, s32[16,128]{1,0:T(8,128)} %bitcast.50, f32[256,16]{1,0:T(8,128)} %pad.4.tap_ref, ...), custom_call_target="tpu_custom_call" | custom-call | tf_op jit(solution)/shard_map/backward/pallas_call | solution.py:571
  153.9 0.0 copy-start.2
  153.9 1.9 dynamic-slice_bitcast_fusion
  155.8 0.0 collective-permute-start.1
  155.8 1.5 collective-permute-done.1.other_ref
  157.3 0.0 copy-start.3
  157.3 0.7 copy-done.3
  158.0 1.8 pack_table.1
  159.8 0.0 all-gather.4.cloned.1.call-update
  159.8 0.0 copy-done.2
  159.8 41.0 %all_to_all.10.words_ref = s32[16,136,128]{2,1,0:T(8,128)} all-to-all(s32[16,136,128]{2,1,0:T(8,128)S(1)} %copy-done.2), channel_id=1, replica_groups=mesh['fsdp'=2,'ctx'=16] {'ctx'}, dimensions={0} | all-to-all | bytes 2228224 | tf_op jit(solution)/shard_map/all_to_all | solution.py:569
  200.8 9.4 %decode_mixer.1 = f32[2,16,128,128]{3,2,1,0:T(8,128)} custom-call(s32[16,136,128]{2,1,0:T(8,128)} %all_to_all.10.words_ref), custom_call_target="tpu_custom_call" | custom-call | tf_op jit(solution)/shard_map/decode_mixer/pallas_call | solution.py:337
  210.2 12.0 %all-gather.4.cloned.1.call-done = s32[4224,128]{1,0:T(8,128)} async-done(((s32[264,128]{1,0:T(8,128)}), s32[4224,128]{1,0:T(8,128)}) %all-gather.4.cloned.1.call-update) | async-done | bytes 2162704 | tf_op jit(solution)/shard_map/all_gather | solution.py:590
  222.3 9.9 %unpack_table.1 = f32[512,2048]{1,0:T(8,128)} custom-call(s32[16,264,128]{2,1,0:T(8,128)} %bitcast.36), custom_call_target="tpu_custom_call" | custom-call | tf_op jit(solution)/shard_map/unpack_table/pallas_call | solution.py:595
  (1 shorter events, 0.0 us)
Async XLA Ops:
  7.2 18.1 %copy-start = (bf16[512,2048]{1,0:T(8,128)(2,1)S(1)}, bf16[512,2048]{1,0:T(8,128)(2,1)}, u32[]{:S(2)}) copy-start(bf16[512,2048]{1,0:T(8,128)(2,1)} %param.12) | copy-start | bytes 6291460
  7.2 18.8 %copy-start.4 = (f32[3,3,4096]{2,1,0:T(4,128)S(1)}, f32[3,3,4096]{2,1,0:T(4,128)}, u32[]{:S(2)}) copy-start(f32[3,3,4096]{2,1,0:T(4,128)} %param.13) | copy-start | bytes 442372
  16.9 103.7 %all-to-all-start.1 = ((s32[16,136,128]{2,1,0:T(8,128)}), s32[16,136,128]{2,1,0:T(8,128)S(1)}, u32[]{:S(2)}, u32[]{:S(2)}) async-start(s32[16,136,128]{2,1,0:T(8,128)} %encode_cotangent.1), calls=%async_computation.1 | async-start | bytes 2228224 | tf_op jit(solution)/shard_map/all_to_all | solution.py:531
  25.2 13.3 %copy-start.5 = (s32[1,128]{1,0:T(1,128)S(1)}, s32[1,128]{1,0:T(1,128)}, u32[]{:S(2)}) copy-start(s32[1,128]{1,0:T(1,128)} %param.11) | copy-start | bytes 1540
  25.2 197.1 %all-gather.4.cloned.1.call-start = ((), (), s32[]{:S(2)}) async-start(), calls=%async_computation.2 | async-start | bytes 2297856 | tf_op jit(solution)/shard_map/all_gather | solution.py:590
  26.0 54.0 %collective-permute-start = (bf16[512,128]{1,0:T(8,128)(2,1)}, bf16[512,128]{1,0:T(8,128)(2,1)}, u32[]{:S(2)}, u32[]{:S(2)}) collective-permute-start(bf16[512,128]{1,0:T(8,128)(2,1)} %constant_dynamic-slice_fusion.5), channel_id=1, source_target_pairs={{0,16},{16,0},{1,17},{17,1},{2,18},{18,2},{3,19},{19,3},{4,20},{20... | collective-permute-start | bytes 393224 | tf_op jit(solution)/shard_map/ppermute | solution.py:535
  120.6 1.0 copy-start.1
  153.9 5.9 %copy-start.2 = (s32[16,136,128]{2,1,0:T(8,128)S(1)}, s32[16,136,128]{2,1,0:T(8,128)}, u32[]{:S(2)}) copy-start(s32[16,136,128]{2,1,0:T(8,128)} %get-tuple-element.6) | copy-start | bytes 3342340
  155.8 1.5 collective-permute-start.1
  157.3 0.7 copy-start.3
Sparse Core Ops, SparseCore 0:
  159.9 62.3 all-gather.3

commit v2 on v1

--- a/solution.py
+++ b/solution.py
@@ -15,7 +15,7 @@
 FULL = 32000.0
 TINY = 2.0**-110
 CODE = 1024.0
-VMEM_BYTES = 56 * 1024 * 1024
+VMEM_BYTES = 60 * 1024 * 1024
 F32 = jnp.float32
 BF16 = jnp.bfloat16
 
@@ -238,9 +238,12 @@
     return sum(taps[3 * stream + j] * terms[j] for j in range(3))
 
 
-def wide_taps(tap_ref, rows):
-    taps = tap_ref[rows, :]
-    return [jnp.broadcast_to(column(taps, i), (SUBLANES, LANES)) for i in range(9)]
+def wide_column(ref, rows, index):
+    return jnp.broadcast_to(ref[rows, index : index + 1], (SUBLANES, LANES))
+
+
+def wide_taps(ref, rows):
+    return [wide_column(ref, rows, i) for i in range(9)]
 
 
 def for_tiles(channels, step):
@@ -308,41 +311,65 @@
     return total
 
 
+GAIN_COLUMN = 9
+UNROLLED = 32
+
+
+def over_slots(count, step):
+    if count <= UNROLLED:
+        for k in range(count):
+            step(k)
+    else:
+        pl.loop(0, count)(step)
+
+
 def encode_kernel(value_ref, out_ref):
     height = value_ref.shape[2]
-    words, code = pack_pair(value_ref[0, 0], value_ref[1, 0])
-    out_ref[0, :height, :] = words
-    out_ref[0, height:, :] = code
+    for i in range(value_ref.shape[1]):
+        words, code = pack_pair(value_ref[0, i], value_ref[1, i])
+        out_ref[i, :height, :] = words
+        out_ref[i, height:, :] = code
 
 
 def decode_kernel(words_ref, out_ref):
     height = out_ref.shape[2]
-    out_ref[0, 0], out_ref[1, 0] = unpack_pair(words_ref[0, :height, :], words_ref[0, height : height + 1, :])
+    for i in range(out_ref.shape[1]):
+        upper, lower = unpack_pair(words_ref[i, :height, :], words_ref[i, height : height + 1, :])
+        out_ref[0, i] = upper
+        out_ref[1, i] = lower
 
 
 def encode(value, blocks):
     half = value.shape[0] // 2 // blocks
+    some = blocks // 4
     return pl.pallas_call(
         encode_kernel,
-        grid=(blocks,),
-        in_specs=[pl.BlockSpec((2, 1, half, LANES), lambda i: (0, i, 0, 0))],
-        out_specs=pl.BlockSpec((1, half + SUBLANES, LANES), lambda i: (i, 0, 0)),
+        grid=(blocks // some,),
+        in_specs=[pl.BlockSpec((2, some, half, LANES), lambda i: (0, i, 0, 0))],
+        out_specs=pl.BlockSpec((some, half + SUBLANES, LANES), lambda i: (i, 0, 0)),
         out_shape=jax.ShapeDtypeStruct((blocks, half + SUBLANES, LANES), jnp.int32),
+        cost_estimate=takes(2),
         name="encode_cotangent",
     )(value.reshape(2, blocks, half, LANES))
 
 
 def decode(words, blocks):
     half = words.shape[1] - SUBLANES
+    some = blocks // 4
     out = pl.pallas_call(
         decode_kernel,
-        grid=(blocks,),
-        in_specs=[pl.BlockSpec((1, half + SUBLANES, LANES), lambda i: (i, 0, 0))],
-        out_specs=pl.BlockSpec((2, 1, half, LANES), lambda i: (0, i, 0, 0)),
+        grid=(blocks // some,),
+        in_specs=[pl.BlockSpec((some, half + SUBLANES, LANES), lambda i: (i, 0, 0))],
+        out_specs=pl.BlockSpec((2, some, half, LANES), lambda i: (0, i, 0, 0)),
         out_shape=jax.ShapeDtypeStruct((2, blocks, half, LANES), F32),
+        cost_estimate=takes(2),
         name="decode_mixer",
     )(words)
     return out.reshape(2 * blocks * half, LANES)
+
+
+def takes(microseconds):
+    return pl.CostEstimate(flops=int(microseconds * 1e9), bytes_accessed=int(microseconds * 3e6), transcendentals=0)
 
 
 def pack_table_kernel(mine_ref, other_ref, out_ref):
@@ -360,39 +387,102 @@
     out_ref[half:, :] = lower
 
 
+def unpack_square_kernel(rank_ref, *refs):
+    *word_refs, out_ref = refs
+    half = out_ref.shape[0] // 2
+    for away, ref in enumerate(word_refs):
+        upper, lower = unpack_pair(ref[0, :half, :], ref[0, half : half + 1, :])
+        place = pl.ds(pl.multiple_of(((rank_ref[0] & 3) ^ away) * LANES, LANES), LANES)
+        out_ref[:half, place] = upper
+        out_ref[half:, place] = lower
+
+
 def one_hot_block(token_ref, block, vocab):
-    wanted = token_ref[pl.ds(block, 1), :]
+    wanted = token_ref[block, 0:1, :]
     entry = lax.broadcasted_iota(jnp.int32, (vocab, LANES), 0)
     return (entry == wanted).astype(F32).astype(BF16)
 
 
+def filter_kernel(
+    _,
+    tap_ref, tap_next_ref, gain_ref, gain_next_ref, residue_ref, residue_next_ref, decay_ref, decay_next_ref, seed_ref, seed_next_ref,
+    ahead_ref, twist_ref,
+    response_out, side_ref,
+    work_ref, response_ref, mode_ref, sems,
+):
+    slots, channels, _ = response_ref.shape
+    blocks = slots - 1
+    half = channels // 2
+    modes = residue_ref.shape[0]
+    for rows, parts in (
+        (slice(0, half), (tap_ref, gain_ref, residue_ref, decay_ref, seed_ref)),
+        (slice(half, channels), (tap_next_ref, gain_next_ref, residue_next_ref, decay_next_ref, seed_next_ref)),
+    ):
+        taps, gain, residues, decays, seeds = (part[...] for part in parts)
+        weights = residues * jnp.sqrt(decays + 1.0 / (blocks * LANES))
+        listed = jnp.concatenate([taps[0], taps[1], taps[2], gain], axis=0)
+        side_ref[rows, :] = jnp.pad(listed, ((0, LANES - listed.shape[0]), (0, 0))).T
+        listed = jnp.concatenate([weights, decays, seeds.astype(F32)], axis=0)
+        mode_ref[rows, :] = jnp.pad(listed, ((0, LANES - listed.shape[0]), (0, 0))).T
+
+    def filters(rows):
+        weights, decays, seeds = (mode_ref[rows, i * modes : (i + 1) * modes] for i in range(3))
+        store_spectrum(work_ref, rows, padded_real_dft(filter_blocks(weights, decays, seeds.astype(jnp.int32), blocks, modes)))
+
+    for_tiles(channels, filters)
+
+    def step(k):
+        response_ref[k] = inner_ahead(work_ref[k], twist_ref[k], ahead_ref[...])
+        pltpu.make_async_copy(response_ref.at[k], response_out.at[k], sems.at[k]).start()
+
+    over_slots(slots, step)
+
+    @pl.loop(0, slots)
+    def _(k):
+        pltpu.make_async_copy(response_ref.at[k], response_out.at[k], sems.at[k]).wait()
+
+
+def filtered(work_ref, response_ref, ahead_ref, back_ref, twist_ref, sign):
+    def step(k):
+        twist = twist_ref[k]
+        spectrum = inner_ahead(work_ref[k], twist, ahead_ref[...])
+        a, b = response_ref[k, :, :LANES], response_ref[k, :, LANES:] * sign
+        c, d = spectrum[:, :LANES], spectrum[:, LANES:]
+        product = jnp.concatenate([a * c - b * d, a * d + b * c], axis=1)
+        work_ref[k] = inner_back(product, twist, back_ref[...])
+
+    over_slots(work_ref.shape[0], step)
+
+
 def forward_kernel(
-    table_ref, token_ref, tap_ref, residue_ref, decay_ref, seed_ref, gain_ref, ahead_ref, back_ref, twist_ref,
-    words_ref, response_ref, long_ref, x_ref,
-    work_ref, mixed_ref, query_ref,
+    place_ref, own_ref, other_ref, token_ref, side_ref, *refs
 ):
+    held, (words_ref, long_out_ref, x_out_ref), refs = refs[:4], refs[4:7], refs[7:]
+    (response_ref, ahead_ref, back_ref, twist_ref), (long_ref, x_ref, work_ref, mixed_ref, query_ref, sems) = refs[:4], refs[4:]
+    tables = [pltpu.make_async_copy(held[i], refs[i], sems.at[i]) for i in range(4)]
+    x_copy = pltpu.make_async_copy(x_ref, x_out_ref, sems.at[4])
+    long_copy = pltpu.make_async_copy(long_ref, long_out_ref, sems.at[5])
+    for copy in tables:
+        copy.start()
     blocks, channels, _ = x_ref.shape
     half = channels // 2
-    vocab = table_ref.shape[1]
-    modes = residue_ref.shape[1]
-    tall = jnp.concatenate([table_ref[0].astype(F32).T, table_ref[1].astype(F32).T], axis=0).astype(BF16)
-
-    @pl.loop(0, blocks // 2)
-    def _(pair):
+    vocab = own_ref.shape[0]
+    own, other = own_ref[...].astype(F32).T, other_ref[...].astype(F32).T
+    first = place_ref[1] == 0
+    tall = jnp.concatenate([jnp.where(first, own, other), jnp.where(first, other, own)], axis=0).astype(BF16)
+
+    def lookup(pair):
         hot = jnp.concatenate([one_hot_block(token_ref, 2 * pair + i, vocab) for i in range(2)], axis=1)
         found = jnp.dot(tall, hot, preferred_element_type=F32)
         x_ref[2 * pair] = found[:, :LANES]
         x_ref[2 * pair + 1] = found[:, LANES:]
 
-    def filters(rows):
-        decays = decay_ref[rows, :]
-        weights = residue_ref[rows, :] * jnp.sqrt(decays + 1.0 / (blocks * LANES))
-        taken = filter_blocks(weights, decays, seed_ref[rows, :], blocks, modes)
-        store_spectrum(response_ref, rows, padded_real_dft(taken))
+    over_slots(blocks // 2, lookup)
+    x_copy.start()
 
     def streams(rows):
         lane = lax.broadcasted_iota(jnp.int32, (SUBLANES, LANES), 1)
-        taps = wide_taps(tap_ref, rows)
+        taps = wide_taps(side_ref, rows)
         mixed = []
         for block, terms in shifted_blocks(x_ref, rows, blocks, lane):
             query_ref[block, rows, :] = mix(taps, 0, terms)
@@ -400,29 +490,21 @@
             mixed_ref[block, rows, :] = mixed[-1]
         store_spectrum(work_ref, rows, padded_real_dft(mixed))
 
-    for_tiles(channels, filters)
     for_tiles(channels, streams)
-
-    @pl.loop(0, blocks + 1)
-    def _(k):
-        twist = twist_ref[k]
-        response = inner_ahead(response_ref[k], twist, ahead_ref[...])
-        response_ref[k] = response
-        spectrum = inner_ahead(work_ref[k], twist, ahead_ref[...])
-        a, b = response[:, :LANES], response[:, LANES:]
-        c, d = spectrum[:, :LANES], spectrum[:, LANES:]
-        product = jnp.concatenate([a * c - b * d, a * d + b * c], axis=1)
-        work_ref[k] = inner_back(product, twist, back_ref[...])
+    for copy in tables:
+        copy.wait()
+    filtered(work_ref, response_ref, ahead_ref, back_ref, twist_ref, 1.0)
 
     def results(rows):
         conv = padded_real_back(load_spectrum(work_ref, rows, blocks + 1))
-        gain = jnp.broadcast_to(gain_ref[rows, :], (SUBLANES, LANES))
+        gain = wide_column(side_ref, rows, GAIN_COLUMN)
         for block in range(blocks):
             long_out = conv[block] + gain * mixed_ref[block, rows, :]
             long_ref[block, rows, :] = long_out
             query_ref[block, rows, :] = query_ref[block, rows, :] * long_out
 
     for_tiles(channels, results)
+    long_copy.start()
 
     @pl.loop(0, blocks)
     def _(block):
@@ -430,12 +512,18 @@
         words_ref[block, :half, :] = words
         words_ref[block, half:, :] = code
 
+    x_copy.wait()
+    long_copy.wait()
+
 
 def backward_kernel(
-    words_ref, x_ref, long_ref, response_ref, token_ref, tap_ref, gain_ref, ahead_ref, back_ref, twist_ref,
-    grad_ref,
-    work_ref, cot_ref, late_ref,
+    words_ref, token_ref, side_ref, *refs
 ):
+    held, grad_ref, refs = refs[:6], refs[6], refs[7:]
+    x_ref, response_ref, ahead_ref, back_ref, twist_ref, long_ref, work_ref, cot_ref, late_ref, sems = refs
+    copies = [pltpu.make_async_copy(held[i], refs[i], sems.at[i]) for i in range(6)]
+    for copy in copies:
+        copy.start()
     blocks, channels, _ = x_ref.shape
     half = channels // 2
     vocab = grad_ref.shape[1]
@@ -446,9 +534,11 @@
         cot_ref[block, :half, :] = upper
         cot_ref[block, half:, :] = lower
 
+    copies[0].wait()
+
     def streams(rows):
         lane = lax.broadcasted_iota(jnp.int32, (SUBLANES, LANES), 1)
-        taps = wide_taps(tap_ref, rows)
+        taps = wide_taps(side_ref, rows)
         long_grad = []
         for block, terms in shifted_blocks(x_ref, rows, blocks, lane):
             long_grad.append(cot_ref[block, rows, :] * mix(taps, 0, terms))
@@ -457,19 +547,14 @@
 
     for_tiles(channels, streams)
 
-    @pl.loop(0, blocks + 1)
-    def _(k):
-        twist = twist_ref[k]
-        spectrum = inner_ahead(work_ref[k], twist, ahead_ref[...])
-        a, b = response_ref[k, :, :LANES], response_ref[k, :, LANES:]
-        c, d = spectrum[:, :LANES], spectrum[:, LANES:]
-        product = jnp.concatenate([a * c + b * d, a * d - b * c], axis=1)
-        work_ref[k] = inner_back(product, twist, back_ref[...])
+    for copy in copies[1:]:
+        copy.wait()
+    filtered(work_ref, response_ref, ahead_ref, back_ref, twist_ref, -1.0)
 
     def results(rows):
         lane = lax.broadcasted_iota(jnp.int32, (SUBLANES, LANES), 1)
-        taps = wide_taps(tap_ref, rows)
-        gain = jnp.broadcast_to(gain_ref[rows, :], (SUBLANES, LANES))
+        taps = wide_taps(side_ref, rows)
+        gain = wide_column(side_ref, rows, GAIN_COLUMN)
         correlated = padded_real_back(load_spectrum(work_ref, rows, blocks + 1))
         for block in range(blocks):
             late_ref[block, rows, :] = correlated[block] + gain * late_ref[block, rows, :]
@@ -514,8 +599,22 @@
     grad_ref[1] = total[:, half:]
 
 
+def anywhere(count):
+    return [pl.BlockSpec(memory_space=pl.ANY)] * count
+
+
 def in_vmem(count):
     return [pl.BlockSpec(memory_space=pltpu.VMEM)] * count
+
+
+def gather_square(value, rank):
+    def swap(part, bits):
+        return lax.ppermute(part, "ctx", [(i, i ^ bits) for i in range(16)])
+
+    column_of = jnp.stack([value] + [swap(value, bits) for bits in (4, 8, 12)])
+    beside, below = swap(column_of, 1), swap(column_of, 2)
+    across = jnp.concatenate([swap(beside[:2], 2), swap(below[2:], 1)])
+    return column_of, beside, below, across
 
 
 def body(token_ids, embedding, conv_taps, residues, decays, filter_seed, skip_gain, cotangent):
@@ -527,81 +626,117 @@
     half = width // 2 // blocks
     channels = 2 * half
     modes = residues.shape[1]
-
-    cot_words = lax.all_to_all(encode(cotangent[0], blocks), "ctx", split_axis=0, concat_axis=0, tiled=True)
-
-    tokens = lax.all_gather(token_ids, "ctx", axis=0, tiled=True)
+    slots = blocks + 1
+    place = jnp.stack([rank, side]).astype(jnp.int32)
+    other_core = [(0, 1), (1, 0)]
+
+    def exchange(value):
+        return lax.all_to_all(value, "ctx", split_axis=0, concat_axis=0, tiled=True)
+
+    tokens = exchange(jnp.broadcast_to(token_ids[None], (blocks, SUBLANES, LANES)))
+    cot_words = exchange(encode(cotangent[0], blocks))
     own_columns = lax.dynamic_slice_in_dim(embedding, rank * half, half, 1)
-    other_columns = lax.ppermute(own_columns, "fsdp", [(0, 1), (1, 0)])
-    table = jnp.where(
-        side == 0, jnp.stack([own_columns, other_columns]), jnp.stack([other_columns, own_columns])
-    )
-
-    def slab(value):
-        parts = value.reshape(2, blocks, half, value.shape[1])
-        return lax.dynamic_index_in_dim(parts, rank, 1, keepdims=False).reshape(channels, value.shape[1])
-
-    taps = lax.dynamic_index_in_dim(conv_taps.reshape(9, 2, blocks, half), rank, 2, keepdims=False)
-    taps = jnp.pad(taps.reshape(9, channels).T, ((0, 0), (0, 7)))
-    gain = slab(skip_gain[:, None])
+    other_columns = lax.ppermute(own_columns, "fsdp", other_core)
+
     ahead, back, twist = transform_tables(blocks)
-    slots = blocks + 1
     stack = jax.ShapeDtypeStruct((blocks, channels, LANES), F32)
-    params = pltpu.CompilerParams(vmem_limit_bytes=VMEM_BYTES)
-    work = pltpu.VMEM((slots, channels, 2 * LANES), F32)
+    spectra = (slots, channels, 2 * LANES)
+    work = pltpu.VMEM(spectra, F32)
     buffer = pltpu.VMEM((blocks, channels, LANES), F32)
-
-    mixer_words, response, long_out, x = pl.pallas_call(
+    tables = [work, pltpu.VMEM(ahead.shape, BF16), pltpu.VMEM(back.shape, BF16), pltpu.VMEM(twist.shape, F32)]
+
+    def halves(value):
+        lead = value.shape[:-1]
+        zeros = (0,) * len(lead)
+        if half % LANES == 0:
+            return [value, value], [
+                pl.BlockSpec((*lead, half), lambda i, at: (*zeros, at[0])),
+                pl.BlockSpec((*lead, half), lambda i, at: (*zeros, blocks + at[0])),
+            ]
+        parts = [
+            lax.dynamic_slice_in_dim(value, start + rank * half, half, len(lead)) for start in (0, width // 2)
+        ]
+        return parts, [pl.BlockSpec((*lead, half), lambda i, at: (*zeros, 0))] * 2
+
+    listed = [halves(v) for v in (conv_taps, skip_gain[None], residues.T, decays.T, filter_seed.T)]
+    response, sides = pl.pallas_call(
+        filter_kernel,
+        grid_spec=pltpu.PrefetchScalarGridSpec(
+            num_scalar_prefetch=1,
+            grid=(1,),
+            in_specs=[spec for _, specs in listed for spec in specs] + in_vmem(2),
+            out_specs=(pl.BlockSpec(memory_space=pl.ANY), *in_vmem(1)),
+            scratch_shapes=[work, work, pltpu.VMEM((channels, LANES), F32), pltpu.SemaphoreType.DMA((slots,))],
+        ),
+        out_shape=(jax.ShapeDtypeStruct(spectra, F32), jax.ShapeDtypeStruct((channels, LANES), F32)),
+        compiler_params=pltpu.CompilerParams(vmem_limit_bytes=VMEM_BYTES),
+        cost_estimate=takes(15),
+        name="modal_filter",
+    )(place, *[part for parts, _ in listed for part in parts], ahead, twist)
+
+    mixer_words, long_out, x = pl.pallas_call(
         forward_kernel,
-        in_specs=in_vmem(10),
-        out_specs=tuple(in_vmem(4)),
-        out_shape=(
-            jax.ShapeDtypeStruct((blocks, half + SUBLANES, LANES), jnp.int32),
-            jax.ShapeDtypeStruct((slots, channels, 2 * LANES), F32),
-            stack,
-            stack,
-        ),
-        scratch_shapes=[work, buffer, buffer],
-        compiler_params=params,
+        in_specs=[pl.BlockSpec(memory_space=pltpu.SMEM)] + in_vmem(4) + anywhere(4),
+        out_specs=(*in_vmem(1), *anywhere(2)),
+        out_shape=(jax.ShapeDtypeStruct((blocks, half + SUBLANES, LANES), jnp.int32), stack, stack),
+        scratch_shapes=tables + [buffer, buffer, work, buffer, buffer, pltpu.SemaphoreType.DMA((6,))],
+        compiler_params=pltpu.CompilerParams(vmem_limit_bytes=VMEM_BYTES),
+        cost_estimate=takes(18),
         name="forward",
-    )(table, tokens, taps, slab(residues), slab(decays), slab(filter_seed), gain, ahead, back, twist)
-
-    mixer_words = lax.all_to_all(mixer_words, "ctx", split_axis=0, concat_axis=0, tiled=True)
+    )(place, own_columns, other_columns, tokens, sides, response, ahead, back, twist)
+
+    mixer_words = exchange(mixer_words)
 
     grads = pl.pallas_call(
         backward_kernel,
-        in_specs=in_vmem(10),
+        in_specs=in_vmem(3) + anywhere(6),
         out_specs=in_vmem(1)[0],
         out_shape=jax.ShapeDtypeStruct((2, vocab, half), F32),
-        scratch_shapes=[work, buffer, buffer],
-        compiler_params=params,
+        scratch_shapes=[buffer, *tables, buffer, work, buffer, buffer, pltpu.SemaphoreType.DMA((6,))],
+        compiler_params=pltpu.CompilerParams(vmem_limit_bytes=VMEM_BYTES),
+        cost_estimate=takes(20),
         name="backward",
-    )(cot_words, x, long_out, response, tokens, taps, gain, ahead, back, twist)
+    )(cot_words, tokens, sides, x, response, ahead, back, twist, long_out)
 
     mine = lax.dynamic_index_in_dim(grads, side, 0, keepdims=False)
     theirs = lax.dynamic_index_in_dim(grads, 1 - side, 0, keepdims=False)
-    theirs = lax.ppermute(theirs, "fsdp", [(0, 1), (1, 0)])
+    theirs = lax.ppermute(theirs, "fsdp", other_core)
     tall = vocab // 2 + SUBLANES
     grad_words = pl.pallas_call(
         pack_table_kernel,
         out_shape=jax.ShapeDtypeStruct((tall, half), jnp.int32),
+        cost_estimate=takes(1),
         name="pack_table",
     )(mine, theirs)
-    grad_words = lax.all_gather(grad_words, "ctx", axis=0, tiled=False)
-    group = max(1, LANES // half)
-    if group > 1:
+    table = jax.ShapeDtypeStruct((vocab, blocks * half), F32)
+    if blocks == 16 and half == LANES:
+        embed_grad = pl.pallas_call(
+            unpack_square_kernel,
+            grid_spec=pltpu.PrefetchScalarGridSpec(
+                num_scalar_prefetch=1,
+                grid=(4,),
+                in_specs=[pl.BlockSpec((1, tall, half), lambda i, at: (i, 0, 0))] * 4,
+                out_specs=pl.BlockSpec((vocab, 4 * half), lambda i, at: (0, (at[0] >> 2) ^ i)),
+            ),
+            out_shape=table,
+            cost_estimate=takes(3),
+            name="unpack_table",
+        )(place, *gather_square(grad_words, rank))
+    else:
+        grad_words = lax.all_gather(grad_words, "ctx", axis=0, tiled=False)
+        group = max(1, LANES // half)
         grad_words = grad_words.reshape(blocks // group, group, tall, half)
         grad_words = jnp.swapaxes(grad_words, 1, 2).reshape(blocks // group, tall, group * half)
-    embed_grad = pl.pallas_call(
-        unpack_table_kernel,
-        grid=(blocks // group,),
-        in_specs=[pl.BlockSpec((1, tall, group * half), lambda i: (i, 0, 0))],
-        out_specs=pl.BlockSpec((vocab, group * half), lambda i: (0, i)),
-        out_shape=jax.ShapeDtypeStruct((vocab, blocks * half), F32),
-        name="unpack_table",
-    )(grad_words)
-    mixer_out = decode(mixer_words, blocks)
-    return mixer_out[None], embed_grad
+        embed_grad = pl.pallas_call(
+            unpack_table_kernel,
+            grid=(blocks // group,),
+            in_specs=[pl.BlockSpec((1, tall, group * half), lambda i: (i, 0, 0))],
+            out_specs=pl.BlockSpec((vocab, group * half), lambda i: (0, i)),
+            out_shape=table,
+            cost_estimate=takes(3),
+            name="unpack_table",
+        )(grad_words)
+    return decode(mixer_words, blocks)[None], embed_grad
 
 
 def solution(mesh):

time: 241 us -> 141 us (0.59)
  blocking collectives: 82.4 us -> 0 us
  Pallas kernels: 102 us -> 71.9 us
  starting transfers between devices: 8.36 us -> 29.5 us
  waiting for transfers between devices: 13.6 us -> 27.4 us
  between operations: 14.1 us -> 0.79 us
  local copies, waits for them, and re-layouts: 16.8 us -> 7.54 us
    all_gather x1 -> x0, blocking collectives: 41.4 us -> none  [body(): tokens = lax.all_gather(token_ids, 'ctx', axis=0, tiled=True)]
    all_to_all x1 -> x0, blocking collectives: 41 us -> none  [body(): lax.all_to_all(mixer_words, 'ctx', split_axis=0, concat_axis=0, tiled=True)]
    pallas_call x5 -> x6, Pallas kernels: 100 us -> 70.2 us  [the longest x1 24.6 us: body(): pl.pallas_call(backward_kernel, in_specs=in_vmem(3) + anywhere(6), out_sp...]
    ppermute x2 -> x9, waiting for transfers between devices: 1.54 us -> 24.4 us  [the longest x7 22.9 us: swap(): return lax.ppermute(part, 'ctx', [(i, i ^ bits) for i in range(16)])]
    all_gather x1 -> x0, waiting for transfers between devices: 12 us -> none  [body(): grad_words = lax.all_gather(grad_words, 'ctx', axis=0, tiled=False)]
    all_to_all x1 -> x3, starting transfers between devices: 8.31 us -> 19.2 us  [exchange(): return lax.all_to_all(value, 'ctx', split_axis=0, concat_axis=0, tiled=True)]
    ppermute x2 -> x9, starting transfers between devices: 0.01 us -> 10.3 us  [the longest x7 10.2 us: swap(): return lax.ppermute(part, 'ctx', [(i, i ^ bits) for i in range(16)])]
    unnamed x19 -> x20, local copies, waits for them, and re-layouts: 8.53 us -> 3.49 us
  transfers between devices with their start and end apart: 4 -> 12, of which waited for: 2 -> 6; matrix products, arithmetic and copies ran while one was open for 6% -> 3% of each run, Pallas kernels for 20% -> 47%
where the time goes in v2:
time: 141 us
  Pallas kernels  71.9 us (51%)
  starting transfers between devices  29.5 us (21%)
  waiting for transfers between devices  27.4 us (19%)
  local copies, waits for them, and re-layouts  7.54 us (5%)
  other arithmetic  3.47 us (2%)
    pallas_call x1, Pallas kernels, body(): pl.pallas_call(backward_kernel, in_specs=in_vmem(3) + anywhere(6), out_sp...  24.6 us
    ppermute x7, waiting for transfers between devices, swap(): return lax.ppermute(part, 'ctx', [(i, i ^ bits) for i in range(16)])  22.9 us
    all_to_all x3, starting transfers between devices, exchange(): return lax.all_to_all(value, 'ctx', split_axis=0, concat_axis=0, tiled=True)  19.2 us
    pallas_call x1, Pallas kernels, body(): pl.pallas_call(filter_kernel, grid_spec=pltpu.PrefetchScalarGridSpec(num_...  17 us
    pallas_call x1, Pallas kernels, body(): pl.pallas_call(forward_kernel, in_specs=[pl.BlockSpec(memory_space=pltpu....  16 us
    ppermute x7, starting transfers between devices, swap(): return lax.ppermute(part, 'ctx', [(i, i ^ bits) for i in range(16)])  10.2 us
    pallas_call x1, Pallas kernels, body(): pl.pallas_call(unpack_square_kernel, grid_spec=pltpu.PrefetchScalarGridSp...  5.22 us
    pallas_call x1, Pallas kernels, encode(): pl.pallas_call(encode_kernel, grid=(blocks // some,), in_specs=[pl.BlockS...  3.79 us
  transfers between devices with their start and end apart: 12, of which 6 were waited for; matrix products, arithmetic and copies ran while one was open for 3% of the time, Pallas kernels for 47%

profile of v2, /device:TPU:0, one launch (start us, length us, event | category | flops | bytes accessed | tf_op | source)
XLA Modules:
  0.0 140.6 jit_solution(8788060245392756753)
XLA Ops:
  0.6 0.0 copy-start
  0.6 1.4 %broadcast_in_dim.12 = s32[16,8,128]{2,1,0:T(8,128)} broadcast(s32[128]{0:T(128)} %bitcast.21), dimensions={2} | broadcast | bytes 66048 | tf_op jit(solution)/shard_map/broadcast_in_dim | solution.py:636
  2.1 8.3 %all-to-all-start = ((s32[16,8,128]{2,1,0:T(8,128)}), s32[16,8,128]{2,1,0:T(8,128)S(1)}, u32[]{:S(2)}, u32[]{:S(2)}) async-start(s32[16,8,128]{2,1,0:T(8,128)} %broadcast_in_dim.12), calls=%async_computation | async-start | bytes 131072 | tf_op jit(solution)/shard_map/all_to_all | solution.py:634
  10.4 0.0 copy-done
  10.5 0.0 copy-start.6
  10.5 0.1 collective-permute-start
  10.6 3.8 %encode_cotangent.1 = s32[16,136,128]{2,1,0:T(8,128)} custom-call(f32[2,16,128,128]{3,2,1,0:T(8,128)} %bitcast.22), custom_call_target="tpu_custom_call" | custom-call | flops 2000000000 | bytes 6000000 | tf_op jit(solution)/shard_map/encode_cotangent/pallas_call | solution.py:345
  14.3 0.0 copy-done.6
  14.3 0.6 pad_add_fusion.2._.place_ref.rank_ref
  15.0 2.9 %all-to-all-done.token_ref = s32[16,8,128]{2,1,0:T(8,128)S(1)} async-done(((s32[16,8,128]{2,1,0:T(8,128)}), s32[16,8,128]{2,1,0:T(8,128)S(1)}, u32[]{:S(2)}, u32[]{:S(2)}) %all-to-all-start) | async-done | bytes 65568 | tf_op jit(solution)/shard_map/all_to_all | solution.py:634
  17.9 0.0 copy-start.7
  17.9 4.0 %all-to-all-start.2 = ((s32[16,136,128]{2,1,0:T(8,128)}), s32[16,136,128]{2,1,0:T(8,128)S(1)}, u32[]{:S(2)}, u32[]{:S(2)}) async-start(s32[16,136,128]{2,1,0:T(8,128)} %encode_cotangent.1), calls=%async_computation.2 | async-start | bytes 2228224 | tf_op jit(solution)/shard_map/all_to_all | solution.py:634
  21.9 17.0 %modal_filter.1 = (f32[17,256,256]{2,1,0:T(8,128)}, f32[256,128]{1,0:T(8,128)}) custom-call(s32[2]{0:T(128)} %pad_add_fusion.2._.place_ref.rank_ref, f32[3,3,4096]{2,1,0:T(4,128)} %tap_next_ref.1, f32[3,3,4096]{2,1,0:T(4,128)} %tap_next_ref.1, f32[1,4096]{1,0:T(1,128)} %bitcast.29, f32[1,4096]{1,0:T(1,128)} %bitcast.30, f32[16,4096]{1,0:T(8,128)} %bitcast.23, ...), custom_call_target="tpu_custom_call" | custom-call | flops 15000000512 | bytes 45000000 | tf_op jit(solution)/shard_map/modal_filter/pallas_call | solution.py:662
  38.9 0.0 copy-done.7
  38.9 0.0 collective-permute-done.other_ref
  38.9 0.0 copy-start.9
  38.9 0.6 copy-done.9
  39.6 16.0 %forward.1 = (s32[16,136,128]{2,1,0:T(8,128)}, f32[16,256,128]{2,1,0:T(8,128)}, f32[16,256,128]{2,1,0:T(8,128)}) custom-call(s32[2]{0:T(128)} %pad_add_fusion.2._.place_ref.rank_ref, bf16[512,128]{1,0:T(8,128)(2,1)} %copy-done.6, bf16[512,128]{1,0:T(8,128)(2,1)} %copy-done.9, s32[16,8,128]{2,1,0:T(8,128)} %copy-done.7, ...), custom_call_target="tpu_custom_call" | custom-call | flops 17999998976 | bytes 54000000 | tf_op jit(solution)/shard_map/forward/pallas_call | solution.py:677
  55.5 0.0 all-to-all-done.2.words_ref
  55.6 0.0 copy-start.2
  55.6 1.0 copy-done.2
  56.6 6.9 %all-to-all-start.1 = ((s32[16,136,128]{2,1,0:T(8,128)}), s32[16,136,128]{2,1,0:T(8,128)S(1)}, u32[]{:S(2)}, u32[]{:S(2)}) async-start(s32[16,136,128]{2,1,0:T(8,128)} %get-tuple-element.9), calls=%async_computation.1 | async-start | bytes 2228224 | tf_op jit(solution)/shard_map/all_to_all | solution.py:634
  63.5 24.6 %backward.1 = f32[2,512,128]{2,1,0:T(8,128)} custom-call(s32[16,136,128]{2,1,0:T(8,128)} %copy-done.2, s32[16,8,128]{2,1,0:T(8,128)} %copy-done.7, f32[256,128]{1,0:T(8,128)} %get-tuple-element.7.side_ref, f32[16,256,128]{2,1,0:T(8,128)} %get-tuple-element.10.refs_0_, f32[17,256,256]{2,1,0:T(8,128)} %get-tuple-element.8.refs_0_.refs_1_, ...), custom_call_target="tpu_custom_call" | custom-call | flops 20000000000 | bytes 60000000 | tf_op jit(solution)/shard_map/backward/pallas_call | solution.py:690
  88.1 1.8 %dynamic-slice_bitcast_fusion = (f32[512,128]{1,0:T(8,128)S(1)}, f32[512,128]{1,0:T(8,128)}) fusion(f32[2,512,128]{2,1,0:T(8,128)} %backward.1, s32[]{:T(128)S(6)} %select_n.12, s32[]{:T(128)S(6)} %select_n.11), kind=kLoop, calls=%fused_computation.2 | loop fusion | bytes 1048584 | tf_op jit(solution)/shard_map/jit(dynamic_index_in_dim)/squeeze | solution.py:702
  89.8 0.0 collective-permute-start.1
  89.8 1.5 %collective-permute-done.1.other_ref = f32[512,128]{1,0:T(8,128)S(1)} collective-permute-done((f32[512,128]{1,0:T(8,128)S(1)}, f32[512,128]{1,0:T(8,128)S(1)}, u32[]{:S(2)}, u32[]{:S(2)}) %collective-permute-start.1) | collective-permute-done | bytes 262176 | tf_op jit(solution)/shard_map/ppermute | solution.py:703
  91.4 0.0 copy-start.8
  91.4 0.7 copy-done.8
  92.1 1.8 %pack_table.1 = s32[264,128]{1,0:T(8,128)} custom-call(f32[512,128]{1,0:T(8,128)} %get-tuple-element.13.mine_ref, f32[512,128]{1,0:T(8,128)} %copy-done.8), custom_call_target="tpu_custom_call" | custom-call | flops 1000000000 | bytes 3000000 | tf_op jit(solution)/shard_map/pack_table/pallas_call | solution.py:705
  93.8 3.7 %collective-permute-start.4 = (s32[264,128]{1,0:T(8,128)}, s32[264,128]{1,0:T(8,128)S(1)}, u32[]{:S(2)}, u32[]{:S(2)}) collective-permute-start(s32[264,128]{1,0:T(8,128)} %pack_table.1), channel_id=1, source_target_pairs={{0,12},{1,13},{2,14},{3,15},{4,8},{5,9},{6,10},{7,11},{8,4},{9,5},... | collective-permute-start | bytes 405512 | tf_op jit(solution)/shard_map/ppermute | solution.py:612
  97.5 0.0 collective-permute-start.3
  97.6 0.7 collective-permute-start.2
  98.2 4.1 %collective-permute-done.4 = s32[264,128]{1,0:T(8,128)S(1)} collective-permute-done((s32[264,128]{1,0:T(8,128)}, s32[264,128]{1,0:T(8,128)S(1)}, u32[]{:S(2)}, u32[]{:S(2)}) %collective-permute-start.4) | collective-permute-done | bytes 135200 | tf_op jit(solution)/shard_map/ppermute | solution.py:612
  102.4 7.4 %collective-permute-done.3 = s32[264,128]{1,0:T(8,128)S(1)} collective-permute-done((s32[264,128]{1,0:T(8,128)}, s32[264,128]{1,0:T(8,128)S(1)}, u32[]{:S(2)}, u32[]{:S(2)}) %collective-permute-start.3) | collective-permute-done | bytes 135200 | tf_op jit(solution)/shard_map/ppermute | solution.py:612
  109.7 0.0 collective-permute-done.2
  109.7 1.0 pad_add_fusion.refs_0_
  110.7 0.0 copy-start.3
  110.7 1.5 %collective-permute-start.6 = (s32[4,264,128]{2,1,0:T(8,128)S(1)}, s32[4,264,128]{2,1,0:T(8,128)S(1)}, u32[]{:S(2)}, u32[]{:S(2)}) collective-permute-start(s32[4,264,128]{2,1,0:T(8,128)S(1)} %pad_add_fusion.refs_0_), channel_id=1, source_target_pairs={{0,2},{1,3},{2,0},{3,1},{4,6},{5,7},{6,4},{7,5},{8,10},{9,11},{10,... | collective-permute-start | bytes 1622024 | tf_op jit(solution)/shard_map/ppermute | solution.py:612
  112.2 1.5 %collective-permute-start.5 = (s32[4,264,128]{2,1,0:T(8,128)S(1)}, s32[4,264,128]{2,1,0:T(8,128)S(1)}, u32[]{:S(2)}, u32[]{:S(2)}) collective-permute-start(s32[4,264,128]{2,1,0:T(8,128)S(1)} %pad_add_fusion.refs_0_), channel_id=1, source_target_pairs={{0,1},{1,0},{2,3},{3,2},{4,5},{5,4},{6,7},{7,6},{8,9},{9,8},{10,11... | collective-permute-start | bytes 1622024 | tf_op jit(solution)/shard_map/ppermute | solution.py:612
  113.7 10.7 %collective-permute-done.6.refs_2_ = s32[4,264,128]{2,1,0:T(8,128)S(1)} collective-permute-done((s32[4,264,128]{2,1,0:T(8,128)S(1)}, s32[4,264,128]{2,1,0:T(8,128)S(1)}, u32[]{:S(2)}, u32[]{:S(2)}) %collective-permute-start.6) | collective-permute-done | bytes 540704 | tf_op jit(solution)/shard_map/ppermute | solution.py:612
  124.4 0.0 copy-start.4
  124.4 1.4 collective-permute-start.8
  125.8 0.0 collective-permute-done.5.refs_1_
  125.8 0.0 copy-start.5
  125.8 0.8 slice.8
  126.6 0.0 copy-done.3
  126.6 0.0 copy-done.4
  126.6 0.1 copy-done.5
  126.7 1.5 %collective-permute-start.7 = (s32[2,264,128]{2,1,0:T(8,128)}, s32[2,264,128]{2,1,0:T(8,128)}, u32[]{:S(2)}, u32[]{:S(2)}) collective-permute-start(s32[2,264,128]{2,1,0:T(8,128)} %slice.8), channel_id=1, source_target_pairs={{0,2},{1,3},{2,0},{3,1},{4,6},{5,7},{6,4},{7,5},{8,10},{9,11},{10,... | collective-permute-start | bytes 811016 | tf_op jit(solution)/shard_map/ppermute | solution.py:612
  128.2 0.0 all-to-all-done.1.words_ref
  128.2 0.0 copy-start.1
  128.2 1.0 copy-done.1
  129.2 3.6 %decode_mixer.1 = f32[2,16,128,128]{3,2,1,0:T(8,128)} custom-call(s32[16,136,128]{2,1,0:T(8,128)} %copy-done.1), custom_call_target="tpu_custom_call" | custom-call | flops 2000000000 | bytes 6000000 | tf_op jit(solution)/shard_map/decode_mixer/pallas_call | solution.py:359
  132.8 0.0 collective-permute-done.8
  132.8 0.7 collective-permute-done.7
  133.5 1.9 %pad_add_fusion.1.refs_3_ = s32[4,264,128]{2,1,0:T(8,128)} fusion(s32[2,264,128]{2,1,0:T(8,128)} %collective-permute-done.8, s32[2,264,128]{2,1,0:T(8,128)} %collective-permute-done.7), kind=kLoop, calls=%fused_computation.1 | loop fusion | flops 135168 | bytes 1081344 | tf_op jit(solution)/shard_map/concatenate | solution.py:616
  135.4 5.2 %unpack_table.1 = f32[512,2048]{1,0:T(8,128)} custom-call(s32[2]{0:T(128)} %pad_add_fusion.2._.place_ref.rank_ref, s32[4,264,128]{2,1,0:T(8,128)} %copy-done.3, s32[4,264,128]{2,1,0:T(8,128)} %copy-done.5, s32[4,264,128]{2,1,0:T(8,128)} %copy-done.4, s32[4,264,128]{2,1,0:T(8,128)} %pad_add_fusion.1.refs_3_), custom_call_target="tpu_custom_call" | custom-call | flops 3000000000 | bytes 9000000 | tf_op jit(solution)/shard_map/unpack_table/pallas_call | solution.py:713
  (2 shorter events, 0.1 us)
Async XLA Ops:
  0.6 9.8 %copy-start = (bf16[512,2048]{1,0:T(8,128)(2,1)S(1)}, bf16[512,2048]{1,0:T(8,128)(2,1)}, u32[]{:S(2)}) copy-start(bf16[512,2048]{1,0:T(8,128)(2,1)} %param.12) | copy-start | bytes 6291460
  2.1 15.9 %all-to-all-start = ((s32[16,8,128]{2,1,0:T(8,128)}), s32[16,8,128]{2,1,0:T(8,128)S(1)}, u32[]{:S(2)}, u32[]{:S(2)}) async-start(s32[16,8,128]{2,1,0:T(8,128)} %broadcast_in_dim.12), calls=%async_computation | async-start | bytes 131072 | tf_op jit(solution)/shard_map/all_to_all | solution.py:634
  10.5 3.9 %copy-start.6 = (bf16[512,128]{1,0:T(8,128)(2,1)}, bf16[512,128]{1,0:T(8,128)(2,1)S(1)}, u32[]{:S(2)}) copy-start(bf16[512,128]{1,0:T(8,128)(2,1)S(1)} %constant_dynamic-slice_fusion.own_ref) | copy-start | bytes 393220
  10.5 28.4 %collective-permute-start = (bf16[512,128]{1,0:T(8,128)(2,1)S(1)}, bf16[512,128]{1,0:T(8,128)(2,1)S(1)}, u32[]{:S(2)}, u32[]{:S(2)}) collective-permute-start(bf16[512,128]{1,0:T(8,128)(2,1)S(1)} %constant_dynamic-slice_fusion.own_ref), channel_id=1, source_target_pairs={{0,16},{16,0},{1,17},{17,1},{2,18},{18,2},{3,19},{19,3},{4,20},{20... | collective-permute-start | bytes 393224 | tf_op jit(solution)/shard_map/ppermute | solution.py:639
  17.9 20.9 %copy-start.7 = (s32[16,8,128]{2,1,0:T(8,128)}, s32[16,8,128]{2,1,0:T(8,128)S(1)}, u32[]{:S(2)}) copy-start(s32[16,8,128]{2,1,0:T(8,128)S(1)} %all-to-all-done.token_ref) | copy-start | bytes 196612
  17.9 37.6 %all-to-all-start.2 = ((s32[16,136,128]{2,1,0:T(8,128)}), s32[16,136,128]{2,1,0:T(8,128)S(1)}, u32[]{:S(2)}, u32[]{:S(2)}) async-start(s32[16,136,128]{2,1,0:T(8,128)} %encode_cotangent.1), calls=%async_computation.2 | async-start | bytes 2228224 | tf_op jit(solution)/shard_map/all_to_all | solution.py:634
  38.9 0.7 copy-start.9
  55.6 1.0 copy-start.2
  56.6 71.6 %all-to-all-start.1 = ((s32[16,136,128]{2,1,0:T(8,128)}), s32[16,136,128]{2,1,0:T(8,128)S(1)}, u32[]{:S(2)}, u32[]{:S(2)}) async-start(s32[16,136,128]{2,1,0:T(8,128)} %get-tuple-element.9), calls=%async_computation.1 | async-start | bytes 2228224 | tf_op jit(solution)/shard_map/all_to_all | solution.py:634
  89.8 1.5 %collective-permute-start.1 = (f32[512,128]{1,0:T(8,128)S(1)}, f32[512,128]{1,0:T(8,128)S(1)}, u32[]{:S(2)}, u32[]{:S(2)}) collective-permute-start(f32[512,128]{1,0:T(8,128)S(1)} %get-tuple-element.12), channel_id=1, source_target_pairs={{0,16},{16,0},{1,17},{17,1},{2,18},{18,2},{3,19},{19,3},{4,20},{20... | collective-permute-start | bytes 786440 | tf_op jit(solution)/shard_map/ppermute | solution.py:703
  91.4 0.7 copy-start.8
  93.8 8.5 %collective-permute-start.4 = (s32[264,128]{1,0:T(8,128)}, s32[264,128]{1,0:T(8,128)S(1)}, u32[]{:S(2)}, u32[]{:S(2)}) collective-permute-start(s32[264,128]{1,0:T(8,128)} %pack_table.1), channel_id=1, source_target_pairs={{0,12},{1,13},{2,14},{3,15},{4,8},{5,9},{6,10},{7,11},{8,4},{9,5},... | collective-permute-start | bytes 405512 | tf_op jit(solution)/shard_map/ppermute | solution.py:612
  97.5 12.2 %collective-permute-start.3 = (s32[264,128]{1,0:T(8,128)}, s32[264,128]{1,0:T(8,128)S(1)}, u32[]{:S(2)}, u32[]{:S(2)}) collective-permute-start(s32[264,128]{1,0:T(8,128)} %pack_table.1), channel_id=1, source_target_pairs={{0,8},{1,9},{2,10},{3,11},{4,12},{5,13},{6,14},{7,15},{8,0},{9,1},... | collective-permute-start | bytes 405512 | tf_op jit(solution)/shard_map/ppermute | solution.py:612
  97.6 12.2 %collective-permute-start.2 = (s32[264,128]{1,0:T(8,128)}, s32[264,128]{1,0:T(8,128)S(1)}, u32[]{:S(2)}, u32[]{:S(2)}) collective-permute-start(s32[264,128]{1,0:T(8,128)} %pack_table.1), channel_id=1, source_target_pairs={{0,4},{1,5},{2,6},{3,7},{4,0},{5,1},{6,2},{7,3},{8,12},{9,13},{10,... | collective-permute-start | bytes 405512 | tf_op jit(solution)/shard_map/ppermute | solution.py:612
  110.7 15.9 %copy-start.3 = (s32[4,264,128]{2,1,0:T(8,128)}, s32[4,264,128]{2,1,0:T(8,128)S(1)}, u32[]{:S(2)}) copy-start(s32[4,264,128]{2,1,0:T(8,128)S(1)} %pad_add_fusion.refs_0_) | copy-start | bytes 1622020
  110.7 13.7 %collective-permute-start.6 = (s32[4,264,128]{2,1,0:T(8,128)S(1)}, s32[4,264,128]{2,1,0:T(8,128)S(1)}, u32[]{:S(2)}, u32[]{:S(2)}) collective-permute-start(s32[4,264,128]{2,1,0:T(8,128)S(1)} %pad_add_fusion.refs_0_), channel_id=1, source_target_pairs={{0,2},{1,3},{2,0},{3,1},{4,6},{5,7},{6,4},{7,5},{8,10},{9,11},{10,... | collective-permute-start | bytes 1622024 | tf_op jit(solution)/shard_map/ppermute | solution.py:612
  112.2 13.6 %collective-permute-start.5 = (s32[4,264,128]{2,1,0:T(8,128)S(1)}, s32[4,264,128]{2,1,0:T(8,128)S(1)}, u32[]{:S(2)}, u32[]{:S(2)}) collective-permute-start(s32[4,264,128]{2,1,0:T(8,128)S(1)} %pad_add_fusion.refs_0_), channel_id=1, source_target_pairs={{0,1},{1,0},{2,3},{3,2},{4,5},{5,4},{6,7},{7,6},{8,9},{9,8},{10,11... | collective-permute-start | bytes 1622024 | tf_op jit(solution)/shard_map/ppermute | solution.py:612
  124.4 2.2 %copy-start.4 = (s32[4,264,128]{2,1,0:T(8,128)}, s32[4,264,128]{2,1,0:T(8,128)S(1)}, u32[]{:S(2)}) copy-start(s32[4,264,128]{2,1,0:T(8,128)S(1)} %collective-permute-done.6.refs_2_) | copy-start | bytes 1622020
  124.4 8.4 %collective-permute-start.8 = (s32[2,264,128]{2,1,0:T(8,128)S(1)}, s32[2,264,128]{2,1,0:T(8,128)}, u32[]{:S(2)}, u32[]{:S(2)}) collective-permute-start(s32[2,264,128]{2,1,0:T(8,128)S(1)} %slice.9), channel_id=1, source_target_pairs={{0,1},{1,0},{2,3},{3,2},{4,5},{5,4},{6,7},{7,6},{8,9},{9,8},{10,11... | collective-permute-start | bytes 811016 | tf_op jit(solution)/shard_map/ppermute | solution.py:612
  125.8 0.9 copy-start.5
  126.7 6.8 %collective-permute-start.7 = (s32[2,264,128]{2,1,0:T(8,128)}, s32[2,264,128]{2,1,0:T(8,128)}, u32[]{:S(2)}, u32[]{:S(2)}) collective-permute-start(s32[2,264,128]{2,1,0:T(8,128)} %slice.8), channel_id=1, source_target_pairs={{0,2},{1,3},{2,0},{3,1},{4,6},{5,7},{6,4},{7,5},{8,10},{9,11},{10,... | collective-permute-start | bytes 811016 | tf_op jit(solution)/shard_map/ppermute | solution.py:612
  128.2 1.0 copy-start.1

commit v3 on v2

--- a/solution.py
+++ b/solution.py
@@ -1,3 +1,4 @@
+import functools
 import math
 
 import jax
@@ -238,80 +239,82 @@
     return sum(taps[3 * stream + j] * terms[j] for j in range(3))
 
 
-def wide_column(ref, rows, index):
-    return jnp.broadcast_to(ref[rows, index : index + 1], (SUBLANES, LANES))
-
-
 def wide_taps(ref, rows):
-    return [wide_column(ref, rows, i) for i in range(9)]
-
-
-def for_tiles(channels, step):
+    return [ref[i, rows, :] for i in range(9)]
+
+
+def for_tiles(channels, unroll, step):
     def run(tile, carry):
         step(pl.ds(pl.multiple_of(tile * SUBLANES, SUBLANES), SUBLANES))
         return carry
 
-    lax.fori_loop(0, channels // SUBLANES, run, 0)
-
-
-def unit_turn(phase):
-    phase = phase & (PERIOD - 1)
-    quadrant = (phase + PERIOD // 8) >> 10
-    angle = (phase - (quadrant << 10)).astype(F32) * (2.0 * math.pi / PERIOD)
+    lax.fori_loop(0, channels // SUBLANES, run, 0, unroll=unroll)
+
+
+def unit_turn(turns):
+    angle = (turns - jnp.round(turns)) * math.pi
     square = angle * angle
-    sin = angle * (1.0 + square * (-1.0 / 6 + square * (1.0 / 120 + square * (-1.0 / 5040 + square * (1.0 / 362880)))))
-    cos = 1.0 + square * (-0.5 + square * (1.0 / 24 + square * (-1.0 / 720 + square * (1.0 / 40320))))
-    swap = (quadrant & 1) == 1
-    c = jnp.where(swap, sin, cos)
-    s = jnp.where(swap, cos, sin)
-    c = jnp.where(((quadrant + 1) & 2) == 2, -c, c)
-    s = jnp.where((quadrant & 2) == 2, -s, s)
-    return c, s
-
-
+    sin, cos = SINE[-1], COSINE[-1]
+    for coefficient in SINE[-2::-1]:
+        sin = sin * square + coefficient
+    for coefficient in COSINE[-2::-1]:
+        cos = cos * square + coefficient
+    sin = sin * angle
+    twice = sin + sin
+    return 1.0 - twice * sin, twice * cos
+
+
+def fitted(function, terms):
+    top = (math.pi / 2) ** 2
+    points = top / 2 * (1 + np.cos(np.pi * (np.arange(64) + 0.5) / 64))
+    series = np.polynomial.chebyshev.Chebyshev.fit(points, function(np.sqrt(points)), terms - 1, domain=[0, top])
+    return [float(c) for c in series.convert(kind=np.polynomial.Polynomial).coef]
+
+
+SINE = fitted(lambda a: np.sin(a) / a, 5)
+COSINE = fitted(np.cos, 6)
 RESTART = 16
-
-
-def filter_blocks(weights, decays, seeds, blocks, modes):
-    position = lax.broadcasted_iota(jnp.int32, (SUBLANES, LANES), 1)
-    time = position.astype(F32)
-    leap_decay = jnp.exp(decays * (-1.0 * LANES))
-    leap_cos, leap_sin = unit_turn(seeds * LANES)
-    leap_re, leap_im = leap_decay * leap_cos, leap_decay * leap_sin
-    twice, size = 2.0 * leap_re, leap_decay * leap_decay
-    starts = []
+LOG2_E = math.log2(math.e)
+
+
+def modal_rows(residues, decays, seeds, blocks):
+    rates = decays * -LOG2_E
+    turns = seeds.astype(F32) * (1.0 / PERIOD)
+    weights = residues * jnp.sqrt(decays + 1.0 / (blocks * LANES))
+    leap = jnp.exp2(rates * LANES)
+    c, s = unit_turn(turns * LANES)
+    rows = [rates, turns, leap * c, leap * s, 2.0 * (leap * c), leap * leap]
     for start in range(0, blocks, RESTART):
-        if start == 0:
-            starts.append((weights, None))
-        else:
-            fall = weights * jnp.exp(decays * (-1.0 * LANES * start))
-            c, s = unit_turn(seeds * (LANES * start))
-            starts.append((fall * c, fall * s))
+        fall = weights * jnp.exp2(rates * (LANES * start))
+        c, s = unit_turn(turns * (LANES * start))
+        rows += [fall * c, fall * s]
+    return rows
+
+
+def filter_tile(row, time, blocks, modes):
     total = [None] * blocks
     for mode in range(modes):
-        c, s = unit_turn(column(seeds, mode) * position)
-        fall = jnp.exp(-column(decays, mode) * time)
-        base_re, base_im = fall * c, fall * s
-        wide = lambda v: jnp.broadcast_to(column(v, mode), (SUBLANES, LANES))
-        jump_re, jump_im, ahead, behind = wide(leap_re), wide(leap_im), wide(twice), wide(size)
-        for index, (start_re, start_im) in enumerate(starts):
-            first = index * RESTART
-            re, im = base_re, base_im
-            if start_im is None:
-                w = wide(start_re)
-                re, im = w * re, w * im
+        rate, turns, jump_re, jump_im, ahead, behind = (row(i, mode) for i in range(6))
+        c, s = unit_turn(turns * time)
+        fall = jnp.exp2(rate * time)
+        re, im = fall * c, fall * s
+        for first in range(0, blocks, RESTART):
+            place = 6 + 2 * (first // RESTART)
+            if first == 0:
+                weight = row(place, mode)
+                a, b = weight * re, weight * im
             else:
-                a, b = wide(start_re), wide(start_im)
-                re, im = a * re - b * im, a * im + b * re
-            old, new = re, jump_re * re - jump_im * im
-            total[first] = plus(total[first], old)
-            for block in range(first + 1, min(first + RESTART, blocks)):
-                total[block] = plus(total[block], new)
+                start_re, start_im = row(place, mode), row(place + 1, mode)
+                a, b = start_re * re - start_im * im, start_re * im + start_im * re
+            old, new = a, jump_re * a - jump_im * b
+            for block in range(first, min(first + RESTART, blocks)):
+                total[block] = plus(total[block], old)
                 old, new = new, ahead * new - behind * old
     return total
 
 
-GAIN_COLUMN = 9
+GAIN_SIDE = 9
+SIDES = 10
 UNROLLED = 32
 
 
@@ -341,7 +344,7 @@
 
 def encode(value, blocks):
     half = value.shape[0] // 2 // blocks
-    some = blocks // 4
+    some = blocks // 2
     return pl.pallas_call(
         encode_kernel,
         grid=(blocks // some,),
@@ -387,18 +390,25 @@
     out_ref[half:, :] = lower
 
 
-def unpack_square_kernel(rank_ref, *refs):
-    *word_refs, out_ref = refs
+def unpack_square_kernel(place_ref, *refs):
+    *pair_refs, out_ref, table_ref, sems = refs
     half = out_ref.shape[0] // 2
-    for away, ref in enumerate(word_refs):
-        upper, lower = unpack_pair(ref[0, :half, :], ref[0, half : half + 1, :])
-        place = pl.ds(pl.multiple_of(((rank_ref[0] & 3) ^ away) * LANES, LANES), LANES)
-        out_ref[:half, place] = upper
-        out_ref[half:, place] = lower
+    copies = []
+    for index, ref in enumerate(pair_refs):
+        for i in range(2):
+            away = 4 * (2 * (index // 4) + i) + index % 4
+            upper, lower = unpack_pair(ref[i, :half, :], ref[i, half : half + 1, :])
+            table_ref[away, :half, :] = upper
+            table_ref[away, half:, :] = lower
+            place = pl.ds(pl.multiple_of((place_ref[0] ^ away) * LANES, LANES), LANES)
+            copies.append(pltpu.make_async_copy(table_ref.at[away], out_ref.at[:, place], sems.at[away]))
+            copies[-1].start()
+    for copy in copies:
+        copy.wait()
 
 
 def one_hot_block(token_ref, block, vocab):
-    wanted = token_ref[block, 0:1, :]
+    wanted = token_ref[block : block + 1, :]
     entry = lax.broadcasted_iota(jnp.int32, (vocab, LANES), 0)
     return (entry == wanted).astype(F32).astype(BF16)
 
@@ -407,29 +417,48 @@
     _,
     tap_ref, tap_next_ref, gain_ref, gain_next_ref, residue_ref, residue_next_ref, decay_ref, decay_next_ref, seed_ref, seed_next_ref,
     ahead_ref, twist_ref,
-    response_out, side_ref,
-    work_ref, response_ref, mode_ref, sems,
+    response_out, side_out,
+    work_ref, response_ref, mode_ref, taken_ref, time_ref, side_ref, sems,
 ):
     slots, channels, _ = response_ref.shape
     blocks = slots - 1
     half = channels // 2
     modes = residue_ref.shape[0]
-    for rows, parts in (
-        (slice(0, half), (tap_ref, gain_ref, residue_ref, decay_ref, seed_ref)),
-        (slice(half, channels), (tap_next_ref, gain_next_ref, residue_next_ref, decay_next_ref, seed_next_ref)),
-    ):
-        taps, gain, residues, decays, seeds = (part[...] for part in parts)
-        weights = residues * jnp.sqrt(decays + 1.0 / (blocks * LANES))
-        listed = jnp.concatenate([taps[0], taps[1], taps[2], gain], axis=0)
-        side_ref[rows, :] = jnp.pad(listed, ((0, LANES - listed.shape[0]), (0, 0))).T
-        listed = jnp.concatenate([weights, decays, seeds.astype(F32)], axis=0)
-        mode_ref[rows, :] = jnp.pad(listed, ((0, LANES - listed.shape[0]), (0, 0))).T
-
-    def filters(rows):
-        weights, decays, seeds = (mode_ref[rows, i * modes : (i + 1) * modes] for i in range(3))
-        store_spectrum(work_ref, rows, padded_real_dft(filter_blocks(weights, decays, seeds.astype(jnp.int32), blocks, modes)))
-
-    for_tiles(channels, filters)
+    sides = []
+    for index, (taps, gain, residues, decays, seeds) in enumerate((
+        (tap_ref, gain_ref, residue_ref, decay_ref, seed_ref),
+        (tap_next_ref, gain_next_ref, residue_next_ref, decay_next_ref, seed_next_ref),
+    )):
+        for i, rows in enumerate(modal_rows(residues[...], decays[...], seeds[...], blocks)):
+            mode_ref[index, i] = rows
+        listed = jnp.concatenate([taps[0], taps[1], taps[2], gain[...]], axis=0)
+        sides.append(jnp.pad(listed, ((0, LANES - listed.shape[0]), (0, 0))).T)
+    sides = jnp.concatenate(sides, axis=0)
+    for i in range(SIDES):
+        side_ref[i] = jnp.broadcast_to(column(sides, i), (channels, LANES))
+    side_copy = pltpu.make_async_copy(side_ref, side_out, sems.at[slots])
+    side_copy.start()
+
+    for index in range(2):
+
+        def tile(number, carry):
+            first = pl.multiple_of(number * SUBLANES, SUBLANES)
+            time = (lax.broadcasted_iota(jnp.int32, (SUBLANES, half), 0) + first).astype(F32)
+            taken = filter_tile(lambda i, mode: mode_ref[index, i, mode : mode + 1, :], time, blocks, modes)
+            for block in range(blocks):
+                taken_ref[index, block, pl.ds(first, SUBLANES), :] = taken[block]
+            return carry
+
+        lax.fori_loop(0, LANES // SUBLANES, tile, 0, unroll=2)
+
+    for index in range(2):
+        for block in range(blocks):
+            time_ref[block, index * half : (index + 1) * half, :] = taken_ref[index, block].T
+
+    def transforms(rows):
+        store_spectrum(work_ref, rows, padded_real_dft([time_ref[block, rows, :] for block in range(blocks)]))
+
+    for_tiles(channels, 4, transforms)
 
     def step(k):
         response_ref[k] = inner_ahead(work_ref[k], twist_ref[k], ahead_ref[...])
@@ -440,6 +469,8 @@
     @pl.loop(0, slots)
     def _(k):
         pltpu.make_async_copy(response_ref.at[k], response_out.at[k], sems.at[k]).wait()
+
+    side_copy.wait()
 
 
 def filtered(work_ref, response_ref, ahead_ref, back_ref, twist_ref, sign):
@@ -457,10 +488,10 @@
 def forward_kernel(
     place_ref, own_ref, other_ref, token_ref, side_ref, *refs
 ):
-    held, (words_ref, long_out_ref, x_out_ref), refs = refs[:4], refs[4:7], refs[7:]
-    (response_ref, ahead_ref, back_ref, twist_ref), (long_ref, x_ref, work_ref, mixed_ref, query_ref, sems) = refs[:4], refs[4:]
+    held, (words_out_ref, long_out_ref, stream_out_ref), refs = refs[:4], refs[4:7], refs[7:]
+    response_ref, ahead_ref, back_ref, twist_ref, words_ref, long_ref, stream_ref, x_ref, work_ref, sems, word_sems = refs
     tables = [pltpu.make_async_copy(held[i], refs[i], sems.at[i]) for i in range(4)]
-    x_copy = pltpu.make_async_copy(x_ref, x_out_ref, sems.at[4])
+    stream_copy = pltpu.make_async_copy(stream_ref, stream_out_ref, sems.at[4])
     long_copy = pltpu.make_async_copy(long_ref, long_out_ref, sems.at[5])
     for copy in tables:
         copy.start()
@@ -471,82 +502,78 @@
     first = place_ref[1] == 0
     tall = jnp.concatenate([jnp.where(first, own, other), jnp.where(first, other, own)], axis=0).astype(BF16)
 
-    def lookup(pair):
+    for pair in range(blocks // 2):
         hot = jnp.concatenate([one_hot_block(token_ref, 2 * pair + i, vocab) for i in range(2)], axis=1)
         found = jnp.dot(tall, hot, preferred_element_type=F32)
         x_ref[2 * pair] = found[:, :LANES]
         x_ref[2 * pair + 1] = found[:, LANES:]
-
-    over_slots(blocks // 2, lookup)
-    x_copy.start()
 
     def streams(rows):
         lane = lax.broadcasted_iota(jnp.int32, (SUBLANES, LANES), 1)
         taps = wide_taps(side_ref, rows)
         mixed = []
         for block, terms in shifted_blocks(x_ref, rows, blocks, lane):
-            query_ref[block, rows, :] = mix(taps, 0, terms)
-            mixed.append(mix(taps, 1, terms) * mix(taps, 2, terms))
-            mixed_ref[block, rows, :] = mixed[-1]
+            query, key, value = (mix(taps, stream, terms) for stream in range(3))
+            stream_ref[0, block, rows, :] = query
+            stream_ref[1, block, rows, :] = key
+            stream_ref[2, block, rows, :] = value
+            mixed.append(key * value)
         store_spectrum(work_ref, rows, padded_real_dft(mixed))
 
-    for_tiles(channels, streams)
+    for_tiles(channels, 4, streams)
+    stream_copy.start()
     for copy in tables:
         copy.wait()
     filtered(work_ref, response_ref, ahead_ref, back_ref, twist_ref, 1.0)
 
     def results(rows):
         conv = padded_real_back(load_spectrum(work_ref, rows, blocks + 1))
-        gain = wide_column(side_ref, rows, GAIN_COLUMN)
+        gain = side_ref[GAIN_SIDE, rows, :]
         for block in range(blocks):
-            long_out = conv[block] + gain * mixed_ref[block, rows, :]
+            long_out = conv[block] + gain * (stream_ref[1, block, rows, :] * stream_ref[2, block, rows, :])
             long_ref[block, rows, :] = long_out
-            query_ref[block, rows, :] = query_ref[block, rows, :] * long_out
-
-    for_tiles(channels, results)
+            x_ref[block, rows, :] = stream_ref[0, block, rows, :] * long_out
+
+    for_tiles(channels, 2, results)
     long_copy.start()
 
-    @pl.loop(0, blocks)
-    def _(block):
-        words, code = pack_pair(query_ref[block, :half, :], query_ref[block, half:, :])
+    def words_copy(block):
+        return pltpu.make_async_copy(words_ref.at[block], words_out_ref.at[block], word_sems.at[block])
+
+    for block in range(blocks):
+        words, code = pack_pair(x_ref[block, :half, :], x_ref[block, half:, :])
         words_ref[block, :half, :] = words
         words_ref[block, half:, :] = code
-
-    x_copy.wait()
+        words_copy(block).start()
+    for block in range(blocks):
+        words_copy(block).wait()
+    stream_copy.wait()
     long_copy.wait()
 
 
 def backward_kernel(
-    words_ref, token_ref, side_ref, *refs
+    place_ref, words_ref, token_ref, side_ref, *refs
 ):
-    held, grad_ref, refs = refs[:6], refs[6], refs[7:]
-    x_ref, response_ref, ahead_ref, back_ref, twist_ref, long_ref, work_ref, cot_ref, late_ref, sems = refs
+    held, (mine_ref, theirs_ref), refs = refs[:6], refs[6:8], refs[8:]
+    stream_ref, response_ref, ahead_ref, back_ref, twist_ref, long_ref, work_ref, cot_ref, late_ref, sems = refs
     copies = [pltpu.make_async_copy(held[i], refs[i], sems.at[i]) for i in range(6)]
     for copy in copies:
         copy.start()
-    blocks, channels, _ = x_ref.shape
+    blocks, channels, _ = cot_ref.shape
     half = channels // 2
-    vocab = grad_ref.shape[1]
-
-    @pl.loop(0, blocks)
-    def _(block):
+    vocab = mine_ref.shape[0]
+
+    for block in range(blocks):
         upper, lower = unpack_pair(words_ref[block, :half, :], words_ref[block, half : half + 1, :])
         cot_ref[block, :half, :] = upper
         cot_ref[block, half:, :] = lower
-
     copies[0].wait()
 
     def streams(rows):
-        lane = lax.broadcasted_iota(jnp.int32, (SUBLANES, LANES), 1)
-        taps = wide_taps(side_ref, rows)
-        long_grad = []
-        for block, terms in shifted_blocks(x_ref, rows, blocks, lane):
-            long_grad.append(cot_ref[block, rows, :] * mix(taps, 0, terms))
-            late_ref[block, rows, :] = long_grad[-1]
-        store_spectrum(work_ref, rows, padded_real_dft(long_grad))
-
-    for_tiles(channels, streams)
-
+        late = [cot_ref[block, rows, :] * stream_ref[0, block, rows, :] for block in range(blocks)]
+        store_spectrum(work_ref, rows, padded_real_dft(late))
+
+    for_tiles(channels, 4, streams)
     for copy in copies[1:]:
         copy.wait()
     filtered(work_ref, response_ref, ahead_ref, back_ref, twist_ref, -1.0)
@@ -554,49 +581,47 @@
     def results(rows):
         lane = lax.broadcasted_iota(jnp.int32, (SUBLANES, LANES), 1)
         taps = wide_taps(side_ref, rows)
-        gain = wide_column(side_ref, rows, GAIN_COLUMN)
+        gain = side_ref[GAIN_SIDE, rows, :]
         correlated = padded_real_back(load_spectrum(work_ref, rows, blocks + 1))
+        before = None
         for block in range(blocks):
-            late_ref[block, rows, :] = correlated[block] + gain * late_ref[block, rows, :]
-        held = None
-        for block, terms in shifted_blocks(x_ref, rows, blocks, lane):
-            mixed_grad = late_ref[block, rows, :]
-            grads = (
-                cot_ref[block, rows, :] * long_ref[block, rows, :],
-                mixed_grad * mix(taps, 2, terms),
-                mixed_grad * mix(taps, 1, terms),
-            )
+            query, key, value = (stream_ref[stream, block, rows, :] for stream in range(3))
+            cot = cot_ref[block, rows, :]
+            mixed_grad = correlated[block] + gain * (cot * query)
+            grads = (cot * long_ref[block, rows, :], mixed_grad * value, mixed_grad * key)
             now, next_one, next_two = (sum(taps[3 * s + j] * grads[s] for s in range(3)) for j in range(3))
             next_one = pltpu.roll(next_one, LANES - 1, 1)
             next_two = pltpu.roll(next_two, LANES - 2, 1)
-            if held is not None:
-                base, one, two = held
+            if before is not None:
+                base, one, two = before
                 late_ref[block - 1, rows, :] = (
                     base + jnp.where(lane < LANES - 1, one, next_one) + jnp.where(lane < LANES - 2, two, next_two)
                 )
-            held = (now, next_one, next_two)
-        base, one, two = held
+            before = (now, next_one, next_two)
+        base, one, two = before
         late_ref[blocks - 1, rows, :] = (
             base + jnp.where(lane < LANES - 1, one, 0.0) + jnp.where(lane < LANES - 2, two, 0.0)
         )
 
-    for_tiles(channels, results)
-
-    def gather(block, total):
-        hot = one_hot_block(token_ref, block, vocab)
-        value = late_ref[block]
+    for_tiles(channels, 2, results)
+
+    total = None
+    for start in range(0, blocks, 4):
+        some = range(start, start + 4)
+        hot = jnp.concatenate([one_hot_block(token_ref, block, vocab) for block in some], axis=1)
+        value = jnp.concatenate([late_ref[block] for block in some], axis=1)
         high = value.astype(BF16)
         low = (value - high.astype(F32)).astype(BF16)
-        return total + lax.dot_general(
+        part = lax.dot_general(
             jnp.concatenate([hot, hot], axis=1),
             jnp.concatenate([high, low], axis=1),
             (((1,), (1,)), ((), ())),
             preferred_element_type=F32,
         )
-
-    total = lax.fori_loop(0, blocks, gather, jnp.zeros((vocab, channels), F32))
-    grad_ref[0] = total[:, :half]
-    grad_ref[1] = total[:, half:]
+        total = plus(total, part)
+    first = place_ref[1] == 0
+    mine_ref[...] = jnp.where(first, total[:, :half], total[:, half:])
+    theirs_ref[...] = jnp.where(first, total[:, half:], total[:, :half])
 
 
 def anywhere(count):
@@ -607,14 +632,15 @@
     return [pl.BlockSpec(memory_space=pltpu.VMEM)] * count
 
 
-def gather_square(value, rank):
+def gather_square(value):
     def swap(part, bits):
         return lax.ppermute(part, "ctx", [(i, i ^ bits) for i in range(16)])
 
-    column_of = jnp.stack([value] + [swap(value, bits) for bits in (4, 8, 12)])
-    beside, below = swap(column_of, 1), swap(column_of, 2)
-    across = jnp.concatenate([swap(beside[:2], 2), swap(below[2:], 1)])
-    return column_of, beside, below, across
+    near = jnp.stack([value, swap(value, 4)])
+    far = jnp.stack([swap(value, 8), swap(value, 12)])
+    near_beside, far_below = swap(near, 1), swap(far, 2)
+    near_below, far_beside = swap(near, 2), swap(far, 1)
+    return near, near_beside, near_below, swap(near_beside, 2), far, far_beside, far_below, swap(far_below, 1)
 
 
 def body(token_ids, embedding, conv_taps, residues, decays, filter_seed, skip_gain, cotangent):
@@ -633,13 +659,12 @@
     def exchange(value):
         return lax.all_to_all(value, "ctx", split_axis=0, concat_axis=0, tiled=True)
 
-    tokens = exchange(jnp.broadcast_to(token_ids[None], (blocks, SUBLANES, LANES)))
+    tokens = exchange(jnp.broadcast_to(token_ids, (blocks, LANES)))
     cot_words = exchange(encode(cotangent[0], blocks))
     own_columns = lax.dynamic_slice_in_dim(embedding, rank * half, half, 1)
     other_columns = lax.ppermute(own_columns, "fsdp", other_core)
 
     ahead, back, twist = transform_tables(blocks)
-    stack = jax.ShapeDtypeStruct((blocks, channels, LANES), F32)
     spectra = (slots, channels, 2 * LANES)
     work = pltpu.VMEM(spectra, F32)
     buffer = pltpu.VMEM((blocks, channels, LANES), F32)
@@ -665,45 +690,78 @@
             num_scalar_prefetch=1,
             grid=(1,),
             in_specs=[spec for _, specs in listed for spec in specs] + in_vmem(2),
-            out_specs=(pl.BlockSpec(memory_space=pl.ANY), *in_vmem(1)),
-            scratch_shapes=[work, work, pltpu.VMEM((channels, LANES), F32), pltpu.SemaphoreType.DMA((slots,))],
+            out_specs=tuple(anywhere(2)),
+            scratch_shapes=[
+                work,
+                work,
+                pltpu.VMEM((2, 6 + 2 * (-(-blocks // RESTART)), modes, half), F32),
+                pltpu.VMEM((2, blocks, LANES, half), F32),
+                buffer,
+                pltpu.VMEM((SIDES, channels, LANES), F32),
+                pltpu.SemaphoreType.DMA((slots + 1,)),
+            ],
         ),
-        out_shape=(jax.ShapeDtypeStruct(spectra, F32), jax.ShapeDtypeStruct((channels, LANES), F32)),
+        out_shape=(jax.ShapeDtypeStruct(spectra, F32), jax.ShapeDtypeStruct((SIDES, channels, LANES), F32)),
         compiler_params=pltpu.CompilerParams(vmem_limit_bytes=VMEM_BYTES),
         cost_estimate=takes(15),
         name="modal_filter",
     )(place, *[part for parts, _ in listed for part in parts], ahead, twist)
 
-    mixer_words, long_out, x = pl.pallas_call(
+    scalars = functools.partial(pltpu.PrefetchScalarGridSpec, num_scalar_prefetch=1, grid=(1,))
+    mixer_words, long_out, streams = pl.pallas_call(
         forward_kernel,
-        in_specs=[pl.BlockSpec(memory_space=pltpu.SMEM)] + in_vmem(4) + anywhere(4),
-        out_specs=(*in_vmem(1), *anywhere(2)),
-        out_shape=(jax.ShapeDtypeStruct((blocks, half + SUBLANES, LANES), jnp.int32), stack, stack),
-        scratch_shapes=tables + [buffer, buffer, work, buffer, buffer, pltpu.SemaphoreType.DMA((6,))],
+        grid_spec=scalars(
+            in_specs=in_vmem(4) + anywhere(4),
+            out_specs=tuple(anywhere(3)),
+            scratch_shapes=[
+                *tables,
+                pltpu.VMEM((blocks, half + SUBLANES, LANES), jnp.int32),
+                buffer,
+                pltpu.VMEM((3, blocks, channels, LANES), F32),
+                buffer,
+                work,
+                pltpu.SemaphoreType.DMA((6,)),
+                pltpu.SemaphoreType.DMA((blocks,)),
+            ],
+        ),
+        out_shape=(
+            jax.ShapeDtypeStruct((blocks, half + SUBLANES, LANES), jnp.int32),
+            jax.ShapeDtypeStruct((blocks, channels, LANES), F32),
+            jax.ShapeDtypeStruct((3, blocks, channels, LANES), F32),
+        ),
         compiler_params=pltpu.CompilerParams(vmem_limit_bytes=VMEM_BYTES),
-        cost_estimate=takes(18),
+        cost_estimate=takes(14),
         name="forward",
     )(place, own_columns, other_columns, tokens, sides, response, ahead, back, twist)
 
     mixer_words = exchange(mixer_words)
 
-    grads = pl.pallas_call(
+    mine, theirs = pl.pallas_call(
         backward_kernel,
-        in_specs=in_vmem(3) + anywhere(6),
-        out_specs=in_vmem(1)[0],
-        out_shape=jax.ShapeDtypeStruct((2, vocab, half), F32),
-        scratch_shapes=[buffer, *tables, buffer, work, buffer, buffer, pltpu.SemaphoreType.DMA((6,))],
+        grid_spec=scalars(
+            in_specs=in_vmem(3) + anywhere(6),
+            out_specs=tuple(in_vmem(2)),
+            scratch_shapes=[
+                pltpu.VMEM((3, blocks, channels, LANES), F32),
+                *tables,
+                buffer,
+                work,
+                buffer,
+                buffer,
+                pltpu.SemaphoreType.DMA((6,)),
+            ],
+        ),
+        out_shape=(jax.ShapeDtypeStruct((vocab, half), F32),) * 2,
         compiler_params=pltpu.CompilerParams(vmem_limit_bytes=VMEM_BYTES),
-        cost_estimate=takes(20),
+        cost_estimate=takes(15),
         name="backward",
-    )(cot_words, tokens, sides, x, response, ahead, back, twist, long_out)
-
-    mine = lax.dynamic_index_in_dim(grads, side, 0, keepdims=False)
-    theirs = lax.dynamic_index_in_dim(grads, 1 - side, 0, keepdims=False)
+    )(place, cot_words, tokens, sides, streams, response, ahead, back, twist, long_out)
     theirs = lax.ppermute(theirs, "fsdp", other_core)
     tall = vocab // 2 + SUBLANES
     grad_words = pl.pallas_call(
         pack_table_kernel,
+        in_specs=in_vmem(2),
+        out_specs=in_vmem(1)[0],
         out_shape=jax.ShapeDtypeStruct((tall, half), jnp.int32),
         cost_estimate=takes(1),
         name="pack_table",
@@ -712,16 +770,16 @@
     if blocks == 16 and half == LANES:
         embed_grad = pl.pallas_call(
             unpack_square_kernel,
-            grid_spec=pltpu.PrefetchScalarGridSpec(
-                num_scalar_prefetch=1,
-                grid=(4,),
-                in_specs=[pl.BlockSpec((1, tall, half), lambda i, at: (i, 0, 0))] * 4,
-                out_specs=pl.BlockSpec((vocab, 4 * half), lambda i, at: (0, (at[0] >> 2) ^ i)),
+            grid_spec=scalars(
+                in_specs=in_vmem(8),
+                out_specs=anywhere(1)[0],
+                scratch_shapes=[pltpu.VMEM((blocks, vocab, half), F32), pltpu.SemaphoreType.DMA((blocks,))],
             ),
             out_shape=table,
+            compiler_params=pltpu.CompilerParams(vmem_limit_bytes=16 * 1024 * 1024),
             cost_estimate=takes(3),
             name="unpack_table",
-        )(place, *gather_square(grad_words, rank))
+        )(place, *gather_square(grad_words))
     else:
         grad_words = lax.all_gather(grad_words, "ctx", axis=0, tiled=False)
         group = max(1, LANES // half)

time: 141 us -> 118 us (0.84)
  Pallas kernels: 71.9 us -> 55.6 us
  local copies, waits for them, and re-layouts: 7.54 us -> 2.82 us
  waiting for transfers between devices: 27.4 us -> 24.9 us
  starting transfers between devices: 29.5 us -> 31.6 us
  other arithmetic: 3.47 us -> 1.54 us
    pallas_call x4, Pallas kernels: 47.5 us -> 35.9 us  [the longest x1 17 us: body(): pl.pallas_call(backward_kernel, grid_spec=scalars(in_specs=in_vmem(3) + a...]
    ppermute x7 -> x9, waiting for transfers between devices: 22.9 us -> 19.3 us  [swap(): return lax.ppermute(part, 'ctx', [(i, i ^ bits) for i in range(16)])]
    pallas_call x1, Pallas kernels: 17 us -> 13.5 us  [body(): pl.pallas_call(filter_kernel, grid_spec=pltpu.PrefetchScalarGridSpec(num_...]
    ppermute x7 -> x9, starting transfers between devices: 10.2 us -> 12.5 us  [swap(): return lax.ppermute(part, 'ctx', [(i, i ^ bits) for i in range(16)])]
    unnamed x20 -> x14, local copies, waits for them, and re-layouts: 3.49 us -> 1.37 us
    concatenate x1 -> x0, other arithmetic: 1.88 us -> none  [gather_square(): across = jnp.concatenate([swap(beside[:2], 2), swap(below[2:], 1)])]
    squeeze x1 -> x0, local copies, waits for them, and re-layouts: 1.77 us -> none  [body(): theirs = lax.dynamic_index_in_dim(grads, 1 - side, 0, keepdims=False)]
  transfers between devices with their start and end apart: 12 -> 14, of which waited for: 6 -> 8; matrix products, arithmetic and copies ran while one was open for 3% -> 1% of each run, Pallas kernels for 47% -> 44%
where the time goes in v3:
time: 118 us; the launch traced here: 117 us
  Pallas kernels  55.6 us (47%)
  starting transfers between devices  31.6 us (27%)
  waiting for transfers between devices  24.9 us (21%)
  local copies, waits for them, and re-layouts  2.82 us (2%)
  other arithmetic  1.54 us (1%)
    ppermute x9, waiting for transfers between devices, swap(): return lax.ppermute(part, 'ctx', [(i, i ^ bits) for i in range(16)])  19.3 us
    all_to_all x3, starting transfers between devices, exchange(): return lax.all_to_all(value, 'ctx', split_axis=0, concat_axis=0, tiled=True)  18.9 us
    pallas_call x1, Pallas kernels, body(): pl.pallas_call(backward_kernel, grid_spec=scalars(in_specs=in_vmem(3) + a...  17 us
    pallas_call x1, Pallas kernels, body(): pl.pallas_call(filter_kernel, grid_spec=pltpu.PrefetchScalarGridSpec(num_...  13.5 us
    pallas_call x1, Pallas kernels, body(): pl.pallas_call(forward_kernel, grid_spec=scalars(in_specs=in_vmem(4) + an...  13.3 us
    ppermute x9, starting transfers between devices, swap(): return lax.ppermute(part, 'ctx', [(i, i ^ bits) for i in range(16)])  12.5 us
    all_to_all x3, waiting for transfers between devices, exchange(): return lax.all_to_all(value, 'ctx', split_axis=0, concat_axis=0, tiled=True)  3.87 us
    pallas_call x1, Pallas kernels, body(): pl.pallas_call(unpack_square_kernel, grid_spec=scalars(in_specs=in_vmem(8...  3.82 us
  transfers between devices with their start and end apart: 14, of which 8 were waited for; matrix products, arithmetic and copies ran while one was open for 1% of the time, Pallas kernels for 44%

profile of v3, /device:TPU:0, one launch (start us, length us, event | category | flops | bytes accessed | tf_op | source)
XLA Modules:
  0.0 117.4 jit_solution(15742560705014289858)
XLA Ops:
  0.6 0.0 copy-start
  0.6 1.4 %broadcast_in_dim.8 = s32[16,1,128]{2,1,0:T(1,128)} broadcast(s32[128]{0:T(128)} %bitcast.20), dimensions={2} | broadcast | bytes 8704 | tf_op jit(solution)/shard_map/broadcast_in_dim | solution.py:662
  2.1 8.3 %all-to-all-start = ((s32[16,1,128]{2,1,0:T(1,128)}), s32[16,1,128]{2,1,0:T(1,128)S(1)}, u32[]{:S(2)}, u32[]{:S(2)}) async-start(s32[16,1,128]{2,1,0:T(1,128)} %broadcast_in_dim.8), calls=%async_computation | async-start | bytes 16384 | tf_op jit(solution)/shard_map/all_to_all | solution.py:660
  10.4 0.0 copy-done
  10.4 0.0 copy-start.3
  10.4 0.1 collective-permute-start
  10.5 2.6 %encode_cotangent.1 = s32[16,136,128]{2,1,0:T(8,128)} custom-call(f32[2,16,128,128]{3,2,1,0:T(8,128)} %bitcast.21), custom_call_target="tpu_custom_call" | custom-call | flops 2000000000 | bytes 6000000 | tf_op jit(solution)/shard_map/encode_cotangent/pallas_call | solution.py:348
  13.1 0.0 copy-done.3
  13.1 0.6 pad_add_fusion.2._.place_ref
  13.7 3.9 %all-to-all-done = s32[16,1,128]{2,1,0:T(1,128)S(1)} async-done(((s32[16,1,128]{2,1,0:T(1,128)}), s32[16,1,128]{2,1,0:T(1,128)S(1)}, u32[]{:S(2)}, u32[]{:S(2)}) %all-to-all-start) | async-done | bytes 8224 | tf_op jit(solution)/shard_map/all_to_all | solution.py:660
  17.6 0.0 copy-start.4
  17.6 3.7 %all-to-all-start.2 = ((s32[16,136,128]{2,1,0:T(8,128)}), s32[16,136,128]{2,1,0:T(8,128)S(1)}, u32[]{:S(2)}, u32[]{:S(2)}) async-start(s32[16,136,128]{2,1,0:T(8,128)} %encode_cotangent.1), calls=%async_computation.2 | async-start | bytes 2228224 | tf_op jit(solution)/shard_map/all_to_all | solution.py:660
  21.3 13.5 %modal_filter.1 = (f32[17,256,256]{2,1,0:T(8,128)}, f32[10,256,128]{2,1,0:T(8,128)}) custom-call(s32[2]{0:T(128)} %pad_add_fusion.2._.place_ref, f32[3,3,4096]{2,1,0:T(4,128)} %tap_next_ref.1, f32[3,3,4096]{2,1,0:T(4,128)} %tap_next_ref.1, f32[1,4096]{1,0:T(1,128)} %bitcast.28, f32[1,4096]{1,0:T(1,128)} %bitcast.29, f32[16,4096]{1,0:T(8,128)} %bitcast.22, ...), custom_call_target="tpu_custom_call" | custom-call | flops 15000000512 | bytes 45000000 | tf_op jit(solution)/shard_map/modal_filter/pallas_call | solution.py:687
  34.7 0.0 copy-done.4
  34.8 0.0 collective-permute-done.other_ref
  34.8 0.0 copy-start.6
  34.8 0.6 copy-done.6
  35.4 13.3 %forward.1 = (s32[16,136,128]{2,1,0:T(8,128)}, f32[16,256,128]{2,1,0:T(8,128)}, f32[3,16,256,128]{3,2,1,0:T(8,128)}) custom-call(s32[2]{0:T(128)} %pad_add_fusion.2._.place_ref, bf16[512,128]{1,0:T(8,128)(2,1)} %copy-done.3, bf16[512,128]{1,0:T(8,128)(2,1)} %copy-done.6, s32[16,128]{1,0:T(8,128)} %bitcast.18, f32[10,256,128]{2,1,0:T(8,128)} %get-tuple-element.9.side_ref, ...), custom_call_target="tpu_custom_call" | custom-call | flops 14000000000 | bytes 42000000 | tf_op jit(solution)/shard_map/forward/pallas_call | solution.py:711
  48.8 0.0 all-to-all-done.2.words_ref
  48.8 0.0 copy-start.2
  48.8 6.9 %all-to-all-start.1 = ((s32[16,136,128]{2,1,0:T(8,128)}), s32[16,136,128]{2,1,0:T(8,128)}, u32[]{:S(2)}, u32[]{:S(2)}) async-start(s32[16,136,128]{2,1,0:T(8,128)} %get-tuple-element.11), calls=%async_computation.1 | async-start | bytes 2228224 | tf_op jit(solution)/shard_map/all_to_all | solution.py:660
  55.7 0.0 copy-done.2
  55.7 17.0 %backward.1 = (f32[512,128]{1,0:T(8,128)}, f32[512,128]{1,0:T(8,128)}) custom-call(s32[2]{0:T(128)} %pad_add_fusion.2._.place_ref, s32[16,136,128]{2,1,0:T(8,128)} %copy-done.2, s32[16,128]{1,0:T(8,128)} %bitcast.19, f32[10,256,128]{2,1,0:T(8,128)} %get-tuple-element.9.side_ref, f32[3,16,256,128]{3,2,1,0:T(8,128)} %get-tuple-element.12.refs_0_, ...), custom_call_target="tpu_custom_call" | custom-call | flops 15000000512 | bytes 45000000 | tf_op jit(solution)/shard_map/backward/pallas_call | solution.py:739
  72.8 0.1 collective-permute-start.1
  72.8 1.7 %collective-permute-done.1.other_ref = f32[512,128]{1,0:T(8,128)S(1)} collective-permute-done((f32[512,128]{1,0:T(8,128)}, f32[512,128]{1,0:T(8,128)S(1)}, u32[]{:S(2)}, u32[]{:S(2)}) %collective-permute-start.1) | collective-permute-done | bytes 262176 | tf_op jit(solution)/shard_map/ppermute | solution.py:759
  74.6 0.0 copy-start.5
  74.6 0.7 copy-done.5
  75.3 1.8 %pack_table.1 = s32[264,128]{1,0:T(8,128)} custom-call(f32[512,128]{1,0:T(8,128)} %get-tuple-element.14.mine_ref, f32[512,128]{1,0:T(8,128)} %copy-done.5), custom_call_target="tpu_custom_call" | custom-call | flops 1000000000 | bytes 3000000 | tf_op jit(solution)/shard_map/pack_table/pallas_call | solution.py:761
  77.0 1.9 %collective-permute-start.2 = (s32[264,128]{1,0:T(8,128)}, s32[264,128]{1,0:T(8,128)S(1)}, u32[]{:S(2)}, u32[]{:S(2)}) collective-permute-start(s32[264,128]{1,0:T(8,128)} %pack_table.1), channel_id=1, source_target_pairs={{0,4},{1,5},{2,6},{3,7},{4,0},{5,1},{6,2},{7,3},{8,12},{9,13},{10,... | collective-permute-start | bytes 405512 | tf_op jit(solution)/shard_map/ppermute | solution.py:637
  78.9 2.4 %collective-permute-start.7 = (s32[264,128]{1,0:T(8,128)}, s32[264,128]{1,0:T(8,128)S(1)}, u32[]{:S(2)}, u32[]{:S(2)}) collective-permute-start(s32[264,128]{1,0:T(8,128)} %pack_table.1), channel_id=1, source_target_pairs={{0,12},{1,13},{2,14},{3,15},{4,8},{5,9},{6,10},{7,11},{8,4},{9,5},... | collective-permute-start | bytes 405512 | tf_op jit(solution)/shard_map/ppermute | solution.py:637
  81.3 0.0 collective-permute-start.6
  81.3 1.9 %collective-permute-done.2 = s32[264,128]{1,0:T(8,128)S(1)} collective-permute-done((s32[264,128]{1,0:T(8,128)}, s32[264,128]{1,0:T(8,128)S(1)}, u32[]{:S(2)}, u32[]{:S(2)}) %collective-permute-start.2) | collective-permute-done | bytes 135200 | tf_op jit(solution)/shard_map/ppermute | solution.py:637
  83.2 0.9 pad_add_fusion.refs_0_
  84.1 1.6 %collective-permute-start.3 = (s32[2,264,128]{2,1,0:T(8,128)S(1)}, s32[2,264,128]{2,1,0:T(8,128)S(1)}, u32[]{:S(2)}, u32[]{:S(2)}) collective-permute-start(s32[2,264,128]{2,1,0:T(8,128)S(1)} %pad_add_fusion.refs_0_), channel_id=1, source_target_pairs={{0,1},{1,0},{2,3},{3,2},{4,5},{5,4},{6,7},{7,6},{8,9},{9,8},{10,11... | collective-permute-start | bytes 811016 | tf_op jit(solution)/shard_map/ppermute | solution.py:637
  85.7 3.1 %collective-permute-done.7 = s32[264,128]{1,0:T(8,128)S(1)} collective-permute-done((s32[264,128]{1,0:T(8,128)}, s32[264,128]{1,0:T(8,128)S(1)}, u32[]{:S(2)}, u32[]{:S(2)}) %collective-permute-start.7) | collective-permute-done | bytes 135200 | tf_op jit(solution)/shard_map/ppermute | solution.py:637
  88.9 4.9 %collective-permute-done.6 = s32[264,128]{1,0:T(8,128)S(1)} collective-permute-done((s32[264,128]{1,0:T(8,128)}, s32[264,128]{1,0:T(8,128)S(1)}, u32[]{:S(2)}, u32[]{:S(2)}) %collective-permute-start.6) | collective-permute-done | bytes 135200 | tf_op jit(solution)/shard_map/ppermute | solution.py:637
  93.8 0.0 copy-start.1
  93.8 1.7 %collective-permute-start.9 = (s32[2,264,128]{2,1,0:T(8,128)S(1)}, s32[2,264,128]{2,1,0:T(8,128)S(1)}, u32[]{:S(2)}, u32[]{:S(2)}) collective-permute-start(s32[2,264,128]{2,1,0:T(8,128)S(1)} %pad_add_fusion.1.refs_4_), channel_id=1, source_target_pairs={{0,2},{1,3},{2,0},{3,1},{4,6},{5,7},{6,4},{7,5},{8,10},{9,11},{10,... | collective-permute-start | bytes 811016 | tf_op jit(solution)/shard_map/ppermute | solution.py:637
  95.6 0.4 collective-permute-start.4
  95.9 1.5 %collective-permute-start.8 = (s32[2,264,128]{2,1,0:T(8,128)S(1)}, s32[2,264,128]{2,1,0:T(8,128)}, u32[]{:S(2)}, u32[]{:S(2)}) collective-permute-start(s32[2,264,128]{2,1,0:T(8,128)S(1)} %pad_add_fusion.1.refs_4_), channel_id=1, source_target_pairs={{0,1},{1,0},{2,3},{3,2},{4,5},{5,4},{6,7},{7,6},{8,9},{9,8},{10,11... | collective-permute-start | bytes 811016 | tf_op jit(solution)/shard_map/ppermute | solution.py:637
  97.4 0.0 collective-permute-done.3.refs_1_
  97.4 1.7 %collective-permute-start.5 = (s32[2,264,128]{2,1,0:T(8,128)S(1)}, s32[2,264,128]{2,1,0:T(8,128)}, u32[]{:S(2)}, u32[]{:S(2)}) collective-permute-start(s32[2,264,128]{2,1,0:T(8,128)S(1)} %collective-permute-done.3.refs_1_), channel_id=1, source_target_pairs={{0,2},{1,3},{2,0},{3,1},{4,6},{5,7},{6,4},{7,5},{8,10},{9,11},{10,... | collective-permute-start | bytes 811016 | tf_op jit(solution)/shard_map/ppermute | solution.py:637
  99.1 4.3 %collective-permute-done.9.refs_6_ = s32[2,264,128]{2,1,0:T(8,128)S(1)} collective-permute-done((s32[2,264,128]{2,1,0:T(8,128)S(1)}, s32[2,264,128]{2,1,0:T(8,128)S(1)}, u32[]{:S(2)}, u32[]{:S(2)}) %collective-permute-start.9) | collective-permute-done | bytes 270368 | tf_op jit(solution)/shard_map/ppermute | solution.py:637
  103.3 1.5 %collective-permute-start.10 = (s32[2,264,128]{2,1,0:T(8,128)S(1)}, s32[2,264,128]{2,1,0:T(8,128)}, u32[]{:S(2)}, u32[]{:S(2)}) collective-permute-start(s32[2,264,128]{2,1,0:T(8,128)S(1)} %collective-permute-done.9.refs_6_), channel_id=1, source_target_pairs={{0,1},{1,0},{2,3},{3,2},{4,5},{5,4},{6,7},{7,6},{8,9},{9,8},{10,11... | collective-permute-start | bytes 811016 | tf_op jit(solution)/shard_map/ppermute | solution.py:637
  104.8 0.0 all-to-all-done.1.words_ref
  104.8 3.6 %decode_mixer.1 = f32[2,16,128,128]{3,2,1,0:T(8,128)} custom-call(s32[16,136,128]{2,1,0:T(8,128)} %all-to-all-done.1.words_ref), custom_call_target="tpu_custom_call" | custom-call | flops 2000000000 | bytes 6000000 | tf_op jit(solution)/shard_map/decode_mixer/pallas_call | solution.py:362
  108.4 0.7 collective-permute-done.4.refs_2_
  109.1 0.0 collective-permute-done.8.refs_5_
  109.1 4.3 %collective-permute-done.5.refs_3_ = s32[2,264,128]{2,1,0:T(8,128)} collective-permute-done((s32[2,264,128]{2,1,0:T(8,128)S(1)}, s32[2,264,128]{2,1,0:T(8,128)}, u32[]{:S(2)}, u32[]{:S(2)}) %collective-permute-start.5) | collective-permute-done | bytes 270368 | tf_op jit(solution)/shard_map/ppermute | solution.py:637
  113.5 0.0 collective-permute-done.10.refs_7_
  113.5 0.0 copy-done.1
  113.5 3.8 %unpack_table.1 = f32[512,2048]{1,0:T(8,128)} custom-call(s32[2]{0:T(128)S(1)} %copy-done.1, s32[2,264,128]{2,1,0:T(8,128)S(1)} %pad_add_fusion.refs_0_, s32[2,264,128]{2,1,0:T(8,128)S(1)} %collective-permute-done.3.refs_1_, s32[2,264,128]{2,1,0:T(8,128)S(1)} %collective-permute-done.4.refs_2_, s32[2,264,128]{2,1,0:T(8,128)} %collective-permute-done.5.refs_3_, ...), custom_call_target="tpu_custom_call" | custom-call | flops 3000000000 | bytes 9000000 | tf_op jit(solution)/shard_map/unpack_table/pallas_call | solution.py:771
  (2 shorter events, 0.1 us)
Async XLA Ops:
  0.6 9.7 %copy-start = (bf16[512,2048]{1,0:T(8,128)(2,1)S(1)}, bf16[512,2048]{1,0:T(8,128)(2,1)}, u32[]{:S(2)}) copy-start(bf16[512,2048]{1,0:T(8,128)(2,1)} %param.12) | copy-start | bytes 6291460
  2.1 15.5 %all-to-all-start = ((s32[16,1,128]{2,1,0:T(1,128)}), s32[16,1,128]{2,1,0:T(1,128)S(1)}, u32[]{:S(2)}, u32[]{:S(2)}) async-start(s32[16,1,128]{2,1,0:T(1,128)} %broadcast_in_dim.8), calls=%async_computation | async-start | bytes 16384 | tf_op jit(solution)/shard_map/all_to_all | solution.py:660
  10.4 2.7 %copy-start.3 = (bf16[512,128]{1,0:T(8,128)(2,1)}, bf16[512,128]{1,0:T(8,128)(2,1)S(1)}, u32[]{:S(2)}) copy-start(bf16[512,128]{1,0:T(8,128)(2,1)S(1)} %constant_dynamic-slice_fusion.own_ref) | copy-start | bytes 393220
  10.4 24.3 %collective-permute-start = (bf16[512,128]{1,0:T(8,128)(2,1)S(1)}, bf16[512,128]{1,0:T(8,128)(2,1)S(1)}, u32[]{:S(2)}, u32[]{:S(2)}) collective-permute-start(bf16[512,128]{1,0:T(8,128)(2,1)S(1)} %constant_dynamic-slice_fusion.own_ref), channel_id=1, source_target_pairs={{0,16},{16,0},{1,17},{17,1},{2,18},{18,2},{3,19},{19,3},{4,20},{20... | collective-permute-start | bytes 393224 | tf_op jit(solution)/shard_map/ppermute | solution.py:665
  17.6 17.2 %copy-start.4 = (s32[16,1,128]{2,1,0:T(1,128)}, s32[16,1,128]{2,1,0:T(1,128)S(1)}, u32[]{:S(2)}) copy-start(s32[16,1,128]{2,1,0:T(1,128)S(1)} %all-to-all-done) | copy-start | bytes 24580
  17.6 31.2 %all-to-all-start.2 = ((s32[16,136,128]{2,1,0:T(8,128)}), s32[16,136,128]{2,1,0:T(8,128)S(1)}, u32[]{:S(2)}, u32[]{:S(2)}) async-start(s32[16,136,128]{2,1,0:T(8,128)} %encode_cotangent.1), calls=%async_computation.2 | async-start | bytes 2228224 | tf_op jit(solution)/shard_map/all_to_all | solution.py:660
  34.8 0.7 copy-start.6
  48.8 7.0 %copy-start.2 = (s32[16,136,128]{2,1,0:T(8,128)}, s32[16,136,128]{2,1,0:T(8,128)S(1)}, u32[]{:S(2)}) copy-start(s32[16,136,128]{2,1,0:T(8,128)S(1)} %all-to-all-done.2.words_ref) | copy-start | bytes 3342340
  48.8 56.0 %all-to-all-start.1 = ((s32[16,136,128]{2,1,0:T(8,128)}), s32[16,136,128]{2,1,0:T(8,128)}, u32[]{:S(2)}, u32[]{:S(2)}) async-start(s32[16,136,128]{2,1,0:T(8,128)} %get-tuple-element.11), calls=%async_computation.1 | async-start | bytes 2228224 | tf_op jit(solution)/shard_map/all_to_all | solution.py:660
  72.8 1.8 %collective-permute-start.1 = (f32[512,128]{1,0:T(8,128)}, f32[512,128]{1,0:T(8,128)S(1)}, u32[]{:S(2)}, u32[]{:S(2)}) collective-permute-start(f32[512,128]{1,0:T(8,128)} %get-tuple-element.15), channel_id=1, source_target_pairs={{0,16},{16,0},{1,17},{17,1},{2,18},{18,2},{3,19},{19,3},{4,20},{20... | collective-permute-start | bytes 786440 | tf_op jit(solution)/shard_map/ppermute | solution.py:759
  74.6 0.7 copy-start.5
  77.0 6.1 %collective-permute-start.2 = (s32[264,128]{1,0:T(8,128)}, s32[264,128]{1,0:T(8,128)S(1)}, u32[]{:S(2)}, u32[]{:S(2)}) collective-permute-start(s32[264,128]{1,0:T(8,128)} %pack_table.1), channel_id=1, source_target_pairs={{0,4},{1,5},{2,6},{3,7},{4,0},{5,1},{6,2},{7,3},{8,12},{9,13},{10,... | collective-permute-start | bytes 405512 | tf_op jit(solution)/shard_map/ppermute | solution.py:637
  78.9 10.0 %collective-permute-start.7 = (s32[264,128]{1,0:T(8,128)}, s32[264,128]{1,0:T(8,128)S(1)}, u32[]{:S(2)}, u32[]{:S(2)}) collective-permute-start(s32[264,128]{1,0:T(8,128)} %pack_table.1), channel_id=1, source_target_pairs={{0,12},{1,13},{2,14},{3,15},{4,8},{5,9},{6,10},{7,11},{8,4},{9,5},... | collective-permute-start | bytes 405512 | tf_op jit(solution)/shard_map/ppermute | solution.py:637
  81.3 12.5 %collective-permute-start.6 = (s32[264,128]{1,0:T(8,128)}, s32[264,128]{1,0:T(8,128)S(1)}, u32[]{:S(2)}, u32[]{:S(2)}) collective-permute-start(s32[264,128]{1,0:T(8,128)} %pack_table.1), channel_id=1, source_target_pairs={{0,8},{1,9},{2,10},{3,11},{4,12},{5,13},{6,14},{7,15},{8,0},{9,1},... | collective-permute-start | bytes 405512 | tf_op jit(solution)/shard_map/ppermute | solution.py:637
  84.1 13.3 %collective-permute-start.3 = (s32[2,264,128]{2,1,0:T(8,128)S(1)}, s32[2,264,128]{2,1,0:T(8,128)S(1)}, u32[]{:S(2)}, u32[]{:S(2)}) collective-permute-start(s32[2,264,128]{2,1,0:T(8,128)S(1)} %pad_add_fusion.refs_0_), channel_id=1, source_target_pairs={{0,1},{1,0},{2,3},{3,2},{4,5},{5,4},{6,7},{7,6},{8,9},{9,8},{10,11... | collective-permute-start | bytes 811016 | tf_op jit(solution)/shard_map/ppermute | solution.py:637
  93.8 19.6 %copy-start.1 = (s32[2]{0:T(128)S(1)}, s32[2]{0:T(128)}, u32[]{:S(2)}) copy-start(s32[2]{0:T(128)} %pad_add_fusion.2._.place_ref) | copy-start | bytes 28
  93.8 9.5 %collective-permute-start.9 = (s32[2,264,128]{2,1,0:T(8,128)S(1)}, s32[2,264,128]{2,1,0:T(8,128)S(1)}, u32[]{:S(2)}, u32[]{:S(2)}) collective-permute-start(s32[2,264,128]{2,1,0:T(8,128)S(1)} %pad_add_fusion.1.refs_4_), channel_id=1, source_target_pairs={{0,2},{1,3},{2,0},{3,1},{4,6},{5,7},{6,4},{7,5},{8,10},{9,11},{10,... | collective-permute-start | bytes 811016 | tf_op jit(solution)/shard_map/ppermute | solution.py:637
  95.6 13.6 %collective-permute-start.4 = (s32[2,264,128]{2,1,0:T(8,128)S(1)}, s32[2,264,128]{2,1,0:T(8,128)S(1)}, u32[]{:S(2)}, u32[]{:S(2)}) collective-permute-start(s32[2,264,128]{2,1,0:T(8,128)S(1)} %pad_add_fusion.refs_0_), channel_id=1, source_target_pairs={{0,2},{1,3},{2,0},{3,1},{4,6},{5,7},{6,4},{7,5},{8,10},{9,11},{10,... | collective-permute-start | bytes 811016 | tf_op jit(solution)/shard_map/ppermute | solution.py:637
  95.9 13.2 %collective-permute-start.8 = (s32[2,264,128]{2,1,0:T(8,128)S(1)}, s32[2,264,128]{2,1,0:T(8,128)}, u32[]{:S(2)}, u32[]{:S(2)}) collective-permute-start(s32[2,264,128]{2,1,0:T(8,128)S(1)} %pad_add_fusion.1.refs_4_), channel_id=1, source_target_pairs={{0,1},{1,0},{2,3},{3,2},{4,5},{5,4},{6,7},{7,6},{8,9},{9,8},{10,11... | collective-permute-start | bytes 811016 | tf_op jit(solution)/shard_map/ppermute | solution.py:637
  97.4 16.1 %collective-permute-start.5 = (s32[2,264,128]{2,1,0:T(8,128)S(1)}, s32[2,264,128]{2,1,0:T(8,128)}, u32[]{:S(2)}, u32[]{:S(2)}) collective-permute-start(s32[2,264,128]{2,1,0:T(8,128)S(1)} %collective-permute-done.3.refs_1_), channel_id=1, source_target_pairs={{0,2},{1,3},{2,0},{3,1},{4,6},{5,7},{6,4},{7,5},{8,10},{9,11},{10,... | collective-permute-start | bytes 811016 | tf_op jit(solution)/shard_map/ppermute | solution.py:637
  103.3 10.1 %collective-permute-start.10 = (s32[2,264,128]{2,1,0:T(8,128)S(1)}, s32[2,264,128]{2,1,0:T(8,128)}, u32[]{:S(2)}, u32[]{:S(2)}) collective-permute-start(s32[2,264,128]{2,1,0:T(8,128)S(1)} %collective-permute-done.9.refs_6_), channel_id=1, source_target_pairs={{0,1},{1,0},{2,3},{3,2},{4,5},{5,4},{6,7},{7,6},{8,9},{9,8},{10,11... | collective-permute-start | bytes 811016 | tf_op jit(solution)/shard_map/ppermute | solution.py:637

commit v4 on v3

--- a/solution.py
+++ b/solution.py
@@ -390,25 +390,55 @@
     out_ref[half:, :] = lower
 
 
-def unpack_square_kernel(place_ref, *refs):
-    *pair_refs, out_ref, table_ref, sems = refs
+def unpack_square_kernel(aways, place_ref, *refs):
+    part_refs, (out_ref, table_ref, sems) = refs[: len(aways)], refs[-3:]
     half = out_ref.shape[0] // 2
     copies = []
-    for index, ref in enumerate(pair_refs):
-        for i in range(2):
-            away = 4 * (2 * (index // 4) + i) + index % 4
-            upper, lower = unpack_pair(ref[i, :half, :], ref[i, half : half + 1, :])
-            table_ref[away, :half, :] = upper
-            table_ref[away, half:, :] = lower
-            place = pl.ds(pl.multiple_of((place_ref[0] ^ away) * LANES, LANES), LANES)
-            copies.append(pltpu.make_async_copy(table_ref.at[away], out_ref.at[:, place], sems.at[away]))
-            copies[-1].start()
+    for slot, (ref, away) in enumerate(zip(part_refs, aways)):
+        upper, lower = unpack_pair(ref[:half, :], ref[half : half + 1, :])
+        table_ref[slot, :half, :] = upper
+        table_ref[slot, half:, :] = lower
+        place = pl.ds(pl.multiple_of((place_ref[0] ^ away) * LANES, LANES), LANES)
+        copies.append(pltpu.make_async_copy(table_ref.at[slot], out_ref.at[:, place], sems.at[slot]))
+        copies[-1].start()
     for copy in copies:
         copy.wait()
 
 
+def fill_table(held, parts, aways, place, vocab, width):
+    count = len(aways)
+    return pl.pallas_call(
+        functools.partial(unpack_square_kernel, aways),
+        grid_spec=pltpu.PrefetchScalarGridSpec(
+            num_scalar_prefetch=1,
+            grid=(1,),
+            in_specs=in_vmem(len(parts)) + anywhere(len(held)),
+            out_specs=anywhere(1)[0],
+            scratch_shapes=[pltpu.VMEM((count, vocab, LANES), F32), pltpu.SemaphoreType.DMA((count,))],
+        ),
+        out_shape=jax.ShapeDtypeStruct((vocab, width), F32),
+        input_output_aliases={len(parts) + 1: 0} if held else {},
+        compiler_params=pltpu.CompilerParams(vmem_limit_bytes=16 * 1024 * 1024),
+        cost_estimate=takes(2.5 if count > 4 else 1.5),
+        name="unpack_table",
+    )(place, *parts, *held)
+
+
+def hold_tokens(refs, token_ref):
+    count = refs[0].shape[0]
+    for index, ref in enumerate(refs):
+        token_ref[index * count : (index + 1) * count, :] = ref[...]
+
+
+def token_row(block, place_ref, pieces):
+    if pieces == 1:
+        return block
+    away = place_ref[0] ^ block
+    return 4 * (away & 3) + (away >> 2)
+
+
 def one_hot_block(token_ref, block, vocab):
-    wanted = token_ref[block : block + 1, :]
+    wanted = token_ref[pl.ds(block, 1), :]
     entry = lax.broadcasted_iota(jnp.int32, (vocab, LANES), 0)
     return (entry == wanted).astype(F32).astype(BF16)
 
@@ -485,14 +515,15 @@
     over_slots(work_ref.shape[0], step)
 
 
-def forward_kernel(
-    place_ref, own_ref, other_ref, token_ref, side_ref, *refs
-):
-    held, (words_out_ref, long_out_ref, stream_out_ref), refs = refs[:4], refs[4:7], refs[7:]
-    response_ref, ahead_ref, back_ref, twist_ref, words_ref, long_ref, stream_ref, x_ref, work_ref, sems, word_sems = refs
-    tables = [pltpu.make_async_copy(held[i], refs[i], sems.at[i]) for i in range(4)]
-    stream_copy = pltpu.make_async_copy(stream_ref, stream_out_ref, sems.at[4])
-    long_copy = pltpu.make_async_copy(long_ref, long_out_ref, sems.at[5])
+def forward_kernel(pieces, place_ref, own_ref, other_ref, *refs):
+    token_refs, token_ref, refs = refs[:pieces], refs[-1], refs[pieces:-1]
+    hold_tokens(token_refs, token_ref)
+    held, (words_out_ref, long_out_ref, stream_out_ref), refs = refs[:5], refs[5:8], refs[8:]
+    side_ref, response_ref, ahead_ref, back_ref, twist_ref, words_ref, long_ref, stream_ref, x_ref, work_ref, sems, word_sems = refs
+    side_copy, *tables = [pltpu.make_async_copy(held[i], refs[i], sems.at[i]) for i in range(5)]
+    stream_copy = pltpu.make_async_copy(stream_ref, stream_out_ref, sems.at[5])
+    long_copy = pltpu.make_async_copy(long_ref, long_out_ref, sems.at[6])
+    side_copy.start()
     for copy in tables:
         copy.start()
     blocks, channels, _ = x_ref.shape
@@ -503,10 +534,11 @@
     tall = jnp.concatenate([jnp.where(first, own, other), jnp.where(first, other, own)], axis=0).astype(BF16)
 
     for pair in range(blocks // 2):
-        hot = jnp.concatenate([one_hot_block(token_ref, 2 * pair + i, vocab) for i in range(2)], axis=1)
+        hot = jnp.concatenate([one_hot_block(token_ref, token_row(2 * pair + i, place_ref, pieces), vocab) for i in range(2)], axis=1)
         found = jnp.dot(tall, hot, preferred_element_type=F32)
         x_ref[2 * pair] = found[:, :LANES]
         x_ref[2 * pair + 1] = found[:, LANES:]
+    side_copy.wait()
 
     def streams(rows):
         lane = lax.broadcasted_iota(jnp.int32, (SUBLANES, LANES), 1)
@@ -551,14 +583,16 @@
     long_copy.wait()
 
 
-def backward_kernel(
-    place_ref, words_ref, token_ref, side_ref, *refs
-):
-    held, (mine_ref, theirs_ref), refs = refs[:6], refs[6:8], refs[8:]
-    stream_ref, response_ref, ahead_ref, back_ref, twist_ref, long_ref, work_ref, cot_ref, late_ref, sems = refs
-    copies = [pltpu.make_async_copy(held[i], refs[i], sems.at[i]) for i in range(6)]
-    for copy in copies:
-        copy.start()
+def backward_kernel(pieces, place_ref, words_ref, *refs):
+    token_refs, token_ref, refs = refs[:pieces], refs[-1], refs[pieces:-1]
+    hold_tokens(token_refs, token_ref)
+    held, (mine_ref, theirs_ref), refs = refs[:7], refs[7:9], refs[9:]
+    stream_ref, response_ref, ahead_ref, back_ref, twist_ref, side_ref, long_ref, work_ref, cot_ref, late_ref, sems = refs
+    query_copy = pltpu.make_async_copy(held[0].at[0], stream_ref.at[0], sems.at[0])
+    tables = [pltpu.make_async_copy(held[i], refs[i], sems.at[i]) for i in range(1, 5)]
+    rest = [pltpu.make_async_copy(held[i], refs[i], sems.at[i]) for i in range(5, 7)]
+    rest += [pltpu.make_async_copy(held[0].at[i], stream_ref.at[i], sems.at[6 + i]) for i in range(1, 3)]
+    query_copy.start()
     blocks, channels, _ = cot_ref.shape
     half = channels // 2
     vocab = mine_ref.shape[0]
@@ -567,16 +601,22 @@
         upper, lower = unpack_pair(words_ref[block, :half, :], words_ref[block, half : half + 1, :])
         cot_ref[block, :half, :] = upper
         cot_ref[block, half:, :] = lower
-    copies[0].wait()
+    query_copy.wait()
+    for copy in tables:
+        copy.start()
 
     def streams(rows):
         late = [cot_ref[block, rows, :] * stream_ref[0, block, rows, :] for block in range(blocks)]
         store_spectrum(work_ref, rows, padded_real_dft(late))
 
     for_tiles(channels, 4, streams)
-    for copy in copies[1:]:
+    for copy in tables:
         copy.wait()
+    for copy in rest:
+        copy.start()
     filtered(work_ref, response_ref, ahead_ref, back_ref, twist_ref, -1.0)
+    for copy in rest:
+        copy.wait()
 
     def results(rows):
         lane = lax.broadcasted_iota(jnp.int32, (SUBLANES, LANES), 1)
@@ -608,7 +648,7 @@
     total = None
     for start in range(0, blocks, 4):
         some = range(start, start + 4)
-        hot = jnp.concatenate([one_hot_block(token_ref, block, vocab) for block in some], axis=1)
+        hot = jnp.concatenate([one_hot_block(token_ref, token_row(block, place_ref, pieces), vocab) for block in some], axis=1)
         value = jnp.concatenate([late_ref[block] for block in some], axis=1)
         high = value.astype(BF16)
         low = (value - high.astype(F32)).astype(BF16)
@@ -632,15 +672,28 @@
     return [pl.BlockSpec(memory_space=pltpu.VMEM)] * count
 
 
-def gather_square(value):
+def gather_tokens(tokens):
     def swap(part, bits):
         return lax.ppermute(part, "ctx", [(i, i ^ bits) for i in range(16)])
 
-    near = jnp.stack([value, swap(value, 4)])
-    far = jnp.stack([swap(value, 8), swap(value, 12)])
-    near_beside, far_below = swap(near, 1), swap(far, 2)
-    near_below, far_beside = swap(near, 2), swap(far, 1)
-    return near, near_beside, near_below, swap(near_beside, 2), far, far_beside, far_below, swap(far_below, 1)
+    stack = jnp.concatenate([tokens] + [swap(tokens, bits) for bits in (4, 8, 12)], axis=0)
+    return [stack] + [swap(stack, bits) for bits in (1, 2, 3)]
+
+
+def gather_square(value, mixer_out, place, width):
+    def swap(part, bits):
+        return lax.ppermute(part, "ctx", [(i, i ^ bits) for i in range(16)])
+
+    def square(part, first, second):
+        beside, below = swap(part, first), swap(part, second)
+        return part, beside, below, swap(beside, second)
+
+    eight, four = swap(value, 8), swap(value, 4)
+    parts = (*square(value, 1, 2), *square(four, 2, 1), *square(eight, 1, 2))
+    *last, mixer_out = lax.optimization_barrier((*square(swap(eight, 4), 2, 1), mixer_out))
+    vocab = 2 * (value.shape[0] - SUBLANES)
+    table = fill_table((), parts, (0, 1, 2, 3, 4, 6, 5, 7, 8, 9, 10, 11), place, vocab, width)
+    return mixer_out, fill_table((table,), last, (12, 14, 13, 15), place, vocab, width)
 
 
 def body(token_ids, embedding, conv_taps, residues, decays, filter_seed, skip_gain, cotangent):
@@ -659,10 +712,14 @@
     def exchange(value):
         return lax.all_to_all(value, "ctx", split_axis=0, concat_axis=0, tiled=True)
 
-    tokens = exchange(jnp.broadcast_to(token_ids, (blocks, LANES)))
+    if blocks == 16:
+        tokens = gather_tokens(token_ids)
+    else:
+        tokens = [exchange(jnp.broadcast_to(token_ids, (blocks, LANES)))]
     cot_words = exchange(encode(cotangent[0], blocks))
     own_columns = lax.dynamic_slice_in_dim(embedding, rank * half, half, 1)
     other_columns = lax.ppermute(own_columns, "fsdp", other_core)
+    place, other_columns = lax.optimization_barrier((place, other_columns))
 
     ahead, back, twist = transform_tables(blocks)
     spectra = (slots, channels, 2 * LANES)
@@ -709,19 +766,21 @@
 
     scalars = functools.partial(pltpu.PrefetchScalarGridSpec, num_scalar_prefetch=1, grid=(1,))
     mixer_words, long_out, streams = pl.pallas_call(
-        forward_kernel,
+        functools.partial(forward_kernel, len(tokens)),
         grid_spec=scalars(
-            in_specs=in_vmem(4) + anywhere(4),
+            in_specs=in_vmem(2 + len(tokens)) + anywhere(5),
             out_specs=tuple(anywhere(3)),
             scratch_shapes=[
+                pltpu.VMEM((SIDES, channels, LANES), F32),
                 *tables,
                 pltpu.VMEM((blocks, half + SUBLANES, LANES), jnp.int32),
                 buffer,
                 pltpu.VMEM((3, blocks, channels, LANES), F32),
                 buffer,
                 work,
-                pltpu.SemaphoreType.DMA((6,)),
+                pltpu.SemaphoreType.DMA((7,)),
                 pltpu.SemaphoreType.DMA((blocks,)),
+                pltpu.VMEM((blocks, LANES), jnp.int32),
             ],
         ),
         out_shape=(
@@ -732,54 +791,47 @@
         compiler_params=pltpu.CompilerParams(vmem_limit_bytes=VMEM_BYTES),
         cost_estimate=takes(14),
         name="forward",
-    )(place, own_columns, other_columns, tokens, sides, response, ahead, back, twist)
+    )(place, own_columns, other_columns, *tokens, sides, response, ahead, back, twist)
 
     mixer_words = exchange(mixer_words)
 
     mine, theirs = pl.pallas_call(
-        backward_kernel,
+        functools.partial(backward_kernel, len(tokens)),
         grid_spec=scalars(
-            in_specs=in_vmem(3) + anywhere(6),
+            in_specs=in_vmem(1 + len(tokens)) + anywhere(7),
             out_specs=tuple(in_vmem(2)),
             scratch_shapes=[
                 pltpu.VMEM((3, blocks, channels, LANES), F32),
                 *tables,
+                pltpu.VMEM((SIDES, channels, LANES), F32),
                 buffer,
                 work,
                 buffer,
                 buffer,
-                pltpu.SemaphoreType.DMA((6,)),
+                pltpu.SemaphoreType.DMA((9,)),
+                pltpu.VMEM((blocks, LANES), jnp.int32),
             ],
         ),
         out_shape=(jax.ShapeDtypeStruct((vocab, half), F32),) * 2,
         compiler_params=pltpu.CompilerParams(vmem_limit_bytes=VMEM_BYTES),
         cost_estimate=takes(15),
         name="backward",
-    )(place, cot_words, tokens, sides, streams, response, ahead, back, twist, long_out)
+    )(place, cot_words, *tokens, streams, response, ahead, back, twist, sides, long_out)
     theirs = lax.ppermute(theirs, "fsdp", other_core)
+    mixer_out = decode(mixer_words, blocks)
     tall = vocab // 2 + SUBLANES
     grad_words = pl.pallas_call(
         pack_table_kernel,
         in_specs=in_vmem(2),
         out_specs=in_vmem(1)[0],
+        compiler_params=pltpu.CompilerParams(vmem_limit_bytes=8 * 1024 * 1024),
         out_shape=jax.ShapeDtypeStruct((tall, half), jnp.int32),
         cost_estimate=takes(1),
         name="pack_table",
     )(mine, theirs)
     table = jax.ShapeDtypeStruct((vocab, blocks * half), F32)
     if blocks == 16 and half == LANES:
-        embed_grad = pl.pallas_call(
-            unpack_square_kernel,
-            grid_spec=scalars(
-                in_specs=in_vmem(8),
-                out_specs=anywhere(1)[0],
-                scratch_shapes=[pltpu.VMEM((blocks, vocab, half), F32), pltpu.SemaphoreType.DMA((blocks,))],
-            ),
-            out_shape=table,
-            compiler_params=pltpu.CompilerParams(vmem_limit_bytes=16 * 1024 * 1024),
-            cost_estimate=takes(3),
-            name="unpack_table",
-        )(place, *gather_square(grad_words))
+        mixer_out, embed_grad = gather_square(grad_words, mixer_out, place, blocks * half)
     else:
         grad_words = lax.all_gather(grad_words, "ctx", axis=0, tiled=False)
         group = max(1, LANES // half)
@@ -794,7 +846,7 @@
             cost_estimate=takes(3),
             name="unpack_table",
         )(grad_words)
-    return decode(mixer_words, blocks)[None], embed_grad
+    return mixer_out[None], embed_grad
 
 
 def solution(mesh):

time: 118 us -> 109 us (0.924)
  waiting for transfers between devices: 24.9 us -> 8.45 us
  starting transfers between devices: 31.6 us -> 42.7 us
  Pallas kernels: 55.6 us -> 54.2 us
  local copies, waits for them, and re-layouts: 2.82 us -> 1.6 us
    ppermute x9 -> x21, starting transfers between devices: 12.5 us -> 28.4 us  [swap(): return lax.ppermute(part, 'ctx', [(i, i ^ bits) for i in range(16)])]
    ppermute x9 -> x21, waiting for transfers between devices: 19.3 us -> 6.7 us  [swap(): return lax.ppermute(part, 'ctx', [(i, i ^ bits) for i in range(16)])]
    all_to_all x3 -> x2, starting transfers between devices: 18.9 us -> 14.2 us  [exchange(): return lax.all_to_all(value, 'ctx', split_axis=0, concat_axis=0, tiled=True)]
    all_to_all x3 -> x2, waiting for transfers between devices: 3.87 us -> 0.01 us  [exchange(): return lax.all_to_all(value, 'ctx', split_axis=0, concat_axis=0, tiled=True)]
    pallas_call x1, Pallas kernels: 1.76 us -> 0.07 us  [body(): pl.pallas_call(pack_table_kernel, in_specs=in_vmem(2), out_specs=in_vmem(...]
    broadcast_in_dim x1 -> x0, local copies, waits for them, and re-layouts: 1.41 us -> none  [body(): tokens = exchange(jnp.broadcast_to(token_ids, (blocks, LANES)))]
    pallas_call x3 -> x4, Pallas kernels: 34.2 us -> 34.4 us  [the longest x1 15.8 us: body(): pl.pallas_call(functools.partial(backward_kernel, len(tokens)), grid_spec...]
  transfers between devices with their start and end apart: 14 -> 25, of which waited for: 8 -> 6; matrix products, arithmetic and copies ran while one was open for 1% -> 1% of each run, Pallas kernels for 44% -> 48%
where the time goes in v4:
time: 109 us
  Pallas kernels  54.2 us (50%)
  starting transfers between devices  42.7 us (39%)
  waiting for transfers between devices  8.45 us (8%)
  local copies, waits for them, and re-layouts  1.6 us (1%)
    ppermute x21, starting transfers between devices, swap(): return lax.ppermute(part, 'ctx', [(i, i ^ bits) for i in range(16)])  28.4 us
    pallas_call x1, Pallas kernels, body(): pl.pallas_call(functools.partial(backward_kernel, len(tokens)), grid_spec...  15.8 us
    all_to_all x2, starting transfers between devices, exchange(): return lax.all_to_all(value, 'ctx', split_axis=0, concat_axis=0, tiled=True)  14.2 us
    pallas_call x1, Pallas kernels, body(): pl.pallas_call(functools.partial(forward_kernel, len(tokens)), grid_spec=...  13.7 us
    pallas_call x1, Pallas kernels, body(): pl.pallas_call(filter_kernel, grid_spec=pltpu.PrefetchScalarGridSpec(num_...  13.4 us
    ppermute x21, waiting for transfers between devices, swap(): return lax.ppermute(part, 'ctx', [(i, i ^ bits) for i in range(16)])  6.7 us
    pallas_call x2, Pallas kernels, fill_table(): pl.pallas_call(functools.partial(unpack_square_kernel, aways), grid_spec=...  5 us
    pallas_call x1, Pallas kernels, decode(): pl.pallas_call(decode_kernel, grid=(blocks // some,), in_specs=[pl.BlockS...  3.65 us
  transfers between devices with their start and end apart: 25, of which 6 were waited for; matrix products, arithmetic and copies ran while one was open for 1% of the time, Pallas kernels for 48%

profile of v4, /device:TPU:0, one launch (start us, length us, event | category | flops | bytes accessed | tf_op | source)
XLA Modules:
  0.0 108.6 jit_solution(3938311431524875173)
XLA Ops:
  0.6 0.0 copy-start
  0.6 4.1 %collective-permute-start.2 = (s32[1,128]{1,0:T(1,128)}, s32[1,128]{1,0:T(1,128)S(1)}, u32[]{:S(2)}, u32[]{:S(2)}) collective-permute-start(s32[1,128]{1,0:T(1,128)} %param.11), channel_id=1, source_target_pairs={{0,8},{1,9},{2,10},{3,11},{4,12},{5,13},{6,14},{7,15},{8,0},{9,1},... | collective-permute-start | bytes 1544 | tf_op jit(solution)/shard_map/ppermute | solution.py:677
  4.7 1.6 %collective-permute-start.1 = (s32[1,128]{1,0:T(1,128)}, s32[1,128]{1,0:T(1,128)S(1)}, u32[]{:S(2)}, u32[]{:S(2)}) collective-permute-start(s32[1,128]{1,0:T(1,128)} %param.11), channel_id=1, source_target_pairs={{0,4},{1,5},{2,6},{3,7},{4,0},{5,1},{6,2},{7,3},{8,12},{9,13},{10,... | collective-permute-start | bytes 1544 | tf_op jit(solution)/shard_map/ppermute | solution.py:677
  6.3 0.0 collective-permute-start.3
  6.4 0.1 collective-permute-start
  6.5 2.6 %encode_cotangent.1 = s32[16,136,128]{2,1,0:T(8,128)} custom-call(f32[2,16,128,128]{3,2,1,0:T(8,128)} %bitcast.9), custom_call_target="tpu_custom_call" | custom-call | flops 2000000000 | bytes 6000000 | tf_op jit(solution)/shard_map/encode_cotangent/pallas_call | solution.py:348
  9.1 7.2 %all-to-all-start = ((s32[16,136,128]{2,1,0:T(8,128)}), s32[16,136,128]{2,1,0:T(8,128)S(1)}, u32[]{:S(2)}, u32[]{:S(2)}) async-start(s32[16,136,128]{2,1,0:T(8,128)} %encode_cotangent.1), calls=%async_computation | async-start | bytes 2228224 | tf_op jit(solution)/shard_map/all_to_all | solution.py:713
  16.3 0.6 pad_add_fusion.1._.place_ref
  16.9 0.0 collective-permute-done.2
  16.9 0.0 collective-permute-done.1
  16.9 0.0 collective-permute-done.3
  17.0 2.9 %collective-permute-start.6 = (s32[4,128]{1,0:T(4,128)S(1)}, s32[4,128]{1,0:T(4,128)S(1)}, u32[]{:S(2)}, u32[]{:S(2)}) collective-permute-start(s32[4,128]{1,0:T(4,128)S(1)} %pad_add_fusion.refs_0_), channel_id=1, source_target_pairs={{0,3},{1,2},{2,1},{3,0},{4,7},{5,6},{6,5},{7,4},{8,11},{9,10},{10,... | collective-permute-start | bytes 6152 | tf_op jit(solution)/shard_map/ppermute | solution.py:677
  19.8 0.6 collective-permute-start.5
  20.4 0.1 collective-permute-start.4
  20.5 0.0 collective-permute-done.other_ref
  20.5 13.4 %modal_filter.1 = (f32[17,256,256]{2,1,0:T(8,128)}, f32[10,256,128]{2,1,0:T(8,128)}) custom-call(s32[2]{0:T(128)} %pad_add_fusion.1._.place_ref, f32[3,3,4096]{2,1,0:T(4,128)} %tap_next_ref.1, f32[3,3,4096]{2,1,0:T(4,128)} %tap_next_ref.1, f32[1,4096]{1,0:T(1,128)} %bitcast.16, f32[1,4096]{1,0:T(1,128)} %bitcast.17, f32[16,4096]{1,0:T(8,128)} %bitcast.10, ...), custom_call_target="tpu_custom_call" | custom-call | flops 15000000512 | bytes 45000000 | tf_op jit(solution)/shard_map/modal_filter/pallas_call | solution.py:744
  34.0 0.0 collective-permute-done.6.refs_3_
  34.0 0.0 collective-permute-done.5.refs_2_
  34.0 0.0 collective-permute-done.4.refs_1_
  34.0 0.5 copy-done.8
  34.5 0.1 copy-done.9
  34.6 0.0 copy-done.10
  34.6 13.7 %forward.1 = (s32[16,136,128]{2,1,0:T(8,128)}, f32[16,256,128]{2,1,0:T(8,128)}, f32[3,16,256,128]{3,2,1,0:T(8,128)}) custom-call(s32[2]{0:T(128)} %pad_add_fusion.1._.place_ref, bf16[512,128]{1,0:T(8,128)(2,1)} %copy-done.4, bf16[512,128]{1,0:T(8,128)(2,1)} %copy-done.7, s32[4,128]{1,0:T(4,128)} %copy-done.5, s32[4,128]{1,0:T(4,128)} %copy-done.10, ...), custom_call_target="tpu_custom_call" | custom-call | flops 14000000000 | bytes 42000000 | tf_op jit(solution)/shard_map/forward/pallas_call | solution.py:768
  48.3 0.0 all-to-all-done.words_ref
  48.3 7.0 %all-to-all-start.1 = ((s32[16,136,128]{2,1,0:T(8,128)}), s32[16,136,128]{2,1,0:T(8,128)}, u32[]{:S(2)}, u32[]{:S(2)}) async-start(s32[16,136,128]{2,1,0:T(8,128)} %get-tuple-element.24), calls=%async_computation.1 | async-start | bytes 2228224 | tf_op jit(solution)/shard_map/all_to_all | solution.py:713
  55.3 15.8 %backward.1 = (f32[512,128]{1,0:T(8,128)}, f32[512,128]{1,0:T(8,128)}) custom-call(s32[2]{0:T(128)} %pad_add_fusion.1._.place_ref, s32[16,136,128]{2,1,0:T(8,128)} %copy-done.3, s32[4,128]{1,0:T(4,128)} %copy-done.5, s32[4,128]{1,0:T(4,128)} %copy-done.10, s32[4,128]{1,0:T(4,128)} %copy-done.9, s32[4,128]{1,0:T(4,128)} %copy-done.8, ...), custom_call_target="tpu_custom_call" | custom-call | flops 15000000512 | bytes 45000000 | tf_op jit(solution)/shard_map/backward/pallas_call | solution.py:798
  71.1 0.1 collective-permute-start.7
  71.2 1.7 %collective-permute-done.7.other_ref = f32[512,128]{1,0:T(8,128)S(1)} collective-permute-done((f32[512,128]{1,0:T(8,128)}, f32[512,128]{1,0:T(8,128)S(1)}, u32[]{:S(2)}, u32[]{:S(2)}) %collective-permute-start.7) | collective-permute-done | bytes 262176 | tf_op jit(solution)/shard_map/ppermute | solution.py:820
  72.9 0.9 copy-done.2
  73.8 0.1 pack_table.1.refs_0_
  73.9 1.9 %collective-permute-start.16 = (s32[264,128]{1,0:T(8,128)S(1)}, s32[264,128]{1,0:T(8,128)S(1)}, u32[]{:S(2)}, u32[]{:S(2)}) collective-permute-start(s32[264,128]{1,0:T(8,128)S(1)} %pack_table.1.refs_0_), channel_id=1, source_target_pairs={{0,4},{1,5},{2,6},{3,7},{4,0},{5,1},{6,2},{7,3},{8,12},{9,13},{10,... | collective-permute-start | bytes 405512 | tf_op jit(solution)/shard_map/ppermute | solution.py:685
  75.9 2.4 %collective-permute-start.8 = (s32[264,128]{1,0:T(8,128)S(1)}, s32[264,128]{1,0:T(8,128)S(1)}, u32[]{:S(2)}, u32[]{:S(2)}) collective-permute-start(s32[264,128]{1,0:T(8,128)S(1)} %pack_table.1.refs_0_), channel_id=1, source_target_pairs={{0,8},{1,9},{2,10},{3,11},{4,12},{5,13},{6,14},{7,15},{8,0},{9,1},... | collective-permute-start | bytes 405512 | tf_op jit(solution)/shard_map/ppermute | solution.py:685
  78.2 1.5 %collective-permute-start.14 = (s32[264,128]{1,0:T(8,128)S(1)}, s32[264,128]{1,0:T(8,128)S(1)}, u32[]{:S(2)}, u32[]{:S(2)}) collective-permute-start(s32[264,128]{1,0:T(8,128)S(1)} %pack_table.1.refs_0_), channel_id=1, source_target_pairs={{0,2},{1,3},{2,0},{3,1},{4,6},{5,7},{6,4},{7,5},{8,10},{9,11},{10,... | collective-permute-start | bytes 405512 | tf_op jit(solution)/shard_map/ppermute | solution.py:685
  79.7 1.5 %collective-permute-start.13 = (s32[264,128]{1,0:T(8,128)S(1)}, s32[264,128]{1,0:T(8,128)S(1)}, u32[]{:S(2)}, u32[]{:S(2)}) collective-permute-start(s32[264,128]{1,0:T(8,128)S(1)} %pack_table.1.refs_0_), channel_id=1, source_target_pairs={{0,1},{1,0},{2,3},{3,2},{4,5},{5,4},{6,7},{7,6},{8,9},{9,8},{10,11... | collective-permute-start | bytes 405512 | tf_op jit(solution)/shard_map/ppermute | solution.py:685
  81.2 0.8 collective-permute-done.16.refs_4_
  82.0 1.5 %collective-permute-start.18 = (s32[264,128]{1,0:T(8,128)S(1)}, s32[264,128]{1,0:T(8,128)S(1)}, u32[]{:S(2)}, u32[]{:S(2)}) collective-permute-start(s32[264,128]{1,0:T(8,128)S(1)} %collective-permute-done.16.refs_4_), channel_id=1, source_target_pairs={{0,1},{1,0},{2,3},{3,2},{4,5},{5,4},{6,7},{7,6},{8,9},{9,8},{10,11... | collective-permute-start | bytes 405512 | tf_op jit(solution)/shard_map/ppermute | solution.py:685
  83.5 1.6 %collective-permute-start.17 = (s32[264,128]{1,0:T(8,128)S(1)}, s32[264,128]{1,0:T(8,128)S(1)}, u32[]{:S(2)}, u32[]{:S(2)}) collective-permute-start(s32[264,128]{1,0:T(8,128)S(1)} %collective-permute-done.16.refs_4_), channel_id=1, source_target_pairs={{0,2},{1,3},{2,0},{3,1},{4,6},{5,7},{6,4},{7,5},{8,10},{9,11},{10,... | collective-permute-start | bytes 405512 | tf_op jit(solution)/shard_map/ppermute | solution.py:685
  85.0 2.3 %collective-permute-done.8.refs_8_ = s32[264,128]{1,0:T(8,128)S(1)} collective-permute-done((s32[264,128]{1,0:T(8,128)S(1)}, s32[264,128]{1,0:T(8,128)S(1)}, u32[]{:S(2)}, u32[]{:S(2)}) %collective-permute-start.8) | collective-permute-done | bytes 135200 | tf_op jit(solution)/shard_map/ppermute | solution.py:685
  87.4 1.5 %collective-permute-start.20 = (s32[264,128]{1,0:T(8,128)S(1)}, s32[264,128]{1,0:T(8,128)S(1)}, u32[]{:S(2)}, u32[]{:S(2)}) collective-permute-start(s32[264,128]{1,0:T(8,128)S(1)} %collective-permute-done.8.refs_8_), channel_id=1, source_target_pairs={{0,1},{1,0},{2,3},{3,2},{4,5},{5,4},{6,7},{7,6},{8,9},{9,8},{10,11... | collective-permute-start | bytes 405512 | tf_op jit(solution)/shard_map/ppermute | solution.py:685
  88.8 0.0 collective-permute-done.14.refs_2_
  88.8 0.0 collective-permute-start.9
  88.9 0.0 collective-permute-done.13.refs_1_
  88.9 1.7 %collective-permute-start.21 = (s32[264,128]{1,0:T(8,128)S(1)}, s32[264,128]{1,0:T(8,128)}, u32[]{:S(2)}, u32[]{:S(2)}) collective-permute-start(s32[264,128]{1,0:T(8,128)S(1)} %collective-permute-done.8.refs_8_), channel_id=1, source_target_pairs={{0,2},{1,3},{2,0},{3,1},{4,6},{5,7},{6,4},{7,5},{8,10},{9,11},{10,... | collective-permute-start | bytes 405512 | tf_op jit(solution)/shard_map/ppermute | solution.py:685
  90.6 0.0 collective-permute-done.18.refs_6_
  90.6 0.4 collective-permute-start.15
  91.0 0.0 collective-permute-done.17.refs_5_
  91.0 0.6 collective-permute-start.19
  91.5 1.5 %collective-permute-done.20.refs_9_ = s32[264,128]{1,0:T(8,128)S(1)} collective-permute-done((s32[264,128]{1,0:T(8,128)S(1)}, s32[264,128]{1,0:T(8,128)S(1)}, u32[]{:S(2)}, u32[]{:S(2)}) %collective-permute-start.20) | collective-permute-done | bytes 135200 | tf_op jit(solution)/shard_map/ppermute | solution.py:685
  93.1 1.6 %collective-permute-start.22 = (s32[264,128]{1,0:T(8,128)S(1)}, s32[264,128]{1,0:T(8,128)}, u32[]{:S(2)}, u32[]{:S(2)}) collective-permute-start(s32[264,128]{1,0:T(8,128)S(1)} %collective-permute-done.20.refs_9_), channel_id=1, source_target_pairs={{0,2},{1,3},{2,0},{3,1},{4,6},{5,7},{6,4},{7,5},{8,10},{9,11},{10,... | collective-permute-start | bytes 405512 | tf_op jit(solution)/shard_map/ppermute | solution.py:685
  94.7 0.0 collective-permute-done.9.refs_0_
  94.7 0.8 collective-permute-start.10
  95.5 0.0 all-to-all-done.1.words_ref
  95.5 3.6 %decode_mixer.1 = f32[2,16,128,128]{3,2,1,0:T(8,128)} custom-call(s32[16,136,128]{2,1,0:T(8,128)} %all-to-all-done.1.words_ref), custom_call_target="tpu_custom_call" | custom-call | flops 2000000000 | bytes 6000000 | tf_op jit(solution)/shard_map/decode_mixer/pallas_call | solution.py:362
  99.2 0.0 collective-permute-done.15.refs_3_
  99.2 1.7 %collective-permute-start.11 = (s32[264,128]{1,0:T(8,128)S(1)}, s32[264,128]{1,0:T(8,128)S(1)}, u32[]{:S(2)}, u32[]{:S(2)}) collective-permute-start(s32[264,128]{1,0:T(8,128)S(1)} %collective-permute-done.9.refs_0_), channel_id=1, source_target_pairs={{0,1},{1,0},{2,3},{3,2},{4,5},{5,4},{6,7},{7,6},{8,9},{9,8},{10,11... | collective-permute-start | bytes 405512 | tf_op jit(solution)/shard_map/ppermute | solution.py:685
  100.9 1.0 collective-permute-done.10.refs_1_
  101.9 0.6 collective-permute-start.12
  102.4 0.0 collective-permute-done.21.refs_10_
  102.4 0.0 collective-permute-done.19.refs_7_
  102.4 0.0 collective-permute-done.22.refs_11_
  102.5 3.4 %unpack_table.2.refs_4_ = f32[512,2048]{1,0:T(8,128)} custom-call(s32[2]{0:T(128)S(1)} %copy-done.1, s32[264,128]{1,0:T(8,128)S(1)} %pack_table.1.refs_0_, s32[264,128]{1,0:T(8,128)S(1)} %collective-permute-done.13.refs_1_, s32[264,128]{1,0:T(8,128)S(1)} %collective-permute-done.14.refs_2_, s32[264,128]{1,0:T(8,128)} %collective-permute-done.15.refs_3_, ...), custom_call_target="tpu_custom_call" | custom-call | flops 2500000000 | bytes 7500000 | tf_op jit(solution)/shard_map/unpack_table/pallas_call | solution.py:410
  105.9 0.0 collective-permute-done.11.refs_2_
  105.9 1.0 collective-permute-done.12.refs_3_
  106.9 1.6 %unpack_table.3 = f32[512,2048]{1,0:T(8,128)} custom-call(s32[2]{0:T(128)S(1)} %copy-done.1, s32[264,128]{1,0:T(8,128)S(1)} %collective-permute-done.9.refs_0_, s32[264,128]{1,0:T(8,128)S(1)} %collective-permute-done.10.refs_1_, s32[264,128]{1,0:T(8,128)S(1)} %collective-permute-done.11.refs_2_, ...), custom_call_target="tpu_custom_call", output_to_operand_aliasing={{}: (5, {})} | custom-call | flops 1500000000 | bytes 4500000 | tf_op jit(solution)/shard_map/unpack_table/pallas_call | solution.py:410
  (19 shorter events, 0.1 us)
Async XLA Ops:
  0.6 5.7 %copy-start = (bf16[512,2048]{1,0:T(8,128)(2,1)S(1)}, bf16[512,2048]{1,0:T(8,128)(2,1)}, u32[]{:S(2)}) copy-start(bf16[512,2048]{1,0:T(8,128)(2,1)} %param.12) | copy-start | bytes 6291460
  0.6 16.3 %collective-permute-start.2 = (s32[1,128]{1,0:T(1,128)}, s32[1,128]{1,0:T(1,128)S(1)}, u32[]{:S(2)}, u32[]{:S(2)}) collective-permute-start(s32[1,128]{1,0:T(1,128)} %param.11), channel_id=1, source_target_pairs={{0,8},{1,9},{2,10},{3,11},{4,12},{5,13},{6,14},{7,15},{8,0},{9,1},... | collective-permute-start | bytes 1544 | tf_op jit(solution)/shard_map/ppermute | solution.py:677
  4.7 12.2 %collective-permute-start.1 = (s32[1,128]{1,0:T(1,128)}, s32[1,128]{1,0:T(1,128)S(1)}, u32[]{:S(2)}, u32[]{:S(2)}) collective-permute-start(s32[1,128]{1,0:T(1,128)} %param.11), channel_id=1, source_target_pairs={{0,4},{1,5},{2,6},{3,7},{4,0},{5,1},{6,2},{7,3},{8,12},{9,13},{10,... | collective-permute-start | bytes 1544 | tf_op jit(solution)/shard_map/ppermute | solution.py:677
  6.3 10.6 %collective-permute-start.3 = (s32[1,128]{1,0:T(1,128)}, s32[1,128]{1,0:T(1,128)S(1)}, u32[]{:S(2)}, u32[]{:S(2)}) collective-permute-start(s32[1,128]{1,0:T(1,128)} %param.11), channel_id=1, source_target_pairs={{0,12},{1,13},{2,14},{3,15},{4,8},{5,9},{6,10},{7,11},{8,4},{9,5},... | collective-permute-start | bytes 1544 | tf_op jit(solution)/shard_map/ppermute | solution.py:677
  6.4 2.7 %copy-start.4 = (bf16[512,128]{1,0:T(8,128)(2,1)}, bf16[512,128]{1,0:T(8,128)(2,1)S(1)}, u32[]{:S(2)}) copy-start(bf16[512,128]{1,0:T(8,128)(2,1)S(1)} %constant_dynamic-slice_fusion.own_ref) | copy-start | bytes 393220
  6.4 14.1 %collective-permute-start = (bf16[512,128]{1,0:T(8,128)(2,1)S(1)}, bf16[512,128]{1,0:T(8,128)(2,1)S(1)}, u32[]{:S(2)}, u32[]{:S(2)}) collective-permute-start(bf16[512,128]{1,0:T(8,128)(2,1)S(1)} %constant_dynamic-slice_fusion.own_ref), channel_id=1, source_target_pairs={{0,16},{16,0},{1,17},{17,1},{2,18},{18,2},{3,19},{19,3},{4,20},{20... | collective-permute-start | bytes 393224 | tf_op jit(solution)/shard_map/ppermute | solution.py:721
  9.1 7.9 %copy-start.6 = (s32[1,128]{1,0:T(1,128)S(1)}, s32[1,128]{1,0:T(1,128)}, u32[]{:S(2)}) copy-start(s32[1,128]{1,0:T(1,128)} %param.11) | copy-start | bytes 1540
  9.1 39.2 %all-to-all-start = ((s32[16,136,128]{2,1,0:T(8,128)}), s32[16,136,128]{2,1,0:T(8,128)S(1)}, u32[]{:S(2)}, u32[]{:S(2)}) async-start(s32[16,136,128]{2,1,0:T(8,128)} %encode_cotangent.1), calls=%async_computation | async-start | bytes 2228224 | tf_op jit(solution)/shard_map/all_to_all | solution.py:713
  16.9 17.0 %copy-start.5 = (s32[4,128]{1,0:T(4,128)}, s32[4,128]{1,0:T(4,128)S(1)}, u32[]{:S(2)}) copy-start(s32[4,128]{1,0:T(4,128)S(1)} %pad_add_fusion.refs_0_) | copy-start | bytes 6148
  17.0 17.0 %collective-permute-start.6 = (s32[4,128]{1,0:T(4,128)S(1)}, s32[4,128]{1,0:T(4,128)S(1)}, u32[]{:S(2)}, u32[]{:S(2)}) collective-permute-start(s32[4,128]{1,0:T(4,128)S(1)} %pad_add_fusion.refs_0_), channel_id=1, source_target_pairs={{0,3},{1,2},{2,1},{3,0},{4,7},{5,6},{6,5},{7,4},{8,11},{9,10},{10,... | collective-permute-start | bytes 6152 | tf_op jit(solution)/shard_map/ppermute | solution.py:677
  19.8 14.2 %collective-permute-start.5 = (s32[4,128]{1,0:T(4,128)S(1)}, s32[4,128]{1,0:T(4,128)S(1)}, u32[]{:S(2)}, u32[]{:S(2)}) collective-permute-start(s32[4,128]{1,0:T(4,128)S(1)} %pad_add_fusion.refs_0_), channel_id=1, source_target_pairs={{0,2},{1,3},{2,0},{3,1},{4,6},{5,7},{6,4},{7,5},{8,10},{9,11},{10,... | collective-permute-start | bytes 6152 | tf_op jit(solution)/shard_map/ppermute | solution.py:677
  20.4 13.6 %collective-permute-start.4 = (s32[4,128]{1,0:T(4,128)S(1)}, s32[4,128]{1,0:T(4,128)S(1)}, u32[]{:S(2)}, u32[]{:S(2)}) collective-permute-start(s32[4,128]{1,0:T(4,128)S(1)} %pad_add_fusion.refs_0_), channel_id=1, source_target_pairs={{0,1},{1,0},{2,3},{3,2},{4,5},{5,4},{6,7},{7,6},{8,9},{9,8},{10,11... | collective-permute-start | bytes 6152 | tf_op jit(solution)/shard_map/ppermute | solution.py:677
  20.5 13.4 %copy-start.7 = (bf16[512,128]{1,0:T(8,128)(2,1)}, bf16[512,128]{1,0:T(8,128)(2,1)S(1)}, u32[]{:S(2)}) copy-start(bf16[512,128]{1,0:T(8,128)(2,1)S(1)} %collective-permute-done.other_ref) | copy-start | bytes 393220
  34.0 0.5 copy-start.8
  34.0 0.6 copy-start.9
  34.0 0.6 copy-start.10
  48.3 7.0 %copy-start.3 = (s32[16,136,128]{2,1,0:T(8,128)}, s32[16,136,128]{2,1,0:T(8,128)S(1)}, u32[]{:S(2)}) copy-start(s32[16,136,128]{2,1,0:T(8,128)S(1)} %all-to-all-done.words_ref) | copy-start | bytes 3342340
  48.3 47.2 %all-to-all-start.1 = ((s32[16,136,128]{2,1,0:T(8,128)}), s32[16,136,128]{2,1,0:T(8,128)}, u32[]{:S(2)}, u32[]{:S(2)}) async-start(s32[16,136,128]{2,1,0:T(8,128)} %get-tuple-element.24), calls=%async_computation.1 | async-start | bytes 2228224 | tf_op jit(solution)/shard_map/all_to_all | solution.py:713
  71.1 1.8 %collective-permute-start.7 = (f32[512,128]{1,0:T(8,128)}, f32[512,128]{1,0:T(8,128)S(1)}, u32[]{:S(2)}, u32[]{:S(2)}) collective-permute-start(f32[512,128]{1,0:T(8,128)} %get-tuple-element.23), channel_id=1, source_target_pairs={{0,16},{16,0},{1,17},{17,1},{2,18},{18,2},{3,19},{19,3},{4,20},{20... | collective-permute-start | bytes 786440 | tf_op jit(solution)/shard_map/ppermute | solution.py:820
  72.9 1.0 copy-start.2
  73.9 28.5 %copy-start.1 = (s32[2]{0:T(128)S(1)}, s32[2]{0:T(128)}, u32[]{:S(2)}) copy-start(s32[2]{0:T(128)} %pad_add_fusion.1._.place_ref) | copy-start | bytes 28
  73.9 8.1 %collective-permute-start.16 = (s32[264,128]{1,0:T(8,128)S(1)}, s32[264,128]{1,0:T(8,128)S(1)}, u32[]{:S(2)}, u32[]{:S(2)}) collective-permute-start(s32[264,128]{1,0:T(8,128)S(1)} %pack_table.1.refs_0_), channel_id=1, source_target_pairs={{0,4},{1,5},{2,6},{3,7},{4,0},{5,1},{6,2},{7,3},{8,12},{9,13},{10,... | collective-permute-start | bytes 405512 | tf_op jit(solution)/shard_map/ppermute | solution.py:685
  75.9 11.5 %collective-permute-start.8 = (s32[264,128]{1,0:T(8,128)S(1)}, s32[264,128]{1,0:T(8,128)S(1)}, u32[]{:S(2)}, u32[]{:S(2)}) collective-permute-start(s32[264,128]{1,0:T(8,128)S(1)} %pack_table.1.refs_0_), channel_id=1, source_target_pairs={{0,8},{1,9},{2,10},{3,11},{4,12},{5,13},{6,14},{7,15},{8,0},{9,1},... | collective-permute-start | bytes 405512 | tf_op jit(solution)/shard_map/ppermute | solution.py:685
  78.2 10.6 %collective-permute-start.14 = (s32[264,128]{1,0:T(8,128)S(1)}, s32[264,128]{1,0:T(8,128)S(1)}, u32[]{:S(2)}, u32[]{:S(2)}) collective-permute-start(s32[264,128]{1,0:T(8,128)S(1)} %pack_table.1.refs_0_), channel_id=1, source_target_pairs={{0,2},{1,3},{2,0},{3,1},{4,6},{5,7},{6,4},{7,5},{8,10},{9,11},{10,... | collective-permute-start | bytes 405512 | tf_op jit(solution)/shard_map/ppermute | solution.py:685
  79.7 9.2 %collective-permute-start.13 = (s32[264,128]{1,0:T(8,128)S(1)}, s32[264,128]{1,0:T(8,128)S(1)}, u32[]{:S(2)}, u32[]{:S(2)}) collective-permute-start(s32[264,128]{1,0:T(8,128)S(1)} %pack_table.1.refs_0_), channel_id=1, source_target_pairs={{0,1},{1,0},{2,3},{3,2},{4,5},{5,4},{6,7},{7,6},{8,9},{9,8},{10,11... | collective-permute-start | bytes 405512 | tf_op jit(solution)/shard_map/ppermute | solution.py:685
  82.0 8.6 %collective-permute-start.18 = (s32[264,128]{1,0:T(8,128)S(1)}, s32[264,128]{1,0:T(8,128)S(1)}, u32[]{:S(2)}, u32[]{:S(2)}) collective-permute-start(s32[264,128]{1,0:T(8,128)S(1)} %collective-permute-done.16.refs_4_), channel_id=1, source_target_pairs={{0,1},{1,0},{2,3},{3,2},{4,5},{5,4},{6,7},{7,6},{8,9},{9,8},{10,11... | collective-permute-start | bytes 405512 | tf_op jit(solution)/shard_map/ppermute | solution.py:685
  83.5 7.5 %collective-permute-start.17 = (s32[264,128]{1,0:T(8,128)S(1)}, s32[264,128]{1,0:T(8,128)S(1)}, u32[]{:S(2)}, u32[]{:S(2)}) collective-permute-start(s32[264,128]{1,0:T(8,128)S(1)} %collective-permute-done.16.refs_4_), channel_id=1, source_target_pairs={{0,2},{1,3},{2,0},{3,1},{4,6},{5,7},{6,4},{7,5},{8,10},{9,11},{10,... | collective-permute-start | bytes 405512 | tf_op jit(solution)/shard_map/ppermute | solution.py:685
  87.4 5.7 %collective-permute-start.20 = (s32[264,128]{1,0:T(8,128)S(1)}, s32[264,128]{1,0:T(8,128)S(1)}, u32[]{:S(2)}, u32[]{:S(2)}) collective-permute-start(s32[264,128]{1,0:T(8,128)S(1)} %collective-permute-done.8.refs_8_), channel_id=1, source_target_pairs={{0,1},{1,0},{2,3},{3,2},{4,5},{5,4},{6,7},{7,6},{8,9},{9,8},{10,11... | collective-permute-start | bytes 405512 | tf_op jit(solution)/shard_map/ppermute | solution.py:685
  88.8 5.8 %collective-permute-start.9 = (s32[264,128]{1,0:T(8,128)S(1)}, s32[264,128]{1,0:T(8,128)S(1)}, u32[]{:S(2)}, u32[]{:S(2)}) collective-permute-start(s32[264,128]{1,0:T(8,128)S(1)} %collective-permute-done.8.refs_8_), channel_id=1, source_target_pairs={{0,4},{1,5},{2,6},{3,7},{4,0},{5,1},{6,2},{7,3},{8,12},{9,13},{10,... | collective-permute-start | bytes 405512 | tf_op jit(solution)/shard_map/ppermute | solution.py:685
  88.9 13.6 %collective-permute-start.21 = (s32[264,128]{1,0:T(8,128)S(1)}, s32[264,128]{1,0:T(8,128)}, u32[]{:S(2)}, u32[]{:S(2)}) collective-permute-start(s32[264,128]{1,0:T(8,128)S(1)} %collective-permute-done.8.refs_8_), channel_id=1, source_target_pairs={{0,2},{1,3},{2,0},{3,1},{4,6},{5,7},{6,4},{7,5},{8,10},{9,11},{10,... | collective-permute-start | bytes 405512 | tf_op jit(solution)/shard_map/ppermute | solution.py:685
  90.6 8.6 %collective-permute-start.15 = (s32[264,128]{1,0:T(8,128)S(1)}, s32[264,128]{1,0:T(8,128)}, u32[]{:S(2)}, u32[]{:S(2)}) collective-permute-start(s32[264,128]{1,0:T(8,128)S(1)} %collective-permute-done.13.refs_1_), channel_id=1, source_target_pairs={{0,2},{1,3},{2,0},{3,1},{4,6},{5,7},{6,4},{7,5},{8,10},{9,11},{10,... | collective-permute-start | bytes 405512 | tf_op jit(solution)/shard_map/ppermute | solution.py:685
  91.0 11.5 %collective-permute-start.19 = (s32[264,128]{1,0:T(8,128)S(1)}, s32[264,128]{1,0:T(8,128)}, u32[]{:S(2)}, u32[]{:S(2)}) collective-permute-start(s32[264,128]{1,0:T(8,128)S(1)} %collective-permute-done.17.refs_5_), channel_id=1, source_target_pairs={{0,1},{1,0},{2,3},{3,2},{4,5},{5,4},{6,7},{7,6},{8,9},{9,8},{10,11... | collective-permute-start | bytes 405512 | tf_op jit(solution)/shard_map/ppermute | solution.py:685
  93.1 9.4 %collective-permute-start.22 = (s32[264,128]{1,0:T(8,128)S(1)}, s32[264,128]{1,0:T(8,128)}, u32[]{:S(2)}, u32[]{:S(2)}) collective-permute-start(s32[264,128]{1,0:T(8,128)S(1)} %collective-permute-done.20.refs_9_), channel_id=1, source_target_pairs={{0,2},{1,3},{2,0},{3,1},{4,6},{5,7},{6,4},{7,5},{8,10},{9,11},{10,... | collective-permute-start | bytes 405512 | tf_op jit(solution)/shard_map/ppermute | solution.py:685
  94.7 7.2 %collective-permute-start.10 = (s32[264,128]{1,0:T(8,128)S(1)}, s32[264,128]{1,0:T(8,128)S(1)}, u32[]{:S(2)}, u32[]{:S(2)}) collective-permute-start(s32[264,128]{1,0:T(8,128)S(1)} %collective-permute-done.9.refs_0_), channel_id=1, source_target_pairs={{0,2},{1,3},{2,0},{3,1},{4,6},{5,7},{6,4},{7,5},{8,10},{9,11},{10,... | collective-permute-start | bytes 405512 | tf_op jit(solution)/shard_map/ppermute | solution.py:685
  99.2 6.7 %collective-permute-start.11 = (s32[264,128]{1,0:T(8,128)S(1)}, s32[264,128]{1,0:T(8,128)S(1)}, u32[]{:S(2)}, u32[]{:S(2)}) collective-permute-start(s32[264,128]{1,0:T(8,128)S(1)} %collective-permute-done.9.refs_0_), channel_id=1, source_target_pairs={{0,1},{1,0},{2,3},{3,2},{4,5},{5,4},{6,7},{7,6},{8,9},{9,8},{10,11... | collective-permute-start | bytes 405512 | tf_op jit(solution)/shard_map/ppermute | solution.py:685
  101.9 5.0 %collective-permute-start.12 = (s32[264,128]{1,0:T(8,128)S(1)}, s32[264,128]{1,0:T(8,128)S(1)}, u32[]{:S(2)}, u32[]{:S(2)}) collective-permute-start(s32[264,128]{1,0:T(8,128)S(1)} %collective-permute-done.10.refs_1_), channel_id=1, source_target_pairs={{0,1},{1,0},{2,3},{3,2},{4,5},{5,4},{6,7},{7,6},{8,9},{9,8},{10,11... | collective-permute-start | bytes 405512 | tf_op jit(solution)/shard_map/ppermute | solution.py:685

commit v5 on v4

--- a/solution.py
+++ b/solution.py
@@ -277,34 +277,27 @@
 LOG2_E = math.log2(math.e)
 
 
-def modal_rows(residues, decays, seeds, blocks):
-    rates = decays * -LOG2_E
-    turns = seeds.astype(F32) * (1.0 / PERIOD)
-    weights = residues * jnp.sqrt(decays + 1.0 / (blocks * LANES))
+def modal_rows(rates, turns, blocks):
     leap = jnp.exp2(rates * LANES)
     c, s = unit_turn(turns * LANES)
-    rows = [rates, turns, leap * c, leap * s, 2.0 * (leap * c), leap * leap]
-    for start in range(0, blocks, RESTART):
-        fall = weights * jnp.exp2(rates * (LANES * start))
+    rows = [leap * c, leap * s, 2.0 * (leap * c), leap * leap]
+    for start in range(RESTART, blocks, RESTART):
+        fall = jnp.exp2(rates * (LANES * start))
         c, s = unit_turn(turns * (LANES * start))
         rows += [fall * c, fall * s]
     return rows
 
 
-def filter_tile(row, time, blocks, modes):
+def filter_tile(row, far, near, blocks, modes):
     total = [None] * blocks
     for mode in range(modes):
-        rate, turns, jump_re, jump_im, ahead, behind = (row(i, mode) for i in range(6))
-        c, s = unit_turn(turns * time)
-        fall = jnp.exp2(rate * time)
-        re, im = fall * c, fall * s
+        jump_re, jump_im, ahead, behind = (row(i, mode) for i in range(4))
+        far_re, far_im, near_re, near_im = far(0, mode), far(1, mode), near(0, mode), near(1, mode)
+        re, im = far_re * near_re - far_im * near_im, far_re * near_im + far_im * near_re
         for first in range(0, blocks, RESTART):
-            place = 6 + 2 * (first // RESTART)
-            if first == 0:
-                weight = row(place, mode)
-                a, b = weight * re, weight * im
-            else:
-                start_re, start_im = row(place, mode), row(place + 1, mode)
+            a, b = re, im
+            if first:
+                start_re, start_im = (row(2 + 2 * (first // RESTART) + i, mode) for i in range(2))
                 a, b = start_re * re - start_im * im, start_re * im + start_im * re
             old, new = a, jump_re * a - jump_im * b
             for block in range(first, min(first + RESTART, blocks)):
@@ -334,12 +327,21 @@
         out_ref[i, height:, :] = code
 
 
-def decode_kernel(words_ref, out_ref):
-    height = out_ref.shape[2]
-    for i in range(out_ref.shape[1]):
-        upper, lower = unpack_pair(words_ref[i, :height, :], words_ref[i, height : height + 1, :])
-        out_ref[0, i] = upper
-        out_ref[1, i] = lower
+def decode_kernel(held_ref, out_ref, words_ref, value_ref, in_sems, sems):
+    blocks, height = value_ref.shape[1:3]
+    copies = []
+    fetches = [pltpu.make_async_copy(held_ref.at[i], words_ref.at[i], in_sems.at[i]) for i in range(blocks)]
+    for fetch in fetches:
+        fetch.start()
+    for block in range(blocks):
+        fetches[block].wait()
+        upper, lower = unpack_pair(words_ref[block, :height, :], words_ref[block, height : height + 1, :])
+        value_ref[0, block] = upper
+        value_ref[1, block] = lower
+        copies.append(pltpu.make_async_copy(value_ref.at[:, block], out_ref.at[:, block], sems.at[block]))
+        copies[-1].start()
+    for copy in copies:
+        copy.wait()
 
 
 def encode(value, blocks):
@@ -358,13 +360,18 @@
 
 def decode(words, blocks):
     half = words.shape[1] - SUBLANES
-    some = blocks // 4
     out = pl.pallas_call(
         decode_kernel,
-        grid=(blocks // some,),
-        in_specs=[pl.BlockSpec((some, half + SUBLANES, LANES), lambda i: (i, 0, 0))],
-        out_specs=pl.BlockSpec((2, some, half, LANES), lambda i: (0, i, 0, 0)),
+        in_specs=anywhere(1),
+        out_specs=anywhere(1)[0],
         out_shape=jax.ShapeDtypeStruct((2, blocks, half, LANES), F32),
+        scratch_shapes=[
+            pltpu.VMEM(words.shape, jnp.int32),
+            pltpu.VMEM((2, blocks, half, LANES), F32),
+            pltpu.SemaphoreType.DMA((blocks,)),
+            pltpu.SemaphoreType.DMA((blocks,)),
+        ],
+        compiler_params=pltpu.CompilerParams(vmem_limit_bytes=VMEM_BYTES),
         cost_estimate=takes(2),
         name="decode_mixer",
     )(words)
@@ -424,44 +431,66 @@
     )(place, *parts, *held)
 
 
-def hold_tokens(refs, token_ref):
-    count = refs[0].shape[0]
-    for index, ref in enumerate(refs):
-        token_ref[index * count : (index + 1) * count, :] = ref[...]
-
-
-def token_row(block, place_ref, pieces):
-    if pieces == 1:
-        return block
+def token_row(token_ref, block, place_ref):
+    if token_ref.shape[0] == 1:
+        return token_ref[0, block : block + 1, :]
     away = place_ref[0] ^ block
-    return 4 * (away & 3) + (away >> 2)
-
-
-def one_hot_block(token_ref, block, vocab):
-    wanted = token_ref[pl.ds(block, 1), :]
+    return token_ref[away & 3, pl.ds(away >> 2, 1), :]
+
+
+def one_hot_block(wanted, vocab):
     entry = lax.broadcasted_iota(jnp.int32, (vocab, LANES), 0)
     return (entry == wanted).astype(F32).astype(BF16)
 
 
 def filter_kernel(
-    _,
-    tap_ref, tap_next_ref, gain_ref, gain_next_ref, residue_ref, residue_next_ref, decay_ref, decay_next_ref, seed_ref, seed_next_ref,
-    ahead_ref, twist_ref,
-    response_out, side_out,
-    work_ref, response_ref, mode_ref, taken_ref, time_ref, side_ref, sems,
+    aligned, place_ref, tap_in, gain_in, residue_in, decay_in, seed_in, ahead_in, twist_in, response_out, side_out,
+    tap_ref, gain_ref, residue_ref, decay_ref, seed_ref, ahead_ref, twist_ref,
+    work_ref, response_ref, mode_ref, far_ref, near_ref, taken_ref, time_ref, side_ref, sems, in_sems,
 ):
     slots, channels, _ = response_ref.shape
     blocks = slots - 1
     half = channels // 2
-    modes = residue_ref.shape[0]
+    modes = residue_ref.shape[1]
+    copies = []
+    for index in range(2):
+        first = pl.multiple_of((index * blocks + place_ref[0]) * half, half)
+        for held, ref in (
+            (residue_in, residue_ref),
+            (decay_in, decay_ref),
+            (seed_in, seed_ref),
+            (tap_in, tap_ref),
+            (gain_in, gain_ref),
+        ):
+            part = held.at[(*[slice(None)] * (len(held.shape) - 1), pl.ds(first, half))] if aligned else held.at[index]
+            copies.append((part, ref.at[index]))
+    copies += [(twist_in, twist_ref), (ahead_in, ahead_ref)]
+    copies = [pltpu.make_async_copy(*pair, in_sems.at[i]) for i, pair in enumerate(copies)]
+    for copy in copies:
+        copy.start()
+    for copy in copies[:10]:
+        copy.wait()
     sides = []
-    for index, (taps, gain, residues, decays, seeds) in enumerate((
-        (tap_ref, gain_ref, residue_ref, decay_ref, seed_ref),
-        (tap_next_ref, gain_next_ref, residue_next_ref, decay_next_ref, seed_next_ref),
-    )):
-        for i, rows in enumerate(modal_rows(residues[...], decays[...], seeds[...], blocks)):
+    for index in range(2):
+        decays = decay_ref[index]
+        rates = decays * -LOG2_E
+        turns = seed_ref[index].astype(F32) * (1.0 / PERIOD)
+        weights = residue_ref[index] * jnp.sqrt(decays + 1.0 / (blocks * LANES))
+        for i, rows in enumerate(modal_rows(rates, turns, blocks)):
             mode_ref[index, i] = rows
-        listed = jnp.concatenate([taps[0], taps[1], taps[2], gain[...]], axis=0)
+        for number in range(LANES // SUBLANES):
+            fall = jnp.exp2(rates * (SUBLANES * number))
+            c, s = unit_turn(turns * (SUBLANES * number))
+            far_ref[index, number, 0] = fall * c
+            far_ref[index, number, 1] = fall * s
+        time = lax.broadcasted_iota(jnp.int32, (SUBLANES, half), 0).astype(F32)
+        for mode in range(modes):
+            row = slice(mode, mode + 1)
+            fall = weights[row] * jnp.exp2(rates[row] * time)
+            c, s = unit_turn(turns[row] * time)
+            near_ref[index, 0, mode] = fall * c
+            near_ref[index, 1, mode] = fall * s
+        listed = jnp.concatenate([tap_ref[index, 0], tap_ref[index, 1], tap_ref[index, 2], gain_ref[index]], axis=0)
         sides.append(jnp.pad(listed, ((0, LANES - listed.shape[0]), (0, 0))).T)
     sides = jnp.concatenate(sides, axis=0)
     for i in range(SIDES):
@@ -473,8 +502,13 @@
 
         def tile(number, carry):
             first = pl.multiple_of(number * SUBLANES, SUBLANES)
-            time = (lax.broadcasted_iota(jnp.int32, (SUBLANES, half), 0) + first).astype(F32)
-            taken = filter_tile(lambda i, mode: mode_ref[index, i, mode : mode + 1, :], time, blocks, modes)
+            taken = filter_tile(
+                lambda i, mode: mode_ref[index, i, mode : mode + 1, :],
+                lambda i, mode: far_ref[index, number, i, mode : mode + 1, :],
+                lambda i, mode: near_ref[index, i, mode],
+                blocks,
+                modes,
+            )
             for block in range(blocks):
                 taken_ref[index, block, pl.ds(first, SUBLANES), :] = taken[block]
             return carry
@@ -489,6 +523,8 @@
         store_spectrum(work_ref, rows, padded_real_dft([time_ref[block, rows, :] for block in range(blocks)]))
 
     for_tiles(channels, 4, transforms)
+    for copy in copies[10:]:
+        copy.wait()
 
     def step(k):
         response_ref[k] = inner_ahead(work_ref[k], twist_ref[k], ahead_ref[...])
@@ -515,30 +551,34 @@
     over_slots(work_ref.shape[0], step)
 
 
-def forward_kernel(pieces, place_ref, own_ref, other_ref, *refs):
-    token_refs, token_ref, refs = refs[:pieces], refs[-1], refs[pieces:-1]
-    hold_tokens(token_refs, token_ref)
-    held, (words_out_ref, long_out_ref, stream_out_ref), refs = refs[:5], refs[5:8], refs[8:]
-    side_ref, response_ref, ahead_ref, back_ref, twist_ref, words_ref, long_ref, stream_ref, x_ref, work_ref, sems, word_sems = refs
-    side_copy, *tables = [pltpu.make_async_copy(held[i], refs[i], sems.at[i]) for i in range(5)]
-    stream_copy = pltpu.make_async_copy(stream_ref, stream_out_ref, sems.at[5])
-    long_copy = pltpu.make_async_copy(long_ref, long_out_ref, sems.at[6])
-    side_copy.start()
-    for copy in tables:
+def forward_kernel(pieces, place_ref, *refs):
+    count = pieces + 7
+    held, (words_out_ref, long_out_ref, stream_out_ref), refs = refs[:count], refs[count : count + 3], refs[count + 3 :]
+    token_ref, own_ref, other_ref, side_ref, response_ref, ahead_ref, back_ref, twist_ref = refs[:8]
+    words_ref, long_ref, stream_ref, x_ref, work_ref, sems, word_sems = refs[8:]
+    copies = [
+        pltpu.make_async_copy(held[i], ref, sems.at[i])
+        for i, ref in enumerate([token_ref.at[j] for j in range(pieces)] + list(refs[1:8]))
+    ]
+    for copy in copies:
         copy.start()
+    stream_copy = pltpu.make_async_copy(stream_ref, stream_out_ref, sems.at[count])
+    long_copy = pltpu.make_async_copy(long_ref, long_out_ref, sems.at[count + 1])
     blocks, channels, _ = x_ref.shape
     half = channels // 2
     vocab = own_ref.shape[0]
+    for copy in copies[: pieces + 2]:
+        copy.wait()
     own, other = own_ref[...].astype(F32).T, other_ref[...].astype(F32).T
     first = place_ref[1] == 0
     tall = jnp.concatenate([jnp.where(first, own, other), jnp.where(first, other, own)], axis=0).astype(BF16)
 
     for pair in range(blocks // 2):
-        hot = jnp.concatenate([one_hot_block(token_ref, token_row(2 * pair + i, place_ref, pieces), vocab) for i in range(2)], axis=1)
+        hot = jnp.concatenate([one_hot_block(token_row(token_ref, 2 * pair + i, place_ref), vocab) for i in range(2)], axis=1)
         found = jnp.dot(tall, hot, preferred_element_type=F32)
         x_ref[2 * pair] = found[:, :LANES]
         x_ref[2 * pair + 1] = found[:, LANES:]
-    side_copy.wait()
+    copies[pieces + 2].wait()
 
     def streams(rows):
         lane = lax.broadcasted_iota(jnp.int32, (SUBLANES, LANES), 1)
@@ -554,7 +594,7 @@
 
     for_tiles(channels, 4, streams)
     stream_copy.start()
-    for copy in tables:
+    for copy in copies[pieces + 3 :]:
         copy.wait()
     filtered(work_ref, response_ref, ahead_ref, back_ref, twist_ref, 1.0)
 
@@ -583,19 +623,25 @@
     long_copy.wait()
 
 
-def backward_kernel(pieces, place_ref, words_ref, *refs):
-    token_refs, token_ref, refs = refs[:pieces], refs[-1], refs[pieces:-1]
-    hold_tokens(token_refs, token_ref)
-    held, (mine_ref, theirs_ref), refs = refs[:7], refs[7:9], refs[9:]
-    stream_ref, response_ref, ahead_ref, back_ref, twist_ref, side_ref, long_ref, work_ref, cot_ref, late_ref, sems = refs
-    query_copy = pltpu.make_async_copy(held[0].at[0], stream_ref.at[0], sems.at[0])
-    tables = [pltpu.make_async_copy(held[i], refs[i], sems.at[i]) for i in range(1, 5)]
-    rest = [pltpu.make_async_copy(held[i], refs[i], sems.at[i]) for i in range(5, 7)]
-    rest += [pltpu.make_async_copy(held[0].at[i], stream_ref.at[i], sems.at[6 + i]) for i in range(1, 3)]
+def backward_kernel(pieces, place_ref, *refs):
+    count = pieces + 8
+    held, (mine_out_ref, theirs_out_ref), refs = refs[:count], refs[count : count + 2], refs[count + 2 :]
+    token_ref, words_ref, stream_ref, response_ref, ahead_ref, back_ref, twist_ref, side_ref, long_ref = refs[:9]
+    mine_ref, theirs_ref, work_ref, cot_ref, late_ref, sems = refs[9:]
+    words_copy = pltpu.make_async_copy(held[pieces], words_ref, sems.at[pieces])
+    query_copy = pltpu.make_async_copy(held[pieces + 1].at[0], stream_ref.at[0], sems.at[pieces + 1])
+    tables = [pltpu.make_async_copy(held[pieces + i], refs[1 + i], sems.at[pieces + i]) for i in range(2, 6)]
+    rest = [pltpu.make_async_copy(held[pieces + i], refs[1 + i], sems.at[pieces + i]) for i in range(6, 8)]
+    rest += [
+        pltpu.make_async_copy(held[pieces + 1].at[i], stream_ref.at[i], sems.at[count + i - 1]) for i in range(1, 3)
+    ]
+    rest += [pltpu.make_async_copy(held[i], token_ref.at[i], sems.at[i]) for i in range(pieces)]
+    words_copy.start()
     query_copy.start()
     blocks, channels, _ = cot_ref.shape
     half = channels // 2
     vocab = mine_ref.shape[0]
+    words_copy.wait()
 
     for block in range(blocks):
         upper, lower = unpack_pair(words_ref[block, :half, :], words_ref[block, half : half + 1, :])
@@ -648,7 +694,7 @@
     total = None
     for start in range(0, blocks, 4):
         some = range(start, start + 4)
-        hot = jnp.concatenate([one_hot_block(token_ref, token_row(block, place_ref, pieces), vocab) for block in some], axis=1)
+        hot = jnp.concatenate([one_hot_block(token_row(token_ref, block, place_ref), vocab) for block in some], axis=1)
         value = jnp.concatenate([late_ref[block] for block in some], axis=1)
         high = value.astype(BF16)
         low = (value - high.astype(F32)).astype(BF16)
@@ -660,8 +706,14 @@
         )
         total = plus(total, part)
     first = place_ref[1] == 0
+    theirs_ref[...] = jnp.where(first, total[:, half:], total[:, :half])
+    theirs_copy = pltpu.make_async_copy(theirs_ref, theirs_out_ref, sems.at[count + 2])
+    theirs_copy.start()
     mine_ref[...] = jnp.where(first, total[:, :half], total[:, half:])
-    theirs_ref[...] = jnp.where(first, total[:, half:], total[:, :half])
+    mine_copy = pltpu.make_async_copy(mine_ref, mine_out_ref, sems.at[count + 3])
+    mine_copy.start()
+    theirs_copy.wait()
+    mine_copy.wait()
 
 
 def anywhere(count):
@@ -728,49 +780,55 @@
     tables = [work, pltpu.VMEM(ahead.shape, BF16), pltpu.VMEM(back.shape, BF16), pltpu.VMEM(twist.shape, F32)]
 
     def halves(value):
-        lead = value.shape[:-1]
-        zeros = (0,) * len(lead)
         if half % LANES == 0:
-            return [value, value], [
-                pl.BlockSpec((*lead, half), lambda i, at: (*zeros, at[0])),
-                pl.BlockSpec((*lead, half), lambda i, at: (*zeros, blocks + at[0])),
-            ]
-        parts = [
-            lax.dynamic_slice_in_dim(value, start + rank * half, half, len(lead)) for start in (0, width // 2)
-        ]
-        return parts, [pl.BlockSpec((*lead, half), lambda i, at: (*zeros, 0))] * 2
-
-    listed = [halves(v) for v in (conv_taps, skip_gain[None], residues.T, decays.T, filter_seed.T)]
+            return value
+        parts = [lax.dynamic_slice_in_dim(value, start + rank * half, half, value.ndim - 1) for start in (0, width // 2)]
+        return jnp.stack(parts)
+
     response, sides = pl.pallas_call(
-        filter_kernel,
+        functools.partial(filter_kernel, half % LANES == 0),
         grid_spec=pltpu.PrefetchScalarGridSpec(
             num_scalar_prefetch=1,
             grid=(1,),
-            in_specs=[spec for _, specs in listed for spec in specs] + in_vmem(2),
+            in_specs=anywhere(7),
             out_specs=tuple(anywhere(2)),
             scratch_shapes=[
+                pltpu.VMEM((2, 3, 3, half), F32),
+                pltpu.VMEM((2, 1, half), F32),
+                pltpu.VMEM((2, modes, half), F32),
+                pltpu.VMEM((2, modes, half), F32),
+                pltpu.VMEM((2, modes, half), jnp.int32),
+                pltpu.VMEM(ahead.shape, BF16),
+                pltpu.VMEM(twist.shape, F32),
                 work,
                 work,
-                pltpu.VMEM((2, 6 + 2 * (-(-blocks // RESTART)), modes, half), F32),
+                pltpu.VMEM((2, 2 + 2 * (-(-blocks // RESTART)), modes, half), F32),
+                pltpu.VMEM((2, LANES // SUBLANES, 2, modes, half), F32),
+                pltpu.VMEM((2, 2, modes, SUBLANES, half), F32),
                 pltpu.VMEM((2, blocks, LANES, half), F32),
                 buffer,
                 pltpu.VMEM((SIDES, channels, LANES), F32),
                 pltpu.SemaphoreType.DMA((slots + 1,)),
+                pltpu.SemaphoreType.DMA((12,)),
             ],
         ),
         out_shape=(jax.ShapeDtypeStruct(spectra, F32), jax.ShapeDtypeStruct((SIDES, channels, LANES), F32)),
         compiler_params=pltpu.CompilerParams(vmem_limit_bytes=VMEM_BYTES),
         cost_estimate=takes(15),
         name="modal_filter",
-    )(place, *[part for parts, _ in listed for part in parts], ahead, twist)
-
+    )(place, *[halves(v) for v in (conv_taps, skip_gain[None], residues.T, decays.T, filter_seed.T)], ahead, twist)
+
+    token_scratch = pltpu.VMEM((len(tokens), *tokens[0].shape), jnp.int32)
     scalars = functools.partial(pltpu.PrefetchScalarGridSpec, num_scalar_prefetch=1, grid=(1,))
     mixer_words, long_out, streams = pl.pallas_call(
         functools.partial(forward_kernel, len(tokens)),
         grid_spec=scalars(
-            in_specs=in_vmem(2 + len(tokens)) + anywhere(5),
+            in_specs=anywhere(len(tokens) + 7),
             out_specs=tuple(anywhere(3)),
             scratch_shapes=[
+                token_scratch,
+                pltpu.VMEM((vocab, half), BF16),
+                pltpu.VMEM((vocab, half), BF16),
                 pltpu.VMEM((SIDES, channels, LANES), F32),
                 *tables,
                 pltpu.VMEM((blocks, half + SUBLANES, LANES), jnp.int32),
@@ -778,9 +836,8 @@
                 pltpu.VMEM((3, blocks, channels, LANES), F32),
                 buffer,
                 work,
-                pltpu.SemaphoreType.DMA((7,)),
+                pltpu.SemaphoreType.DMA((len(tokens) + 9,)),
                 pltpu.SemaphoreType.DMA((blocks,)),
-                pltpu.VMEM((blocks, LANES), jnp.int32),
             ],
         ),
         out_shape=(
@@ -791,32 +848,35 @@
         compiler_params=pltpu.CompilerParams(vmem_limit_bytes=VMEM_BYTES),
         cost_estimate=takes(14),
         name="forward",
-    )(place, own_columns, other_columns, *tokens, sides, response, ahead, back, twist)
+    )(place, *tokens, own_columns, other_columns, sides, response, ahead, back, twist)
 
     mixer_words = exchange(mixer_words)
 
     mine, theirs = pl.pallas_call(
         functools.partial(backward_kernel, len(tokens)),
         grid_spec=scalars(
-            in_specs=in_vmem(1 + len(tokens)) + anywhere(7),
-            out_specs=tuple(in_vmem(2)),
+            in_specs=anywhere(len(tokens) + 8),
+            out_specs=tuple(anywhere(2)),
             scratch_shapes=[
+                token_scratch,
+                pltpu.VMEM((blocks, half + SUBLANES, LANES), jnp.int32),
                 pltpu.VMEM((3, blocks, channels, LANES), F32),
                 *tables,
                 pltpu.VMEM((SIDES, channels, LANES), F32),
                 buffer,
+                pltpu.VMEM((vocab, half), F32),
+                pltpu.VMEM((vocab, half), F32),
                 work,
                 buffer,
                 buffer,
-                pltpu.SemaphoreType.DMA((9,)),
-                pltpu.VMEM((blocks, LANES), jnp.int32),
+                pltpu.SemaphoreType.DMA((len(tokens) + 12,)),
             ],
         ),
         out_shape=(jax.ShapeDtypeStruct((vocab, half), F32),) * 2,
         compiler_params=pltpu.CompilerParams(vmem_limit_bytes=VMEM_BYTES),
         cost_estimate=takes(15),
         name="backward",
-    )(place, cot_words, *tokens, streams, response, ahead, back, twist, sides, long_out)
+    )(place, *tokens, cot_words, streams, response, ahead, back, twist, sides, long_out)
     theirs = lax.ppermute(theirs, "fsdp", other_core)
     mixer_out = decode(mixer_words, blocks)
     tall = vocab // 2 + SUBLANES

time: 109 us -> 107 us (0.982)
  Pallas kernels: 54.2 us -> 49.7 us
  waiting for transfers between devices: 8.45 us -> 10.4 us
    pallas_call x2, Pallas kernels: 17.1 us -> 14.2 us  [the longest x1 11.7 us: body(): pl.pallas_call(functools.partial(filter_kernel, half % LANES == 0), grid_...]
    ppermute x21, waiting for transfers between devices: 6.7 us -> 8.61 us  [swap(): return lax.ppermute(part, 'ctx', [(i, i ^ bits) for i in range(16)])]
  transfers between devices with their start and end apart: 25 -> 25, of which waited for: 6 -> 7; matrix products, arithmetic and copies ran while one was open for 1% -> 1% of each run, Pallas kernels for 48% -> 45%
where the time goes in v5:
time: 107 us; the launch traced here: 106 us
  Pallas kernels  49.7 us (46%)
  starting transfers between devices  42.8 us (40%)
  waiting for transfers between devices  10.4 us (10%)
  local copies, waits for them, and re-layouts  1.6 us (1%)
    ppermute x21, starting transfers between devices, swap(): return lax.ppermute(part, 'ctx', [(i, i ^ bits) for i in range(16)])  28.5 us
    pallas_call x1, Pallas kernels, body(): pl.pallas_call(functools.partial(backward_kernel, len(tokens)), grid_spec...  14.9 us
    all_to_all x2, starting transfers between devices, exchange(): return lax.all_to_all(value, 'ctx', split_axis=0, concat_axis=0, tiled=True)  14.2 us
    pallas_call x1, Pallas kernels, body(): pl.pallas_call(functools.partial(forward_kernel, len(tokens)), grid_spec=...  12.9 us
    pallas_call x1, Pallas kernels, body(): pl.pallas_call(functools.partial(filter_kernel, half % LANES == 0), grid_...  11.7 us
    ppermute x21, waiting for transfers between devices, swap(): return lax.ppermute(part, 'ctx', [(i, i ^ bits) for i in range(16)])  8.61 us
    pallas_call x2, Pallas kernels, fill_table(): pl.pallas_call(functools.partial(unpack_square_kernel, aways), grid_spec=...  5 us
    pallas_call x1, Pallas kernels, encode(): pl.pallas_call(encode_kernel, grid=(blocks // some,), in_specs=[pl.BlockS...  2.6 us
  transfers between devices with their start and end apart: 25, of which 7 were waited for; matrix products, arithmetic and copies ran while one was open for 1% of the time, Pallas kernels for 45%

profile of v5, /device:TPU:0, one launch (start us, length us, event | category | flops | bytes accessed | tf_op | source)
XLA Modules:
  0.0 106.1 jit_solution(5118430081405027728)
XLA Ops:
  0.6 0.0 copy-start
  0.6 4.1 %collective-permute-start.2 = (s32[1,128]{1,0:T(1,128)}, s32[1,128]{1,0:T(1,128)S(1)}, u32[]{:S(2)}, u32[]{:S(2)}) collective-permute-start(s32[1,128]{1,0:T(1,128)} %param.11), channel_id=1, source_target_pairs={{0,8},{1,9},{2,10},{3,11},{4,12},{5,13},{6,14},{7,15},{8,0},{9,1},... | collective-permute-start | bytes 1544 | tf_op jit(solution)/shard_map/ppermute | solution.py:729
  4.7 1.6 %collective-permute-start.1 = (s32[1,128]{1,0:T(1,128)}, s32[1,128]{1,0:T(1,128)S(1)}, u32[]{:S(2)}, u32[]{:S(2)}) collective-permute-start(s32[1,128]{1,0:T(1,128)} %param.11), channel_id=1, source_target_pairs={{0,4},{1,5},{2,6},{3,7},{4,0},{5,1},{6,2},{7,3},{8,12},{9,13},{10,... | collective-permute-start | bytes 1544 | tf_op jit(solution)/shard_map/ppermute | solution.py:729
  6.3 0.0 collective-permute-start.3
  6.4 0.1 collective-permute-start
  6.5 2.6 %encode_cotangent.1 = s32[16,136,128]{2,1,0:T(8,128)} custom-call(f32[2,16,128,128]{3,2,1,0:T(8,128)} %bitcast.9), custom_call_target="tpu_custom_call" | custom-call | flops 2000000000 | bytes 6000000 | tf_op jit(solution)/shard_map/encode_cotangent/pallas_call | solution.py:350
  9.1 7.2 %all-to-all-start = ((s32[16,136,128]{2,1,0:T(8,128)}), s32[16,136,128]{2,1,0:T(8,128)S(1)}, u32[]{:S(2)}, u32[]{:S(2)}) async-start(s32[16,136,128]{2,1,0:T(8,128)} %encode_cotangent.1), calls=%async_computation | async-start | bytes 2228224 | tf_op jit(solution)/shard_map/all_to_all | solution.py:765
  16.3 0.6 pad_add_fusion.1.place_ref
  16.9 0.0 collective-permute-done.2
  16.9 0.0 collective-permute-done.1
  16.9 0.0 collective-permute-done.3
  17.0 2.9 %collective-permute-start.6 = (s32[4,128]{1,0:T(4,128)S(1)}, s32[4,128]{1,0:T(4,128)S(1)}, u32[]{:S(2)}, u32[]{:S(2)}) collective-permute-start(s32[4,128]{1,0:T(4,128)S(1)} %pad_add_fusion.refs_0_), channel_id=1, source_target_pairs={{0,3},{1,2},{2,1},{3,0},{4,7},{5,6},{6,5},{7,4},{8,11},{9,10},{10,... | collective-permute-start | bytes 6152 | tf_op jit(solution)/shard_map/ppermute | solution.py:729
  19.8 0.6 collective-permute-start.5
  20.4 0.1 collective-permute-start.4
  20.5 0.0 collective-permute-done.refs_5_
  20.5 11.7 %modal_filter.1 = (f32[17,256,256]{2,1,0:T(8,128)}, f32[10,256,128]{2,1,0:T(8,128)}) custom-call(s32[2]{0:T(128)} %pad_add_fusion.1.place_ref, f32[3,3,4096]{2,1,0:T(4,128)} %tap_in.1, f32[1,4096]{1,0:T(1,128)} %bitcast.13, f32[16,4096]{1,0:T(8,128)} %bitcast.10, f32[16,4096]{1,0:T(8,128)} %bitcast.11, s32[16,4096]{1,0:T(8,128)} %bitcast.12, ...), custom_call_target="tpu_custom_call" | custom-call | flops 15000000512 | bytes 45000000 | tf_op jit(solution)/shard_map/modal_filter/pallas_call | solution.py:788
  32.2 0.0 collective-permute-done.6.refs_3_
  32.2 0.0 collective-permute-done.5.refs_2_
  32.3 0.0 collective-permute-done.4.refs_1_
  32.3 0.5 copy-done.8
  32.8 0.1 copy-done.9
  32.8 0.0 copy-done.10
  32.9 12.9 %forward.1 = (s32[16,136,128]{2,1,0:T(8,128)}, f32[16,256,128]{2,1,0:T(8,128)}, f32[3,16,256,128]{3,2,1,0:T(8,128)}) custom-call(s32[2]{0:T(128)} %pad_add_fusion.1.place_ref, s32[4,128]{1,0:T(4,128)} %copy-done.5, s32[4,128]{1,0:T(4,128)} %copy-done.10, s32[4,128]{1,0:T(4,128)} %copy-done.9, s32[4,128]{1,0:T(4,128)} %copy-done.8, ...), custom_call_target="tpu_custom_call" | custom-call | flops 14000000000 | bytes 42000000 | tf_op jit(solution)/shard_map/forward/pallas_call | solution.py:823
  45.8 0.0 all-to-all-done.refs_4_
  45.8 7.0 %all-to-all-start.1 = ((s32[16,136,128]{2,1,0:T(8,128)}), s32[16,136,128]{2,1,0:T(8,128)}, u32[]{:S(2)}, u32[]{:S(2)}) async-start(s32[16,136,128]{2,1,0:T(8,128)} %get-tuple-element.24), calls=%async_computation.1 | async-start | bytes 2228224 | tf_op jit(solution)/shard_map/all_to_all | solution.py:765
  52.8 14.9 %backward.1 = (f32[512,128]{1,0:T(8,128)}, f32[512,128]{1,0:T(8,128)}) custom-call(s32[2]{0:T(128)} %pad_add_fusion.1.place_ref, s32[4,128]{1,0:T(4,128)} %copy-done.5, s32[4,128]{1,0:T(4,128)} %copy-done.10, s32[4,128]{1,0:T(4,128)} %copy-done.9, s32[4,128]{1,0:T(4,128)} %copy-done.8, s32[16,136,128]{2,1,0:T(8,128)} %copy-done.3, ...), custom_call_target="tpu_custom_call" | custom-call | flops 15000000512 | bytes 45000000 | tf_op jit(solution)/shard_map/backward/pallas_call | solution.py:855
  67.7 0.1 collective-permute-start.7
  67.8 1.7 %collective-permute-done.7.other_ref = f32[512,128]{1,0:T(8,128)S(1)} collective-permute-done((f32[512,128]{1,0:T(8,128)}, f32[512,128]{1,0:T(8,128)S(1)}, u32[]{:S(2)}, u32[]{:S(2)}) %collective-permute-start.7) | collective-permute-done | bytes 262176 | tf_op jit(solution)/shard_map/ppermute | solution.py:880
  69.6 0.9 copy-done.2
  70.5 0.1 pack_table.1.refs_0_
  70.6 1.9 %collective-permute-start.16 = (s32[264,128]{1,0:T(8,128)S(1)}, s32[264,128]{1,0:T(8,128)S(1)}, u32[]{:S(2)}, u32[]{:S(2)}) collective-permute-start(s32[264,128]{1,0:T(8,128)S(1)} %pack_table.1.refs_0_), channel_id=1, source_target_pairs={{0,4},{1,5},{2,6},{3,7},{4,0},{5,1},{6,2},{7,3},{8,12},{9,13},{10,... | collective-permute-start | bytes 405512 | tf_op jit(solution)/shard_map/ppermute | solution.py:737
  72.5 2.4 %collective-permute-start.8 = (s32[264,128]{1,0:T(8,128)S(1)}, s32[264,128]{1,0:T(8,128)S(1)}, u32[]{:S(2)}, u32[]{:S(2)}) collective-permute-start(s32[264,128]{1,0:T(8,128)S(1)} %pack_table.1.refs_0_), channel_id=1, source_target_pairs={{0,8},{1,9},{2,10},{3,11},{4,12},{5,13},{6,14},{7,15},{8,0},{9,1},... | collective-permute-start | bytes 405512 | tf_op jit(solution)/shard_map/ppermute | solution.py:737
  74.9 1.5 %collective-permute-start.14 = (s32[264,128]{1,0:T(8,128)S(1)}, s32[264,128]{1,0:T(8,128)S(1)}, u32[]{:S(2)}, u32[]{:S(2)}) collective-permute-start(s32[264,128]{1,0:T(8,128)S(1)} %pack_table.1.refs_0_), channel_id=1, source_target_pairs={{0,2},{1,3},{2,0},{3,1},{4,6},{5,7},{6,4},{7,5},{8,10},{9,11},{10,... | collective-permute-start | bytes 405512 | tf_op jit(solution)/shard_map/ppermute | solution.py:737
  76.4 1.5 %collective-permute-start.13 = (s32[264,128]{1,0:T(8,128)S(1)}, s32[264,128]{1,0:T(8,128)S(1)}, u32[]{:S(2)}, u32[]{:S(2)}) collective-permute-start(s32[264,128]{1,0:T(8,128)S(1)} %pack_table.1.refs_0_), channel_id=1, source_target_pairs={{0,1},{1,0},{2,3},{3,2},{4,5},{5,4},{6,7},{7,6},{8,9},{9,8},{10,11... | collective-permute-start | bytes 405512 | tf_op jit(solution)/shard_map/ppermute | solution.py:737
  77.8 0.9 collective-permute-done.16.refs_4_
  78.8 1.7 %collective-permute-start.18 = (s32[264,128]{1,0:T(8,128)S(1)}, s32[264,128]{1,0:T(8,128)S(1)}, u32[]{:S(2)}, u32[]{:S(2)}) collective-permute-start(s32[264,128]{1,0:T(8,128)S(1)} %collective-permute-done.16.refs_4_), channel_id=1, source_target_pairs={{0,1},{1,0},{2,3},{3,2},{4,5},{5,4},{6,7},{7,6},{8,9},{9,8},{10,11... | collective-permute-start | bytes 405512 | tf_op jit(solution)/shard_map/ppermute | solution.py:737
  80.4 1.9 %collective-permute-start.17 = (s32[264,128]{1,0:T(8,128)S(1)}, s32[264,128]{1,0:T(8,128)S(1)}, u32[]{:S(2)}, u32[]{:S(2)}) collective-permute-start(s32[264,128]{1,0:T(8,128)S(1)} %collective-permute-done.16.refs_4_), channel_id=1, source_target_pairs={{0,2},{1,3},{2,0},{3,1},{4,6},{5,7},{6,4},{7,5},{8,10},{9,11},{10,... | collective-permute-start | bytes 405512 | tf_op jit(solution)/shard_map/ppermute | solution.py:737
  82.3 2.6 %collective-permute-done.8.refs_8_ = s32[264,128]{1,0:T(8,128)S(1)} collective-permute-done((s32[264,128]{1,0:T(8,128)S(1)}, s32[264,128]{1,0:T(8,128)S(1)}, u32[]{:S(2)}, u32[]{:S(2)}) %collective-permute-start.8) | collective-permute-done | bytes 135200 | tf_op jit(solution)/shard_map/ppermute | solution.py:737
  84.9 1.5 %collective-permute-start.20 = (s32[264,128]{1,0:T(8,128)S(1)}, s32[264,128]{1,0:T(8,128)S(1)}, u32[]{:S(2)}, u32[]{:S(2)}) collective-permute-start(s32[264,128]{1,0:T(8,128)S(1)} %collective-permute-done.8.refs_8_), channel_id=1, source_target_pairs={{0,1},{1,0},{2,3},{3,2},{4,5},{5,4},{6,7},{7,6},{8,9},{9,8},{10,11... | collective-permute-start | bytes 405512 | tf_op jit(solution)/shard_map/ppermute | solution.py:737
  86.4 0.0 collective-permute-done.14.refs_2_
  86.4 0.0 collective-permute-start.9
  86.4 0.0 collective-permute-done.13.refs_1_
  86.4 1.7 %collective-permute-start.21 = (s32[264,128]{1,0:T(8,128)S(1)}, s32[264,128]{1,0:T(8,128)}, u32[]{:S(2)}, u32[]{:S(2)}) collective-permute-start(s32[264,128]{1,0:T(8,128)S(1)} %collective-permute-done.8.refs_8_), channel_id=1, source_target_pairs={{0,2},{1,3},{2,0},{3,1},{4,6},{5,7},{6,4},{7,5},{8,10},{9,11},{10,... | collective-permute-start | bytes 405512 | tf_op jit(solution)/shard_map/ppermute | solution.py:737
  88.1 0.0 collective-permute-done.18.refs_6_
  88.1 0.4 collective-permute-start.15
  88.5 0.0 collective-permute-done.17.refs_5_
  88.5 0.6 collective-permute-start.19
  89.0 1.5 %collective-permute-done.20.refs_9_ = s32[264,128]{1,0:T(8,128)S(1)} collective-permute-done((s32[264,128]{1,0:T(8,128)S(1)}, s32[264,128]{1,0:T(8,128)S(1)}, u32[]{:S(2)}, u32[]{:S(2)}) %collective-permute-start.20) | collective-permute-done | bytes 135200 | tf_op jit(solution)/shard_map/ppermute | solution.py:737
  90.6 1.6 %collective-permute-start.22 = (s32[264,128]{1,0:T(8,128)S(1)}, s32[264,128]{1,0:T(8,128)}, u32[]{:S(2)}, u32[]{:S(2)}) collective-permute-start(s32[264,128]{1,0:T(8,128)S(1)} %collective-permute-done.20.refs_9_), channel_id=1, source_target_pairs={{0,2},{1,3},{2,0},{3,1},{4,6},{5,7},{6,4},{7,5},{8,10},{9,11},{10,... | collective-permute-start | bytes 405512 | tf_op jit(solution)/shard_map/ppermute | solution.py:737
  92.2 0.0 collective-permute-done.9.refs_0_
  92.2 0.8 collective-permute-start.10
  93.0 0.0 all-to-all-done.1.held_ref
  93.0 2.5 %decode_mixer.1 = f32[2,16,128,128]{3,2,1,0:T(8,128)} custom-call(s32[16,136,128]{2,1,0:T(8,128)} %all-to-all-done.1.held_ref), custom_call_target="tpu_custom_call" | custom-call | flops 2000000000 | bytes 6000000 | tf_op jit(solution)/shard_map/decode_mixer/pallas_call | solution.py:363
  95.5 0.4 collective-permute-done.15.refs_3_
  96.0 1.4 %collective-permute-start.11 = (s32[264,128]{1,0:T(8,128)S(1)}, s32[264,128]{1,0:T(8,128)S(1)}, u32[]{:S(2)}, u32[]{:S(2)}) collective-permute-start(s32[264,128]{1,0:T(8,128)S(1)} %collective-permute-done.9.refs_0_), channel_id=1, source_target_pairs={{0,1},{1,0},{2,3},{3,2},{4,5},{5,4},{6,7},{7,6},{8,9},{9,8},{10,11... | collective-permute-start | bytes 405512 | tf_op jit(solution)/shard_map/ppermute | solution.py:737
  97.3 2.1 %collective-permute-done.10.refs_1_ = s32[264,128]{1,0:T(8,128)S(1)} collective-permute-done((s32[264,128]{1,0:T(8,128)S(1)}, s32[264,128]{1,0:T(8,128)S(1)}, u32[]{:S(2)}, u32[]{:S(2)}) %collective-permute-start.10) | collective-permute-done | bytes 135200 | tf_op jit(solution)/shard_map/ppermute | solution.py:737
  99.4 0.6 collective-permute-start.12
  99.9 0.0 collective-permute-done.21.refs_10_
  99.9 0.0 collective-permute-done.19.refs_7_
  100.0 0.0 collective-permute-done.22.refs_11_
  100.0 3.4 %unpack_table.2.refs_4_ = f32[512,2048]{1,0:T(8,128)} custom-call(s32[2]{0:T(128)S(1)} %copy-done.1, s32[264,128]{1,0:T(8,128)S(1)} %pack_table.1.refs_0_, s32[264,128]{1,0:T(8,128)S(1)} %collective-permute-done.13.refs_1_, s32[264,128]{1,0:T(8,128)S(1)} %collective-permute-done.14.refs_2_, s32[264,128]{1,0:T(8,128)} %collective-permute-done.15.refs_3_, ...), custom_call_target="tpu_custom_call" | custom-call | flops 2500000000 | bytes 7500000 | tf_op jit(solution)/shard_map/unpack_table/pallas_call | solution.py:417
  103.4 0.0 collective-permute-done.11.refs_2_
  103.4 1.0 collective-permute-done.12.refs_3_
  104.4 1.6 %unpack_table.3 = f32[512,2048]{1,0:T(8,128)} custom-call(s32[2]{0:T(128)S(1)} %copy-done.1, s32[264,128]{1,0:T(8,128)S(1)} %collective-permute-done.9.refs_0_, s32[264,128]{1,0:T(8,128)S(1)} %collective-permute-done.10.refs_1_, s32[264,128]{1,0:T(8,128)S(1)} %collective-permute-done.11.refs_2_, ...), custom_call_target="tpu_custom_call", output_to_operand_aliasing={{}: (5, {})} | custom-call | flops 1500000000 | bytes 4500000 | tf_op jit(solution)/shard_map/unpack_table/pallas_call | solution.py:417
  (19 shorter events, 0.1 us)
Async XLA Ops:
  0.6 5.7 %copy-start = (bf16[512,2048]{1,0:T(8,128)(2,1)S(1)}, bf16[512,2048]{1,0:T(8,128)(2,1)}, u32[]{:S(2)}) copy-start(bf16[512,2048]{1,0:T(8,128)(2,1)} %param.12) | copy-start | bytes 6291460
  0.6 16.3 %collective-permute-start.2 = (s32[1,128]{1,0:T(1,128)}, s32[1,128]{1,0:T(1,128)S(1)}, u32[]{:S(2)}, u32[]{:S(2)}) collective-permute-start(s32[1,128]{1,0:T(1,128)} %param.11), channel_id=1, source_target_pairs={{0,8},{1,9},{2,10},{3,11},{4,12},{5,13},{6,14},{7,15},{8,0},{9,1},... | collective-permute-start | bytes 1544 | tf_op jit(solution)/shard_map/ppermute | solution.py:729
  4.7 12.2 %collective-permute-start.1 = (s32[1,128]{1,0:T(1,128)}, s32[1,128]{1,0:T(1,128)S(1)}, u32[]{:S(2)}, u32[]{:S(2)}) collective-permute-start(s32[1,128]{1,0:T(1,128)} %param.11), channel_id=1, source_target_pairs={{0,4},{1,5},{2,6},{3,7},{4,0},{5,1},{6,2},{7,3},{8,12},{9,13},{10,... | collective-permute-start | bytes 1544 | tf_op jit(solution)/shard_map/ppermute | solution.py:729
  6.3 10.6 %collective-permute-start.3 = (s32[1,128]{1,0:T(1,128)}, s32[1,128]{1,0:T(1,128)S(1)}, u32[]{:S(2)}, u32[]{:S(2)}) collective-permute-start(s32[1,128]{1,0:T(1,128)} %param.11), channel_id=1, source_target_pairs={{0,12},{1,13},{2,14},{3,15},{4,8},{5,9},{6,10},{7,11},{8,4},{9,5},... | collective-permute-start | bytes 1544 | tf_op jit(solution)/shard_map/ppermute | solution.py:729
  6.4 2.7 %copy-start.4 = (bf16[512,128]{1,0:T(8,128)(2,1)}, bf16[512,128]{1,0:T(8,128)(2,1)S(1)}, u32[]{:S(2)}) copy-start(bf16[512,128]{1,0:T(8,128)(2,1)S(1)} %constant_dynamic-slice_fusion.refs_4_) | copy-start | bytes 393220
  6.4 14.1 %collective-permute-start = (bf16[512,128]{1,0:T(8,128)(2,1)S(1)}, bf16[512,128]{1,0:T(8,128)(2,1)S(1)}, u32[]{:S(2)}, u32[]{:S(2)}) collective-permute-start(bf16[512,128]{1,0:T(8,128)(2,1)S(1)} %constant_dynamic-slice_fusion.refs_4_), channel_id=1, source_target_pairs={{0,16},{16,0},{1,17},{17,1},{2,18},{18,2},{3,19},{19,3},{4,20},{20... | collective-permute-start | bytes 393224 | tf_op jit(solution)/shard_map/ppermute | solution.py:773
  9.1 7.9 %copy-start.6 = (s32[1,128]{1,0:T(1,128)S(1)}, s32[1,128]{1,0:T(1,128)}, u32[]{:S(2)}) copy-start(s32[1,128]{1,0:T(1,128)} %param.11) | copy-start | bytes 1540
  9.1 36.7 %all-to-all-start = ((s32[16,136,128]{2,1,0:T(8,128)}), s32[16,136,128]{2,1,0:T(8,128)S(1)}, u32[]{:S(2)}, u32[]{:S(2)}) async-start(s32[16,136,128]{2,1,0:T(8,128)} %encode_cotangent.1), calls=%async_computation | async-start | bytes 2228224 | tf_op jit(solution)/shard_map/all_to_all | solution.py:765
  16.9 15.3 %copy-start.5 = (s32[4,128]{1,0:T(4,128)}, s32[4,128]{1,0:T(4,128)S(1)}, u32[]{:S(2)}) copy-start(s32[4,128]{1,0:T(4,128)S(1)} %pad_add_fusion.refs_0_) | copy-start | bytes 6148
  17.0 15.3 %collective-permute-start.6 = (s32[4,128]{1,0:T(4,128)S(1)}, s32[4,128]{1,0:T(4,128)S(1)}, u32[]{:S(2)}, u32[]{:S(2)}) collective-permute-start(s32[4,128]{1,0:T(4,128)S(1)} %pad_add_fusion.refs_0_), channel_id=1, source_target_pairs={{0,3},{1,2},{2,1},{3,0},{4,7},{5,6},{6,5},{7,4},{8,11},{9,10},{10,... | collective-permute-start | bytes 6152 | tf_op jit(solution)/shard_map/ppermute | solution.py:729
  19.8 12.4 %collective-permute-start.5 = (s32[4,128]{1,0:T(4,128)S(1)}, s32[4,128]{1,0:T(4,128)S(1)}, u32[]{:S(2)}, u32[]{:S(2)}) collective-permute-start(s32[4,128]{1,0:T(4,128)S(1)} %pad_add_fusion.refs_0_), channel_id=1, source_target_pairs={{0,2},{1,3},{2,0},{3,1},{4,6},{5,7},{6,4},{7,5},{8,10},{9,11},{10,... | collective-permute-start | bytes 6152 | tf_op jit(solution)/shard_map/ppermute | solution.py:729
  20.4 11.9 %collective-permute-start.4 = (s32[4,128]{1,0:T(4,128)S(1)}, s32[4,128]{1,0:T(4,128)S(1)}, u32[]{:S(2)}, u32[]{:S(2)}) collective-permute-start(s32[4,128]{1,0:T(4,128)S(1)} %pad_add_fusion.refs_0_), channel_id=1, source_target_pairs={{0,1},{1,0},{2,3},{3,2},{4,5},{5,4},{6,7},{7,6},{8,9},{9,8},{10,11... | collective-permute-start | bytes 6152 | tf_op jit(solution)/shard_map/ppermute | solution.py:729
  20.5 11.7 %copy-start.7 = (bf16[512,128]{1,0:T(8,128)(2,1)}, bf16[512,128]{1,0:T(8,128)(2,1)S(1)}, u32[]{:S(2)}) copy-start(bf16[512,128]{1,0:T(8,128)(2,1)S(1)} %collective-permute-done.refs_5_) | copy-start | bytes 393220
  32.2 0.5 copy-start.8
  32.3 0.6 copy-start.9
  32.3 0.6 copy-start.10
  45.8 7.0 %copy-start.3 = (s32[16,136,128]{2,1,0:T(8,128)}, s32[16,136,128]{2,1,0:T(8,128)S(1)}, u32[]{:S(2)}) copy-start(s32[16,136,128]{2,1,0:T(8,128)S(1)} %all-to-all-done.refs_4_) | copy-start | bytes 3342340
  45.8 47.2 %all-to-all-start.1 = ((s32[16,136,128]{2,1,0:T(8,128)}), s32[16,136,128]{2,1,0:T(8,128)}, u32[]{:S(2)}, u32[]{:S(2)}) async-start(s32[16,136,128]{2,1,0:T(8,128)} %get-tuple-element.24), calls=%async_computation.1 | async-start | bytes 2228224 | tf_op jit(solution)/shard_map/all_to_all | solution.py:765
  67.7 1.8 %collective-permute-start.7 = (f32[512,128]{1,0:T(8,128)}, f32[512,128]{1,0:T(8,128)S(1)}, u32[]{:S(2)}, u32[]{:S(2)}) collective-permute-start(f32[512,128]{1,0:T(8,128)} %get-tuple-element.23), channel_id=1, source_target_pairs={{0,16},{16,0},{1,17},{17,1},{2,18},{18,2},{3,19},{19,3},{4,20},{20... | collective-permute-start | bytes 786440 | tf_op jit(solution)/shard_map/ppermute | solution.py:880
  69.5 1.0 copy-start.2
  70.6 29.4 %copy-start.1 = (s32[2]{0:T(128)S(1)}, s32[2]{0:T(128)}, u32[]{:S(2)}) copy-start(s32[2]{0:T(128)} %pad_add_fusion.1.place_ref) | copy-start | bytes 28
  70.6 8.2 %collective-permute-start.16 = (s32[264,128]{1,0:T(8,128)S(1)}, s32[264,128]{1,0:T(8,128)S(1)}, u32[]{:S(2)}, u32[]{:S(2)}) collective-permute-start(s32[264,128]{1,0:T(8,128)S(1)} %pack_table.1.refs_0_), channel_id=1, source_target_pairs={{0,4},{1,5},{2,6},{3,7},{4,0},{5,1},{6,2},{7,3},{8,12},{9,13},{10,... | collective-permute-start | bytes 405512 | tf_op jit(solution)/shard_map/ppermute | solution.py:737
  72.5 12.4 %collective-permute-start.8 = (s32[264,128]{1,0:T(8,128)S(1)}, s32[264,128]{1,0:T(8,128)S(1)}, u32[]{:S(2)}, u32[]{:S(2)}) collective-permute-start(s32[264,128]{1,0:T(8,128)S(1)} %pack_table.1.refs_0_), channel_id=1, source_target_pairs={{0,8},{1,9},{2,10},{3,11},{4,12},{5,13},{6,14},{7,15},{8,0},{9,1},... | collective-permute-start | bytes 405512 | tf_op jit(solution)/shard_map/ppermute | solution.py:737
  74.9 11.5 %collective-permute-start.14 = (s32[264,128]{1,0:T(8,128)S(1)}, s32[264,128]{1,0:T(8,128)S(1)}, u32[]{:S(2)}, u32[]{:S(2)}) collective-permute-start(s32[264,128]{1,0:T(8,128)S(1)} %pack_table.1.refs_0_), channel_id=1, source_target_pairs={{0,2},{1,3},{2,0},{3,1},{4,6},{5,7},{6,4},{7,5},{8,10},{9,11},{10,... | collective-permute-start | bytes 405512 | tf_op jit(solution)/shard_map/ppermute | solution.py:737
  76.4 10.0 %collective-permute-start.13 = (s32[264,128]{1,0:T(8,128)S(1)}, s32[264,128]{1,0:T(8,128)S(1)}, u32[]{:S(2)}, u32[]{:S(2)}) collective-permute-start(s32[264,128]{1,0:T(8,128)S(1)} %pack_table.1.refs_0_), channel_id=1, source_target_pairs={{0,1},{1,0},{2,3},{3,2},{4,5},{5,4},{6,7},{7,6},{8,9},{9,8},{10,11... | collective-permute-start | bytes 405512 | tf_op jit(solution)/shard_map/ppermute | solution.py:737
  78.8 9.3 %collective-permute-start.18 = (s32[264,128]{1,0:T(8,128)S(1)}, s32[264,128]{1,0:T(8,128)S(1)}, u32[]{:S(2)}, u32[]{:S(2)}) collective-permute-start(s32[264,128]{1,0:T(8,128)S(1)} %collective-permute-done.16.refs_4_), channel_id=1, source_target_pairs={{0,1},{1,0},{2,3},{3,2},{4,5},{5,4},{6,7},{7,6},{8,9},{9,8},{10,11... | collective-permute-start | bytes 405512 | tf_op jit(solution)/shard_map/ppermute | solution.py:737
  80.4 8.1 %collective-permute-start.17 = (s32[264,128]{1,0:T(8,128)S(1)}, s32[264,128]{1,0:T(8,128)S(1)}, u32[]{:S(2)}, u32[]{:S(2)}) collective-permute-start(s32[264,128]{1,0:T(8,128)S(1)} %collective-permute-done.16.refs_4_), channel_id=1, source_target_pairs={{0,2},{1,3},{2,0},{3,1},{4,6},{5,7},{6,4},{7,5},{8,10},{9,11},{10,... | collective-permute-start | bytes 405512 | tf_op jit(solution)/shard_map/ppermute | solution.py:737
  84.9 5.7 %collective-permute-start.20 = (s32[264,128]{1,0:T(8,128)S(1)}, s32[264,128]{1,0:T(8,128)S(1)}, u32[]{:S(2)}, u32[]{:S(2)}) collective-permute-start(s32[264,128]{1,0:T(8,128)S(1)} %collective-permute-done.8.refs_8_), channel_id=1, source_target_pairs={{0,1},{1,0},{2,3},{3,2},{4,5},{5,4},{6,7},{7,6},{8,9},{9,8},{10,11... | collective-permute-start | bytes 405512 | tf_op jit(solution)/shard_map/ppermute | solution.py:737
  86.4 5.8 %collective-permute-start.9 = (s32[264,128]{1,0:T(8,128)S(1)}, s32[264,128]{1,0:T(8,128)S(1)}, u32[]{:S(2)}, u32[]{:S(2)}) collective-permute-start(s32[264,128]{1,0:T(8,128)S(1)} %collective-permute-done.8.refs_8_), channel_id=1, source_target_pairs={{0,4},{1,5},{2,6},{3,7},{4,0},{5,1},{6,2},{7,3},{8,12},{9,13},{10,... | collective-permute-start | bytes 405512 | tf_op jit(solution)/shard_map/ppermute | solution.py:737
  86.4 13.6 %collective-permute-start.21 = (s32[264,128]{1,0:T(8,128)S(1)}, s32[264,128]{1,0:T(8,128)}, u32[]{:S(2)}, u32[]{:S(2)}) collective-permute-start(s32[264,128]{1,0:T(8,128)S(1)} %collective-permute-done.8.refs_8_), channel_id=1, source_target_pairs={{0,2},{1,3},{2,0},{3,1},{4,6},{5,7},{6,4},{7,5},{8,10},{9,11},{10,... | collective-permute-start | bytes 405512 | tf_op jit(solution)/shard_map/ppermute | solution.py:737
  88.1 7.9 %collective-permute-start.15 = (s32[264,128]{1,0:T(8,128)S(1)}, s32[264,128]{1,0:T(8,128)}, u32[]{:S(2)}, u32[]{:S(2)}) collective-permute-start(s32[264,128]{1,0:T(8,128)S(1)} %collective-permute-done.13.refs_1_), channel_id=1, source_target_pairs={{0,2},{1,3},{2,0},{3,1},{4,6},{5,7},{6,4},{7,5},{8,10},{9,11},{10,... | collective-permute-start | bytes 405512 | tf_op jit(solution)/shard_map/ppermute | solution.py:737
  88.5 11.5 %collective-permute-start.19 = (s32[264,128]{1,0:T(8,128)S(1)}, s32[264,128]{1,0:T(8,128)}, u32[]{:S(2)}, u32[]{:S(2)}) collective-permute-start(s32[264,128]{1,0:T(8,128)S(1)} %collective-permute-done.17.refs_5_), channel_id=1, source_target_pairs={{0,1},{1,0},{2,3},{3,2},{4,5},{5,4},{6,7},{7,6},{8,9},{9,8},{10,11... | collective-permute-start | bytes 405512 | tf_op jit(solution)/shard_map/ppermute | solution.py:737
  90.6 9.4 %collective-permute-start.22 = (s32[264,128]{1,0:T(8,128)S(1)}, s32[264,128]{1,0:T(8,128)}, u32[]{:S(2)}, u32[]{:S(2)}) collective-permute-start(s32[264,128]{1,0:T(8,128)S(1)} %collective-permute-done.20.refs_9_), channel_id=1, source_target_pairs={{0,2},{1,3},{2,0},{3,1},{4,6},{5,7},{6,4},{7,5},{8,10},{9,11},{10,... | collective-permute-start | bytes 405512 | tf_op jit(solution)/shard_map/ppermute | solution.py:737
  92.2 7.2 %collective-permute-start.10 = (s32[264,128]{1,0:T(8,128)S(1)}, s32[264,128]{1,0:T(8,128)S(1)}, u32[]{:S(2)}, u32[]{:S(2)}) collective-permute-start(s32[264,128]{1,0:T(8,128)S(1)} %collective-permute-done.9.refs_0_), channel_id=1, source_target_pairs={{0,2},{1,3},{2,0},{3,1},{4,6},{5,7},{6,4},{7,5},{8,10},{9,11},{10,... | collective-permute-start | bytes 405512 | tf_op jit(solution)/shard_map/ppermute | solution.py:737
  96.0 7.4 %collective-permute-start.11 = (s32[264,128]{1,0:T(8,128)S(1)}, s32[264,128]{1,0:T(8,128)S(1)}, u32[]{:S(2)}, u32[]{:S(2)}) collective-permute-start(s32[264,128]{1,0:T(8,128)S(1)} %collective-permute-done.9.refs_0_), channel_id=1, source_target_pairs={{0,1},{1,0},{2,3},{3,2},{4,5},{5,4},{6,7},{7,6},{8,9},{9,8},{10,11... | collective-permute-start | bytes 405512 | tf_op jit(solution)/shard_map/ppermute | solution.py:737
  99.4 5.0 %collective-permute-start.12 = (s32[264,128]{1,0:T(8,128)S(1)}, s32[264,128]{1,0:T(8,128)S(1)}, u32[]{:S(2)}, u32[]{:S(2)}) collective-permute-start(s32[264,128]{1,0:T(8,128)S(1)} %collective-permute-done.10.refs_1_), channel_id=1, source_target_pairs={{0,1},{1,0},{2,3},{3,2},{4,5},{5,4},{6,7},{7,6},{8,9},{9,8},{10,11... | collective-permute-start | bytes 405512 | tf_op jit(solution)/shard_map/ppermute | solution.py:737

commit v6 on v5

--- a/solution.py
+++ b/solution.py
@@ -319,12 +319,21 @@
         pl.loop(0, count)(step)
 
 
-def encode_kernel(value_ref, out_ref):
-    height = value_ref.shape[2]
-    for i in range(value_ref.shape[1]):
-        words, code = pack_pair(value_ref[0, i], value_ref[1, i])
-        out_ref[i, :height, :] = words
-        out_ref[i, height:, :] = code
+def encode_kernel(held_ref, words_out_ref, value_ref, words_ref, in_sems, sems):
+    blocks, height = value_ref.shape[1:3]
+    fetches = [pltpu.make_async_copy(held_ref.at[:, i], value_ref.at[:, i], in_sems.at[i]) for i in range(blocks)]
+    for fetch in fetches:
+        fetch.start()
+    copies = []
+    for block in range(blocks):
+        fetches[block].wait()
+        words, code = pack_pair(value_ref[0, block], value_ref[1, block])
+        words_ref[block, :height, :] = words
+        words_ref[block, height:, :] = code
+        copies.append(pltpu.make_async_copy(words_ref.at[block], words_out_ref.at[block], sems.at[block]))
+        copies[-1].start()
+    for copy in copies:
+        copy.wait()
 
 
 def decode_kernel(held_ref, out_ref, words_ref, value_ref, in_sems, sems):
@@ -346,13 +355,19 @@
 
 def encode(value, blocks):
     half = value.shape[0] // 2 // blocks
-    some = blocks // 2
+    words = (blocks, half + SUBLANES, LANES)
     return pl.pallas_call(
         encode_kernel,
-        grid=(blocks // some,),
-        in_specs=[pl.BlockSpec((2, some, half, LANES), lambda i: (0, i, 0, 0))],
-        out_specs=pl.BlockSpec((some, half + SUBLANES, LANES), lambda i: (i, 0, 0)),
-        out_shape=jax.ShapeDtypeStruct((blocks, half + SUBLANES, LANES), jnp.int32),
+        in_specs=anywhere(1),
+        out_specs=anywhere(1)[0],
+        out_shape=jax.ShapeDtypeStruct(words, jnp.int32),
+        scratch_shapes=[
+            pltpu.VMEM((2, blocks, half, LANES), F32),
+            pltpu.VMEM(words, jnp.int32),
+            pltpu.SemaphoreType.DMA((blocks,)),
+            pltpu.SemaphoreType.DMA((blocks,)),
+        ],
+        compiler_params=pltpu.CompilerParams(vmem_limit_bytes=VMEM_BYTES),
         cost_estimate=takes(2),
         name="encode_cotangent",
     )(value.reshape(2, blocks, half, LANES))
@@ -405,7 +420,7 @@
         upper, lower = unpack_pair(ref[:half, :], ref[half : half + 1, :])
         table_ref[slot, :half, :] = upper
         table_ref[slot, half:, :] = lower
-        place = pl.ds(pl.multiple_of((place_ref[0] ^ away) * LANES, LANES), LANES)
+        place = pl.ds(pl.multiple_of(((place_ref[0] >> 1) ^ away) * LANES, LANES), LANES)
         copies.append(pltpu.make_async_copy(table_ref.at[slot], out_ref.at[:, place], sems.at[slot]))
         copies[-1].start()
     for copy in copies:
@@ -434,7 +449,7 @@
 def token_row(token_ref, block, place_ref):
     if token_ref.shape[0] == 1:
         return token_ref[0, block : block + 1, :]
-    away = place_ref[0] ^ block
+    away = (place_ref[0] >> 1) ^ block
     return token_ref[away & 3, pl.ds(away >> 2, 1), :]
 
 
@@ -454,7 +469,7 @@
     modes = residue_ref.shape[1]
     copies = []
     for index in range(2):
-        first = pl.multiple_of((index * blocks + place_ref[0]) * half, half)
+        first = pl.multiple_of((index * blocks + (place_ref[0] >> 1)) * half, half)
         for held, ref in (
             (residue_in, residue_ref),
             (decay_in, decay_ref),
@@ -563,14 +578,19 @@
     for copy in copies:
         copy.start()
     stream_copy = pltpu.make_async_copy(stream_ref, stream_out_ref, sems.at[count])
-    long_copy = pltpu.make_async_copy(long_ref, long_out_ref, sems.at[count + 1])
     blocks, channels, _ = x_ref.shape
     half = channels // 2
+    long_copies = []
+    for index in range(2):
+        rows = pl.ds(index * half, half)
+        long_copies.append(
+            pltpu.make_async_copy(long_ref.at[:, rows], long_out_ref.at[:, rows], sems.at[count + 1 + index])
+        )
     vocab = own_ref.shape[0]
     for copy in copies[: pieces + 2]:
         copy.wait()
     own, other = own_ref[...].astype(F32).T, other_ref[...].astype(F32).T
-    first = place_ref[1] == 0
+    first = (place_ref[0] & 1) == 0
     tall = jnp.concatenate([jnp.where(first, own, other), jnp.where(first, other, own)], axis=0).astype(BF16)
 
     for pair in range(blocks // 2):
@@ -592,7 +612,7 @@
             mixed.append(key * value)
         store_spectrum(work_ref, rows, padded_real_dft(mixed))
 
-    for_tiles(channels, 4, streams)
+    for_tiles(channels, 8, streams)
     stream_copy.start()
     for copy in copies[pieces + 3 :]:
         copy.wait()
@@ -606,8 +626,10 @@
             long_ref[block, rows, :] = long_out
             x_ref[block, rows, :] = stream_ref[0, block, rows, :] * long_out
 
-    for_tiles(channels, 2, results)
-    long_copy.start()
+    for_tiles(half, 2, results)
+    long_copies[0].start()
+    for_tiles(half, 2, lambda rows: results(pl.ds(half + rows.start, SUBLANES)))
+    long_copies[1].start()
 
     def words_copy(block):
         return pltpu.make_async_copy(words_ref.at[block], words_out_ref.at[block], word_sems.at[block])
@@ -620,7 +642,8 @@
     for block in range(blocks):
         words_copy(block).wait()
     stream_copy.wait()
-    long_copy.wait()
+    for copy in long_copies:
+        copy.wait()
 
 
 def backward_kernel(pieces, place_ref, *refs):
@@ -705,7 +728,7 @@
             preferred_element_type=F32,
         )
         total = plus(total, part)
-    first = place_ref[1] == 0
+    first = (place_ref[0] & 1) == 0
     theirs_ref[...] = jnp.where(first, total[:, half:], total[:, :half])
     theirs_copy = pltpu.make_async_copy(theirs_ref, theirs_out_ref, sems.at[count + 2])
     theirs_copy.start()
@@ -741,7 +764,9 @@
         return part, beside, below, swap(beside, second)
 
     eight, four = swap(value, 8), swap(value, 4)
-    parts = (*square(value, 1, 2), *square(four, 2, 1), *square(eight, 1, 2))
+    mine = square(value, 1, 2)
+    eight, across = lax.optimization_barrier((eight, mine[3]))
+    parts = (*mine[:3], across, *square(four, 2, 1), *square(eight, 1, 2))
     *last, mixer_out = lax.optimization_barrier((*square(swap(eight, 4), 2, 1), mixer_out))
     vocab = 2 * (value.shape[0] - SUBLANES)
     table = fill_table((), parts, (0, 1, 2, 3, 4, 6, 5, 7, 8, 9, 10, 11), place, vocab, width)
@@ -758,7 +783,7 @@
     channels = 2 * half
     modes = residues.shape[1]
     slots = blocks + 1
-    place = jnp.stack([rank, side]).astype(jnp.int32)
+    place = jnp.reshape(2 * rank + side, (1,)).astype(jnp.int32)
     other_core = [(0, 1), (1, 0)]
 
     def exchange(value):
@@ -771,7 +796,6 @@
     cot_words = exchange(encode(cotangent[0], blocks))
     own_columns = lax.dynamic_slice_in_dim(embedding, rank * half, half, 1)
     other_columns = lax.ppermute(own_columns, "fsdp", other_core)
-    place, other_columns = lax.optimization_barrier((place, other_columns))
 
     ahead, back, twist = transform_tables(blocks)
     spectra = (slots, channels, 2 * LANES)
@@ -836,7 +860,7 @@
                 pltpu.VMEM((3, blocks, channels, LANES), F32),
                 buffer,
                 work,
-                pltpu.SemaphoreType.DMA((len(tokens) + 9,)),
+                pltpu.SemaphoreType.DMA((len(tokens) + 10,)),
                 pltpu.SemaphoreType.DMA((blocks,)),
             ],
         ),

time: 107 us -> 103 us (0.963)
  Pallas kernels: 49.7 us -> 46.1 us
    pallas_call x1, Pallas kernels: 12.9 us -> 11.7 us  [body(): pl.pallas_call(functools.partial(forward_kernel, len(tokens)), grid_spec=...]
    pallas_call x2, Pallas kernels: 5 us -> 3.92 us  [fill_table(): pl.pallas_call(functools.partial(unpack_square_kernel, aways), grid_spec=...]
  transfers between devices with their start and end apart: 25 -> 25, of which waited for: 7 -> 7; matrix products, arithmetic and copies ran while one was open for 1% -> 0% of each run, Pallas kernels for 45% -> 44%
where the time goes in v6:
time: 103 us; the launch traced here: 102 us
  Pallas kernels  46.1 us (45%)
  starting transfers between devices  42.3 us (41%)
  waiting for transfers between devices  11.2 us (11%)
  local copies, waits for them, and re-layouts  1.67 us (2%)
  between operations  1.1 us (1%)
    ppermute x21, starting transfers between devices, swap(): return lax.ppermute(part, 'ctx', [(i, i ^ bits) for i in range(16)])  28.1 us
    pallas_call x1, Pallas kernels, body(): pl.pallas_call(functools.partial(backward_kernel, len(tokens)), grid_spec...  14.3 us
    all_to_all x2, starting transfers between devices, exchange(): return lax.all_to_all(value, 'ctx', split_axis=0, concat_axis=0, tiled=True)  14.1 us
    pallas_call x1, Pallas kernels, body(): pl.pallas_call(functools.partial(forward_kernel, len(tokens)), grid_spec=...  11.7 us
    pallas_call x1, Pallas kernels, body(): pl.pallas_call(functools.partial(filter_kernel, half % LANES == 0), grid_...  11 us
    ppermute x21, waiting for transfers between devices, swap(): return lax.ppermute(part, 'ctx', [(i, i ^ bits) for i in range(16)])  9.47 us
    pallas_call x2, Pallas kernels, fill_table(): pl.pallas_call(functools.partial(unpack_square_kernel, aways), grid_spec=...  3.92 us
    pallas_call x1, Pallas kernels, encode(): pl.pallas_call(encode_kernel, in_specs=anywhere(1), out_specs=anywhere(1)...  2.68 us
  transfers between devices with their start and end apart: 25, of which 7 were waited for; matrix products, arithmetic and copies ran while one was open for 0% of the time, Pallas kernels for 44%

profile of v6, /device:TPU:0, one launch (start us, length us, event | category | flops | bytes accessed | tf_op | source)
XLA Modules:
  0.0 102.4 jit_solution(7528224496006444522)
XLA Ops:
  0.6 0.0 copy-start
  0.6 4.1 %collective-permute-start.1 = (s32[1,128]{1,0:T(1,128)}, s32[1,128]{1,0:T(1,128)S(1)}, u32[]{:S(2)}, u32[]{:S(2)}) collective-permute-start(s32[1,128]{1,0:T(1,128)} %param.11), channel_id=1, source_target_pairs={{0,8},{1,9},{2,10},{3,11},{4,12},{5,13},{6,14},{7,15},{8,0},{9,1},... | collective-permute-start | bytes 1544 | tf_op jit(solution)/shard_map/ppermute | solution.py:752
  4.7 1.6 %collective-permute-start = (s32[1,128]{1,0:T(1,128)}, s32[1,128]{1,0:T(1,128)S(1)}, u32[]{:S(2)}, u32[]{:S(2)}) collective-permute-start(s32[1,128]{1,0:T(1,128)} %param.11), channel_id=1, source_target_pairs={{0,4},{1,5},{2,6},{3,7},{4,0},{5,1},{6,2},{7,3},{8,12},{9,13},{10,... | collective-permute-start | bytes 1544 | tf_op jit(solution)/shard_map/ppermute | solution.py:752
  6.3 0.0 collective-permute-start.2
  6.4 0.1 collective-permute-start.6
  6.5 2.7 %encode_cotangent.1 = s32[16,136,128]{2,1,0:T(8,128)} custom-call(f32[2,16,128,128]{3,2,1,0:T(8,128)} %bitcast.8), custom_call_target="tpu_custom_call" | custom-call | flops 2000000000 | bytes 6000000 | tf_op jit(solution)/shard_map/encode_cotangent/pallas_call | solution.py:359
  9.2 0.0 copy-start.5
  9.2 7.1 %all-to-all-start = ((s32[16,136,128]{2,1,0:T(8,128)}), s32[16,136,128]{2,1,0:T(8,128)S(1)}, u32[]{:S(2)}, u32[]{:S(2)}) async-start(s32[16,136,128]{2,1,0:T(8,128)} %encode_cotangent.1), calls=%async_computation | async-start | bytes 2228224 | tf_op jit(solution)/shard_map/all_to_all | solution.py:790
  16.3 0.0 collective-permute-done.1
  16.3 0.0 collective-permute-done
  16.3 0.0 collective-permute-done.2
  16.4 2.9 %collective-permute-start.5 = (s32[4,128]{1,0:T(4,128)S(1)}, s32[4,128]{1,0:T(4,128)S(1)}, u32[]{:S(2)}, u32[]{:S(2)}) collective-permute-start(s32[4,128]{1,0:T(4,128)S(1)} %pad_add_fusion.refs_0_), channel_id=1, source_target_pairs={{0,3},{1,2},{2,1},{3,0},{4,7},{5,6},{6,5},{7,4},{8,11},{9,10},{10,... | collective-permute-start | bytes 6152 | tf_op jit(solution)/shard_map/ppermute | solution.py:752
  19.2 0.6 collective-permute-start.4
  19.8 0.1 collective-permute-start.3
  19.9 11.0 %modal_filter.1 = (f32[17,256,256]{2,1,0:T(8,128)}, f32[10,256,128]{2,1,0:T(8,128)}) custom-call(s32[1]{0:T(128)} %bitcast.place_ref, f32[3,3,4096]{2,1,0:T(4,128)} %tap_in.1, f32[1,4096]{1,0:T(1,128)} %bitcast.12, f32[16,4096]{1,0:T(8,128)} %bitcast.9, f32[16,4096]{1,0:T(8,128)} %bitcast.10, s32[16,4096]{1,0:T(8,128)} %bitcast.11, ...), custom_call_target="tpu_custom_call" | custom-call | flops 15000000512 | bytes 45000000 | tf_op jit(solution)/shard_map/modal_filter/pallas_call | solution.py:812
  30.9 0.0 collective-permute-done.5.refs_3_
  31.0 0.0 collective-permute-done.4.refs_2_
  31.0 0.0 collective-permute-done.3.refs_1_
  31.0 0.0 collective-permute-done.6.refs_5_
  31.0 0.5 copy-done.7
  31.5 0.0 copy-done.8
  31.6 0.0 copy-done.9
  31.6 0.1 copy-done.6
  31.7 11.7 %forward.1 = (s32[16,136,128]{2,1,0:T(8,128)}, f32[16,256,128]{2,1,0:T(8,128)}, f32[3,16,256,128]{3,2,1,0:T(8,128)}) custom-call(s32[1]{0:T(128)} %bitcast.place_ref, s32[4,128]{1,0:T(4,128)} %copy-done.4, s32[4,128]{1,0:T(4,128)} %copy-done.9, s32[4,128]{1,0:T(4,128)} %copy-done.8, s32[4,128]{1,0:T(4,128)} %copy-done.7, bf16[512,128]{1,0:T(8,128)(2,1)} %copy-done.3, ...), custom_call_target="tpu_custom_call" | custom-call | flops 14000000000 | bytes 42000000 | tf_op jit(solution)/shard_map/forward/pallas_call | solution.py:847
  43.3 0.0 all-to-all-done.refs_4_
  43.4 7.0 %all-to-all-start.1 = ((s32[16,136,128]{2,1,0:T(8,128)}), s32[16,136,128]{2,1,0:T(8,128)}, u32[]{:S(2)}, u32[]{:S(2)}) async-start(s32[16,136,128]{2,1,0:T(8,128)} %get-tuple-element.23), calls=%async_computation.1 | async-start | bytes 2228224 | tf_op jit(solution)/shard_map/all_to_all | solution.py:790
  50.3 14.3 %backward.1 = (f32[512,128]{1,0:T(8,128)}, f32[512,128]{1,0:T(8,128)}) custom-call(s32[1]{0:T(128)} %bitcast.place_ref, s32[4,128]{1,0:T(4,128)} %copy-done.4, s32[4,128]{1,0:T(4,128)} %copy-done.9, s32[4,128]{1,0:T(4,128)} %copy-done.8, s32[4,128]{1,0:T(4,128)} %copy-done.7, s32[16,136,128]{2,1,0:T(8,128)} %copy-done.2, ...), custom_call_target="tpu_custom_call" | custom-call | flops 15000000512 | bytes 45000000 | tf_op jit(solution)/shard_map/backward/pallas_call | solution.py:879
  64.6 0.1 collective-permute-start.7
  64.7 1.7 %collective-permute-done.7.other_ref = f32[512,128]{1,0:T(8,128)S(1)} collective-permute-done((f32[512,128]{1,0:T(8,128)}, f32[512,128]{1,0:T(8,128)S(1)}, u32[]{:S(2)}, u32[]{:S(2)}) %collective-permute-start.7) | collective-permute-done | bytes 262176 | tf_op jit(solution)/shard_map/ppermute | solution.py:904
  66.4 0.9 copy-done.1
  67.4 0.1 pack_table.1.refs_0_
  67.4 1.9 %collective-permute-start.9 = (s32[264,128]{1,0:T(8,128)S(1)}, s32[264,128]{1,0:T(8,128)S(1)}, u32[]{:S(2)}, u32[]{:S(2)}) collective-permute-start(s32[264,128]{1,0:T(8,128)S(1)} %pack_table.1.refs_0_), channel_id=1, source_target_pairs={{0,1},{1,0},{2,3},{3,2},{4,5},{5,4},{6,7},{7,6},{8,9},{9,8},{10,11... | collective-permute-start | bytes 405512 | tf_op jit(solution)/shard_map/ppermute | solution.py:760
  69.4 1.5 %collective-permute-start.16 = (s32[264,128]{1,0:T(8,128)S(1)}, s32[264,128]{1,0:T(8,128)S(1)}, u32[]{:S(2)}, u32[]{:S(2)}) collective-permute-start(s32[264,128]{1,0:T(8,128)S(1)} %pack_table.1.refs_0_), channel_id=1, source_target_pairs={{0,4},{1,5},{2,6},{3,7},{4,0},{5,1},{6,2},{7,3},{8,12},{9,13},{10,... | collective-permute-start | bytes 405512 | tf_op jit(solution)/shard_map/ppermute | solution.py:760
  70.8 2.4 %collective-permute-start.8 = (s32[264,128]{1,0:T(8,128)S(1)}, s32[264,128]{1,0:T(8,128)S(1)}, u32[]{:S(2)}, u32[]{:S(2)}) collective-permute-start(s32[264,128]{1,0:T(8,128)S(1)} %pack_table.1.refs_0_), channel_id=1, source_target_pairs={{0,8},{1,9},{2,10},{3,11},{4,12},{5,13},{6,14},{7,15},{8,0},{9,1},... | collective-permute-start | bytes 405512 | tf_op jit(solution)/shard_map/ppermute | solution.py:760
  73.2 2.8 %collective-permute-done.9.refs_1_ = s32[264,128]{1,0:T(8,128)S(1)} collective-permute-done((s32[264,128]{1,0:T(8,128)S(1)}, s32[264,128]{1,0:T(8,128)S(1)}, u32[]{:S(2)}, u32[]{:S(2)}) %collective-permute-start.9) | collective-permute-done | bytes 135200 | tf_op jit(solution)/shard_map/ppermute | solution.py:760
  76.0 1.5 %collective-permute-start.10 = (s32[264,128]{1,0:T(8,128)S(1)}, s32[264,128]{1,0:T(8,128)S(1)}, u32[]{:S(2)}, u32[]{:S(2)}) collective-permute-start(s32[264,128]{1,0:T(8,128)S(1)} %collective-permute-done.9.refs_1_), channel_id=1, source_target_pairs={{0,2},{1,3},{2,0},{3,1},{4,6},{5,7},{6,4},{7,5},{8,10},{9,11},{10,... | collective-permute-start | bytes 405512 | tf_op jit(solution)/shard_map/ppermute | solution.py:760
  77.6 0.5 collective-permute-start.15
  78.0 0.0 collective-permute-done.16.refs_4_
  78.0 1.5 %collective-permute-start.17 = (s32[264,128]{1,0:T(8,128)S(1)}, s32[264,128]{1,0:T(8,128)S(1)}, u32[]{:S(2)}, u32[]{:S(2)}) collective-permute-start(s32[264,128]{1,0:T(8,128)S(1)} %collective-permute-done.16.refs_4_), channel_id=1, source_target_pairs={{0,2},{1,3},{2,0},{3,1},{4,6},{5,7},{6,4},{7,5},{8,10},{9,11},{10,... | collective-permute-start | bytes 405512 | tf_op jit(solution)/shard_map/ppermute | solution.py:760
  79.6 2.9 %collective-permute-done.8.refs_8_ = s32[264,128]{1,0:T(8,128)S(1)} collective-permute-done((s32[264,128]{1,0:T(8,128)S(1)}, s32[264,128]{1,0:T(8,128)S(1)}, u32[]{:S(2)}, u32[]{:S(2)}) %collective-permute-start.8) | collective-permute-done | bytes 135200 | tf_op jit(solution)/shard_map/ppermute | solution.py:760
  82.4 0.0 collective-permute-done.10.refs_3_
  82.5 1.5 %collective-permute-start.20 = (s32[264,128]{1,0:T(8,128)S(1)}, s32[264,128]{1,0:T(8,128)S(1)}, u32[]{:S(2)}, u32[]{:S(2)}) collective-permute-start(s32[264,128]{1,0:T(8,128)S(1)} %collective-permute-done.8.refs_8_), channel_id=1, source_target_pairs={{0,1},{1,0},{2,3},{3,2},{4,5},{5,4},{6,7},{7,6},{8,9},{9,8},{10,11... | collective-permute-start | bytes 405512 | tf_op jit(solution)/shard_map/ppermute | solution.py:760
  84.0 1.2 %collective-permute-start.11 = (s32[264,128]{1,0:T(8,128)S(1)}, s32[264,128]{1,0:T(8,128)S(1)}, u32[]{:S(2)}, u32[]{:S(2)}) collective-permute-start(s32[264,128]{1,0:T(8,128)S(1)} %collective-permute-done.8.refs_8_), channel_id=1, source_target_pairs={{0,4},{1,5},{2,6},{3,7},{4,0},{5,1},{6,2},{7,3},{8,12},{9,13},{10,... | collective-permute-start | bytes 405512 | tf_op jit(solution)/shard_map/ppermute | solution.py:760
  85.1 0.0 collective-permute-start.18
  85.1 0.2 collective-permute-done.15.refs_2_
  85.3 1.6 %collective-permute-start.21 = (s32[264,128]{1,0:T(8,128)S(1)}, s32[264,128]{1,0:T(8,128)}, u32[]{:S(2)}, u32[]{:S(2)}) collective-permute-start(s32[264,128]{1,0:T(8,128)S(1)} %collective-permute-done.8.refs_8_), channel_id=1, source_target_pairs={{0,2},{1,3},{2,0},{3,1},{4,6},{5,7},{6,4},{7,5},{8,10},{9,11},{10,... | collective-permute-start | bytes 405512 | tf_op jit(solution)/shard_map/ppermute | solution.py:760
  87.0 0.9 collective-permute-done.17.refs_5_
  87.9 1.9 %collective-permute-start.19 = (s32[264,128]{1,0:T(8,128)S(1)}, s32[264,128]{1,0:T(8,128)}, u32[]{:S(2)}, u32[]{:S(2)}) collective-permute-start(s32[264,128]{1,0:T(8,128)S(1)} %collective-permute-done.17.refs_5_), channel_id=1, source_target_pairs={{0,1},{1,0},{2,3},{3,2},{4,5},{5,4},{6,7},{7,6},{8,9},{9,8},{10,11... | collective-permute-start | bytes 405512 | tf_op jit(solution)/shard_map/ppermute | solution.py:760
  89.8 0.0 collective-permute-done.20.refs_9_
  89.8 0.7 collective-permute-start.22
  90.4 0.0 collective-permute-done.11.refs_0_
  90.4 1.4 %collective-permute-start.12 = (s32[264,128]{1,0:T(8,128)S(1)}, s32[264,128]{1,0:T(8,128)S(1)}, u32[]{:S(2)}, u32[]{:S(2)}) collective-permute-start(s32[264,128]{1,0:T(8,128)S(1)} %collective-permute-done.11.refs_0_), channel_id=1, source_target_pairs={{0,2},{1,3},{2,0},{3,1},{4,6},{5,7},{6,4},{7,5},{8,10},{9,11},{10,... | collective-permute-start | bytes 405512 | tf_op jit(solution)/shard_map/ppermute | solution.py:760
  91.8 0.0 all-to-all-done.1.held_ref
  91.8 2.5 %decode_mixer.1 = f32[2,16,128,128]{3,2,1,0:T(8,128)} custom-call(s32[16,136,128]{2,1,0:T(8,128)} %all-to-all-done.1.held_ref), custom_call_target="tpu_custom_call" | custom-call | flops 2000000000 | bytes 6000000 | tf_op jit(solution)/shard_map/decode_mixer/pallas_call | solution.py:378
  94.3 0.0 collective-permute-done.18.refs_6_
  94.3 0.4 collective-permute-start.13
  94.7 1.5 %collective-permute-done.12.refs_1_ = s32[264,128]{1,0:T(8,128)S(1)} collective-permute-done((s32[264,128]{1,0:T(8,128)S(1)}, s32[264,128]{1,0:T(8,128)S(1)}, u32[]{:S(2)}, u32[]{:S(2)}) %collective-permute-start.12) | collective-permute-done | bytes 135200 | tf_op jit(solution)/shard_map/ppermute | solution.py:760
  96.2 1.0 collective-permute-start.14
  97.2 0.0 collective-permute-done.19.refs_7_
  97.2 0.0 collective-permute-done.21.refs_10_
  97.2 0.0 collective-permute-done.22.refs_11_
  97.2 2.9 %unpack_table.2.refs_4_ = f32[512,2048]{1,0:T(8,128)} custom-call(s32[1]{0:T(128)} %bitcast.place_ref, s32[264,128]{1,0:T(8,128)S(1)} %pack_table.1.refs_0_, s32[264,128]{1,0:T(8,128)S(1)} %collective-permute-done.9.refs_1_, s32[264,128]{1,0:T(8,128)S(1)} %collective-permute-done.15.refs_2_, s32[264,128]{1,0:T(8,128)S(1)} %collective-permute-done.10.refs_3_, ...), custom_call_target="tpu_custom_call" | custom-call | flops 2500000000 | bytes 7500000 | tf_op jit(solution)/shard_map/unpack_table/pallas_call | solution.py:432
  100.1 1.1 %collective-permute-done.14.refs_3_ = s32[264,128]{1,0:T(8,128)S(1)} collective-permute-done((s32[264,128]{1,0:T(8,128)S(1)}, s32[264,128]{1,0:T(8,128)S(1)}, u32[]{:S(2)}, u32[]{:S(2)}) %collective-permute-start.14) | collective-permute-done | bytes 135200 | tf_op jit(solution)/shard_map/ppermute | solution.py:760
  101.2 1.0 %unpack_table.3 = f32[512,2048]{1,0:T(8,128)} custom-call(s32[1]{0:T(128)} %bitcast.place_ref, s32[264,128]{1,0:T(8,128)S(1)} %collective-permute-done.11.refs_0_, s32[264,128]{1,0:T(8,128)S(1)} %collective-permute-done.12.refs_1_, s32[264,128]{1,0:T(8,128)S(1)} %collective-permute-done.13.refs_2_, ...), custom_call_target="tpu_custom_call", output_to_operand_aliasing={{}: (5, {})} | custom-call | flops 1500000000 | bytes 4500000 | tf_op jit(solution)/shard_map/unpack_table/pallas_call | solution.py:432
  (16 shorter events, 0.1 us)
Async XLA Ops:
  0.6 5.7 %copy-start = (bf16[512,2048]{1,0:T(8,128)(2,1)S(1)}, bf16[512,2048]{1,0:T(8,128)(2,1)}, u32[]{:S(2)}) copy-start(bf16[512,2048]{1,0:T(8,128)(2,1)} %param.12) | copy-start | bytes 6291460
  0.6 15.6 %collective-permute-start.1 = (s32[1,128]{1,0:T(1,128)}, s32[1,128]{1,0:T(1,128)S(1)}, u32[]{:S(2)}, u32[]{:S(2)}) collective-permute-start(s32[1,128]{1,0:T(1,128)} %param.11), channel_id=1, source_target_pairs={{0,8},{1,9},{2,10},{3,11},{4,12},{5,13},{6,14},{7,15},{8,0},{9,1},... | collective-permute-start | bytes 1544 | tf_op jit(solution)/shard_map/ppermute | solution.py:752
  4.7 11.5 %collective-permute-start = (s32[1,128]{1,0:T(1,128)}, s32[1,128]{1,0:T(1,128)S(1)}, u32[]{:S(2)}, u32[]{:S(2)}) collective-permute-start(s32[1,128]{1,0:T(1,128)} %param.11), channel_id=1, source_target_pairs={{0,4},{1,5},{2,6},{3,7},{4,0},{5,1},{6,2},{7,3},{8,12},{9,13},{10,... | collective-permute-start | bytes 1544 | tf_op jit(solution)/shard_map/ppermute | solution.py:752
  6.3 10.0 %collective-permute-start.2 = (s32[1,128]{1,0:T(1,128)}, s32[1,128]{1,0:T(1,128)S(1)}, u32[]{:S(2)}, u32[]{:S(2)}) collective-permute-start(s32[1,128]{1,0:T(1,128)} %param.11), channel_id=1, source_target_pairs={{0,12},{1,13},{2,14},{3,15},{4,8},{5,9},{6,10},{7,11},{8,4},{9,5},... | collective-permute-start | bytes 1544 | tf_op jit(solution)/shard_map/ppermute | solution.py:752
  6.4 2.8 %copy-start.3 = (bf16[512,128]{1,0:T(8,128)(2,1)}, bf16[512,128]{1,0:T(8,128)(2,1)S(1)}, u32[]{:S(2)}) copy-start(bf16[512,128]{1,0:T(8,128)(2,1)S(1)} %constant_dynamic-slice_fusion.refs_4_) | copy-start | bytes 393220
  6.4 24.6 %collective-permute-start.6 = (bf16[512,128]{1,0:T(8,128)(2,1)S(1)}, bf16[512,128]{1,0:T(8,128)(2,1)S(1)}, u32[]{:S(2)}, u32[]{:S(2)}) collective-permute-start(bf16[512,128]{1,0:T(8,128)(2,1)S(1)} %constant_dynamic-slice_fusion.refs_4_), channel_id=1, source_target_pairs={{0,16},{16,0},{1,17},{17,1},{2,18},{18,2},{3,19},{19,3},{4,20},{20... | collective-permute-start | bytes 393224 | tf_op jit(solution)/shard_map/ppermute | solution.py:798
  9.2 7.2 %copy-start.5 = (s32[1,128]{1,0:T(1,128)S(1)}, s32[1,128]{1,0:T(1,128)}, u32[]{:S(2)}) copy-start(s32[1,128]{1,0:T(1,128)} %param.11) | copy-start | bytes 1540
  9.2 34.2 %all-to-all-start = ((s32[16,136,128]{2,1,0:T(8,128)}), s32[16,136,128]{2,1,0:T(8,128)S(1)}, u32[]{:S(2)}, u32[]{:S(2)}) async-start(s32[16,136,128]{2,1,0:T(8,128)} %encode_cotangent.1), calls=%async_computation | async-start | bytes 2228224 | tf_op jit(solution)/shard_map/all_to_all | solution.py:790
  16.3 14.6 %copy-start.4 = (s32[4,128]{1,0:T(4,128)}, s32[4,128]{1,0:T(4,128)S(1)}, u32[]{:S(2)}) copy-start(s32[4,128]{1,0:T(4,128)S(1)} %pad_add_fusion.refs_0_) | copy-start | bytes 6148
  16.4 14.6 %collective-permute-start.5 = (s32[4,128]{1,0:T(4,128)S(1)}, s32[4,128]{1,0:T(4,128)S(1)}, u32[]{:S(2)}, u32[]{:S(2)}) collective-permute-start(s32[4,128]{1,0:T(4,128)S(1)} %pad_add_fusion.refs_0_), channel_id=1, source_target_pairs={{0,3},{1,2},{2,1},{3,0},{4,7},{5,6},{6,5},{7,4},{8,11},{9,10},{10,... | collective-permute-start | bytes 6152 | tf_op jit(solution)/shard_map/ppermute | solution.py:752
  19.2 11.7 %collective-permute-start.4 = (s32[4,128]{1,0:T(4,128)S(1)}, s32[4,128]{1,0:T(4,128)S(1)}, u32[]{:S(2)}, u32[]{:S(2)}) collective-permute-start(s32[4,128]{1,0:T(4,128)S(1)} %pad_add_fusion.refs_0_), channel_id=1, source_target_pairs={{0,2},{1,3},{2,0},{3,1},{4,6},{5,7},{6,4},{7,5},{8,10},{9,11},{10,... | collective-permute-start | bytes 6152 | tf_op jit(solution)/shard_map/ppermute | solution.py:752
  19.8 11.2 %collective-permute-start.3 = (s32[4,128]{1,0:T(4,128)S(1)}, s32[4,128]{1,0:T(4,128)S(1)}, u32[]{:S(2)}, u32[]{:S(2)}) collective-permute-start(s32[4,128]{1,0:T(4,128)S(1)} %pad_add_fusion.refs_0_), channel_id=1, source_target_pairs={{0,1},{1,0},{2,3},{3,2},{4,5},{5,4},{6,7},{7,6},{8,9},{9,8},{10,11... | collective-permute-start | bytes 6152 | tf_op jit(solution)/shard_map/ppermute | solution.py:752
  30.9 0.6 copy-start.7
  31.0 0.6 copy-start.8
  31.0 0.6 copy-start.9
  31.0 0.7 copy-start.6
  43.3 7.0 %copy-start.2 = (s32[16,136,128]{2,1,0:T(8,128)}, s32[16,136,128]{2,1,0:T(8,128)S(1)}, u32[]{:S(2)}) copy-start(s32[16,136,128]{2,1,0:T(8,128)S(1)} %all-to-all-done.refs_4_) | copy-start | bytes 3342340
  43.4 48.4 %all-to-all-start.1 = ((s32[16,136,128]{2,1,0:T(8,128)}), s32[16,136,128]{2,1,0:T(8,128)}, u32[]{:S(2)}, u32[]{:S(2)}) async-start(s32[16,136,128]{2,1,0:T(8,128)} %get-tuple-element.23), calls=%async_computation.1 | async-start | bytes 2228224 | tf_op jit(solution)/shard_map/all_to_all | solution.py:790
  64.6 1.8 %collective-permute-start.7 = (f32[512,128]{1,0:T(8,128)}, f32[512,128]{1,0:T(8,128)S(1)}, u32[]{:S(2)}, u32[]{:S(2)}) collective-permute-start(f32[512,128]{1,0:T(8,128)} %get-tuple-element.21), channel_id=1, source_target_pairs={{0,16},{16,0},{1,17},{17,1},{2,18},{18,2},{3,19},{19,3},{4,20},{20... | collective-permute-start | bytes 786440 | tf_op jit(solution)/shard_map/ppermute | solution.py:904
  66.4 1.0 copy-start.1
  67.4 8.6 %collective-permute-start.9 = (s32[264,128]{1,0:T(8,128)S(1)}, s32[264,128]{1,0:T(8,128)S(1)}, u32[]{:S(2)}, u32[]{:S(2)}) collective-permute-start(s32[264,128]{1,0:T(8,128)S(1)} %pack_table.1.refs_0_), channel_id=1, source_target_pairs={{0,1},{1,0},{2,3},{3,2},{4,5},{5,4},{6,7},{7,6},{8,9},{9,8},{10,11... | collective-permute-start | bytes 405512 | tf_op jit(solution)/shard_map/ppermute | solution.py:760
  69.4 8.7 %collective-permute-start.16 = (s32[264,128]{1,0:T(8,128)S(1)}, s32[264,128]{1,0:T(8,128)S(1)}, u32[]{:S(2)}, u32[]{:S(2)}) collective-permute-start(s32[264,128]{1,0:T(8,128)S(1)} %pack_table.1.refs_0_), channel_id=1, source_target_pairs={{0,4},{1,5},{2,6},{3,7},{4,0},{5,1},{6,2},{7,3},{8,12},{9,13},{10,... | collective-permute-start | bytes 405512 | tf_op jit(solution)/shard_map/ppermute | solution.py:760
  70.8 11.6 %collective-permute-start.8 = (s32[264,128]{1,0:T(8,128)S(1)}, s32[264,128]{1,0:T(8,128)S(1)}, u32[]{:S(2)}, u32[]{:S(2)}) collective-permute-start(s32[264,128]{1,0:T(8,128)S(1)} %pack_table.1.refs_0_), channel_id=1, source_target_pairs={{0,8},{1,9},{2,10},{3,11},{4,12},{5,13},{6,14},{7,15},{8,0},{9,1},... | collective-permute-start | bytes 405512 | tf_op jit(solution)/shard_map/ppermute | solution.py:760
  76.0 6.5 %collective-permute-start.10 = (s32[264,128]{1,0:T(8,128)S(1)}, s32[264,128]{1,0:T(8,128)S(1)}, u32[]{:S(2)}, u32[]{:S(2)}) collective-permute-start(s32[264,128]{1,0:T(8,128)S(1)} %collective-permute-done.9.refs_1_), channel_id=1, source_target_pairs={{0,2},{1,3},{2,0},{3,1},{4,6},{5,7},{6,4},{7,5},{8,10},{9,11},{10,... | collective-permute-start | bytes 405512 | tf_op jit(solution)/shard_map/ppermute | solution.py:760
  77.6 7.8 %collective-permute-start.15 = (s32[264,128]{1,0:T(8,128)S(1)}, s32[264,128]{1,0:T(8,128)S(1)}, u32[]{:S(2)}, u32[]{:S(2)}) collective-permute-start(s32[264,128]{1,0:T(8,128)S(1)} %pack_table.1.refs_0_), channel_id=1, source_target_pairs={{0,2},{1,3},{2,0},{3,1},{4,6},{5,7},{6,4},{7,5},{8,10},{9,11},{10,... | collective-permute-start | bytes 405512 | tf_op jit(solution)/shard_map/ppermute | solution.py:760
  78.0 9.9 %collective-permute-start.17 = (s32[264,128]{1,0:T(8,128)S(1)}, s32[264,128]{1,0:T(8,128)S(1)}, u32[]{:S(2)}, u32[]{:S(2)}) collective-permute-start(s32[264,128]{1,0:T(8,128)S(1)} %collective-permute-done.16.refs_4_), channel_id=1, source_target_pairs={{0,2},{1,3},{2,0},{3,1},{4,6},{5,7},{6,4},{7,5},{8,10},{9,11},{10,... | collective-permute-start | bytes 405512 | tf_op jit(solution)/shard_map/ppermute | solution.py:760
  82.5 7.3 %collective-permute-start.20 = (s32[264,128]{1,0:T(8,128)S(1)}, s32[264,128]{1,0:T(8,128)S(1)}, u32[]{:S(2)}, u32[]{:S(2)}) collective-permute-start(s32[264,128]{1,0:T(8,128)S(1)} %collective-permute-done.8.refs_8_), channel_id=1, source_target_pairs={{0,1},{1,0},{2,3},{3,2},{4,5},{5,4},{6,7},{7,6},{8,9},{9,8},{10,11... | collective-permute-start | bytes 405512 | tf_op jit(solution)/shard_map/ppermute | solution.py:760
  84.0 6.5 %collective-permute-start.11 = (s32[264,128]{1,0:T(8,128)S(1)}, s32[264,128]{1,0:T(8,128)S(1)}, u32[]{:S(2)}, u32[]{:S(2)}) collective-permute-start(s32[264,128]{1,0:T(8,128)S(1)} %collective-permute-done.8.refs_8_), channel_id=1, source_target_pairs={{0,4},{1,5},{2,6},{3,7},{4,0},{5,1},{6,2},{7,3},{8,12},{9,13},{10,... | collective-permute-start | bytes 405512 | tf_op jit(solution)/shard_map/ppermute | solution.py:760
  85.1 9.2 %collective-permute-start.18 = (s32[264,128]{1,0:T(8,128)S(1)}, s32[264,128]{1,0:T(8,128)}, u32[]{:S(2)}, u32[]{:S(2)}) collective-permute-start(s32[264,128]{1,0:T(8,128)S(1)} %collective-permute-done.16.refs_4_), channel_id=1, source_target_pairs={{0,1},{1,0},{2,3},{3,2},{4,5},{5,4},{6,7},{7,6},{8,9},{9,8},{10,11... | collective-permute-start | bytes 405512 | tf_op jit(solution)/shard_map/ppermute | solution.py:760
  85.3 11.9 %collective-permute-start.21 = (s32[264,128]{1,0:T(8,128)S(1)}, s32[264,128]{1,0:T(8,128)}, u32[]{:S(2)}, u32[]{:S(2)}) collective-permute-start(s32[264,128]{1,0:T(8,128)S(1)} %collective-permute-done.8.refs_8_), channel_id=1, source_target_pairs={{0,2},{1,3},{2,0},{3,1},{4,6},{5,7},{6,4},{7,5},{8,10},{9,11},{10,... | collective-permute-start | bytes 405512 | tf_op jit(solution)/shard_map/ppermute | solution.py:760
  87.9 9.3 %collective-permute-start.19 = (s32[264,128]{1,0:T(8,128)S(1)}, s32[264,128]{1,0:T(8,128)}, u32[]{:S(2)}, u32[]{:S(2)}) collective-permute-start(s32[264,128]{1,0:T(8,128)S(1)} %collective-permute-done.17.refs_5_), channel_id=1, source_target_pairs={{0,1},{1,0},{2,3},{3,2},{4,5},{5,4},{6,7},{7,6},{8,9},{9,8},{10,11... | collective-permute-start | bytes 405512 | tf_op jit(solution)/shard_map/ppermute | solution.py:760
  89.8 7.4 %collective-permute-start.22 = (s32[264,128]{1,0:T(8,128)S(1)}, s32[264,128]{1,0:T(8,128)}, u32[]{:S(2)}, u32[]{:S(2)}) collective-permute-start(s32[264,128]{1,0:T(8,128)S(1)} %collective-permute-done.20.refs_9_), channel_id=1, source_target_pairs={{0,2},{1,3},{2,0},{3,1},{4,6},{5,7},{6,4},{7,5},{8,10},{9,11},{10,... | collective-permute-start | bytes 405512 | tf_op jit(solution)/shard_map/ppermute | solution.py:760
  90.4 5.8 %collective-permute-start.12 = (s32[264,128]{1,0:T(8,128)S(1)}, s32[264,128]{1,0:T(8,128)S(1)}, u32[]{:S(2)}, u32[]{:S(2)}) collective-permute-start(s32[264,128]{1,0:T(8,128)S(1)} %collective-permute-done.11.refs_0_), channel_id=1, source_target_pairs={{0,2},{1,3},{2,0},{3,1},{4,6},{5,7},{6,4},{7,5},{8,10},{9,11},{10,... | collective-permute-start | bytes 405512 | tf_op jit(solution)/shard_map/ppermute | solution.py:760
  94.3 5.8 %collective-permute-start.13 = (s32[264,128]{1,0:T(8,128)S(1)}, s32[264,128]{1,0:T(8,128)S(1)}, u32[]{:S(2)}, u32[]{:S(2)}) collective-permute-start(s32[264,128]{1,0:T(8,128)S(1)} %collective-permute-done.11.refs_0_), channel_id=1, source_target_pairs={{0,1},{1,0},{2,3},{3,2},{4,5},{5,4},{6,7},{7,6},{8,9},{9,8},{10,11... | collective-permute-start | bytes 405512 | tf_op jit(solution)/shard_map/ppermute | solution.py:760
  96.2 5.0 %collective-permute-start.14 = (s32[264,128]{1,0:T(8,128)S(1)}, s32[264,128]{1,0:T(8,128)S(1)}, u32[]{:S(2)}, u32[]{:S(2)}) collective-permute-start(s32[264,128]{1,0:T(8,128)S(1)} %collective-permute-done.12.refs_1_), channel_id=1, source_target_pairs={{0,1},{1,0},{2,3},{3,2},{4,5},{5,4},{6,7},{7,6},{8,9},{9,8},{10,11... | collective-permute-start | bytes 405512 | tf_op jit(solution)/shard_map/ppermute | solution.py:760

commit v7 on v6

--- a/solution.py
+++ b/solution.py
@@ -665,20 +665,20 @@
     half = channels // 2
     vocab = mine_ref.shape[0]
     words_copy.wait()
+    for copy in tables:
+        copy.start()
 
     for block in range(blocks):
         upper, lower = unpack_pair(words_ref[block, :half, :], words_ref[block, half : half + 1, :])
         cot_ref[block, :half, :] = upper
         cot_ref[block, half:, :] = lower
     query_copy.wait()
-    for copy in tables:
-        copy.start()
 
     def streams(rows):
         late = [cot_ref[block, rows, :] * stream_ref[0, block, rows, :] for block in range(blocks)]
         store_spectrum(work_ref, rows, padded_real_dft(late))
 
-    for_tiles(channels, 4, streams)
+    for_tiles(channels, 8, streams)
     for copy in tables:
         copy.wait()
     for copy in rest:
@@ -712,7 +712,7 @@
             base + jnp.where(lane < LANES - 1, one, 0.0) + jnp.where(lane < LANES - 2, two, 0.0)
         )
 
-    for_tiles(channels, 2, results)
+    for_tiles(channels, 4, results)
 
     total = None
     for start in range(0, blocks, 4):

time: 103 us -> 102 us (level)
  starting transfers between devices: 42.3 us -> 43.5 us
    ppermute x21, starting transfers between devices: 28.1 us -> 29.3 us  [swap(): return lax.ppermute(part, 'ctx', [(i, i ^ bits) for i in range(16)])]
  transfers between devices with their start and end apart: 25 -> 25, of which waited for: 7 -> 6; matrix products, arithmetic and copies ran while one was open for 0% -> 0% of each run, Pallas kernels for 44% -> 43%
where the time goes in v7:
time: 102 us
  Pallas kernels  45.2 us (44%)
  starting transfers between devices  43.5 us (43%)
  waiting for transfers between devices  10.3 us (10%)
  local copies, waits for them, and re-layouts  1.67 us (2%)
  between operations  1.1 us (1%)
    ppermute x21, starting transfers between devices, swap(): return lax.ppermute(part, 'ctx', [(i, i ^ bits) for i in range(16)])  29.3 us
    all_to_all x2, starting transfers between devices, exchange(): return lax.all_to_all(value, 'ctx', split_axis=0, concat_axis=0, tiled=True)  14.1 us
    pallas_call x1, Pallas kernels, body(): pl.pallas_call(functools.partial(backward_kernel, len(tokens)), grid_spec...  13.4 us
    pallas_call x1, Pallas kernels, body(): pl.pallas_call(functools.partial(forward_kernel, len(tokens)), grid_spec=...  11.7 us
    pallas_call x1, Pallas kernels, body(): pl.pallas_call(functools.partial(filter_kernel, half % LANES == 0), grid_...  11 us
    ppermute x21, waiting for transfers between devices, swap(): return lax.ppermute(part, 'ctx', [(i, i ^ bits) for i in range(16)])  8.6 us
    pallas_call x2, Pallas kernels, fill_table(): pl.pallas_call(functools.partial(unpack_square_kernel, aways), grid_spec=...  3.92 us
    pallas_call x1, Pallas kernels, encode(): pl.pallas_call(encode_kernel, in_specs=anywhere(1), out_specs=anywhere(1)...  2.68 us
  transfers between devices with their start and end apart: 25, of which 6 were waited for; matrix products, arithmetic and copies ran while one was open for 0% of the time, Pallas kernels for 43%

profile of v7, /device:TPU:0, one launch (start us, length us, event | category | flops | bytes accessed | tf_op | source)
XLA Modules:
  0.0 101.9 jit_solution(10180755194699863805)
XLA Ops:
  0.6 0.0 copy-start
  0.6 4.1 %collective-permute-start.1 = (s32[1,128]{1,0:T(1,128)}, s32[1,128]{1,0:T(1,128)S(1)}, u32[]{:S(2)}, u32[]{:S(2)}) collective-permute-start(s32[1,128]{1,0:T(1,128)} %param.11), channel_id=1, source_target_pairs={{0,8},{1,9},{2,10},{3,11},{4,12},{5,13},{6,14},{7,15},{8,0},{9,1},... | collective-permute-start | bytes 1544 | tf_op jit(solution)/shard_map/ppermute | solution.py:752
  4.7 1.6 %collective-permute-start = (s32[1,128]{1,0:T(1,128)}, s32[1,128]{1,0:T(1,128)S(1)}, u32[]{:S(2)}, u32[]{:S(2)}) collective-permute-start(s32[1,128]{1,0:T(1,128)} %param.11), channel_id=1, source_target_pairs={{0,4},{1,5},{2,6},{3,7},{4,0},{5,1},{6,2},{7,3},{8,12},{9,13},{10,... | collective-permute-start | bytes 1544 | tf_op jit(solution)/shard_map/ppermute | solution.py:752
  6.3 0.0 collective-permute-start.2
  6.4 0.1 collective-permute-start.6
  6.5 2.7 %encode_cotangent.1 = s32[16,136,128]{2,1,0:T(8,128)} custom-call(f32[2,16,128,128]{3,2,1,0:T(8,128)} %bitcast.8), custom_call_target="tpu_custom_call" | custom-call | flops 2000000000 | bytes 6000000 | tf_op jit(solution)/shard_map/encode_cotangent/pallas_call | solution.py:359
  9.2 0.0 copy-start.5
  9.2 7.1 %all-to-all-start = ((s32[16,136,128]{2,1,0:T(8,128)}), s32[16,136,128]{2,1,0:T(8,128)S(1)}, u32[]{:S(2)}, u32[]{:S(2)}) async-start(s32[16,136,128]{2,1,0:T(8,128)} %encode_cotangent.1), calls=%async_computation | async-start | bytes 2228224 | tf_op jit(solution)/shard_map/all_to_all | solution.py:790
  16.3 0.0 collective-permute-done.1
  16.3 0.0 collective-permute-done
  16.3 0.0 collective-permute-done.2
  16.4 2.9 %collective-permute-start.5 = (s32[4,128]{1,0:T(4,128)S(1)}, s32[4,128]{1,0:T(4,128)S(1)}, u32[]{:S(2)}, u32[]{:S(2)}) collective-permute-start(s32[4,128]{1,0:T(4,128)S(1)} %pad_add_fusion.refs_0_), channel_id=1, source_target_pairs={{0,3},{1,2},{2,1},{3,0},{4,7},{5,6},{6,5},{7,4},{8,11},{9,10},{10,... | collective-permute-start | bytes 6152 | tf_op jit(solution)/shard_map/ppermute | solution.py:752
  19.2 0.6 collective-permute-start.4
  19.8 0.1 collective-permute-start.3
  19.9 11.0 %modal_filter.1 = (f32[17,256,256]{2,1,0:T(8,128)}, f32[10,256,128]{2,1,0:T(8,128)}) custom-call(s32[1]{0:T(128)} %bitcast.place_ref, f32[3,3,4096]{2,1,0:T(4,128)} %tap_in.1, f32[1,4096]{1,0:T(1,128)} %bitcast.12, f32[16,4096]{1,0:T(8,128)} %bitcast.9, f32[16,4096]{1,0:T(8,128)} %bitcast.10, s32[16,4096]{1,0:T(8,128)} %bitcast.11, ...), custom_call_target="tpu_custom_call" | custom-call | flops 15000000512 | bytes 45000000 | tf_op jit(solution)/shard_map/modal_filter/pallas_call | solution.py:812
  30.9 0.0 collective-permute-done.5.refs_3_
  31.0 0.0 collective-permute-done.4.refs_2_
  31.0 0.0 collective-permute-done.3.refs_1_
  31.0 0.0 collective-permute-done.6.refs_5_
  31.0 0.5 copy-done.7
  31.5 0.0 copy-done.8
  31.6 0.0 copy-done.9
  31.6 0.1 copy-done.6
  31.7 11.7 %forward.1 = (s32[16,136,128]{2,1,0:T(8,128)}, f32[16,256,128]{2,1,0:T(8,128)}, f32[3,16,256,128]{3,2,1,0:T(8,128)}) custom-call(s32[1]{0:T(128)} %bitcast.place_ref, s32[4,128]{1,0:T(4,128)} %copy-done.4, s32[4,128]{1,0:T(4,128)} %copy-done.9, s32[4,128]{1,0:T(4,128)} %copy-done.8, s32[4,128]{1,0:T(4,128)} %copy-done.7, bf16[512,128]{1,0:T(8,128)(2,1)} %copy-done.3, ...), custom_call_target="tpu_custom_call" | custom-call | flops 14000000000 | bytes 42000000 | tf_op jit(solution)/shard_map/forward/pallas_call | solution.py:847
  43.3 0.0 all-to-all-done.refs_4_
  43.4 7.0 %all-to-all-start.1 = ((s32[16,136,128]{2,1,0:T(8,128)}), s32[16,136,128]{2,1,0:T(8,128)}, u32[]{:S(2)}, u32[]{:S(2)}) async-start(s32[16,136,128]{2,1,0:T(8,128)} %get-tuple-element.23), calls=%async_computation.1 | async-start | bytes 2228224 | tf_op jit(solution)/shard_map/all_to_all | solution.py:790
  50.3 13.4 %backward.1 = (f32[512,128]{1,0:T(8,128)}, f32[512,128]{1,0:T(8,128)}) custom-call(s32[1]{0:T(128)} %bitcast.place_ref, s32[4,128]{1,0:T(4,128)} %copy-done.4, s32[4,128]{1,0:T(4,128)} %copy-done.9, s32[4,128]{1,0:T(4,128)} %copy-done.8, s32[4,128]{1,0:T(4,128)} %copy-done.7, s32[16,136,128]{2,1,0:T(8,128)} %copy-done.2, ...), custom_call_target="tpu_custom_call" | custom-call | flops 15000000512 | bytes 45000000 | tf_op jit(solution)/shard_map/backward/pallas_call | solution.py:879
  63.7 0.1 collective-permute-start.7
  63.8 1.7 %collective-permute-done.7.other_ref = f32[512,128]{1,0:T(8,128)S(1)} collective-permute-done((f32[512,128]{1,0:T(8,128)}, f32[512,128]{1,0:T(8,128)S(1)}, u32[]{:S(2)}, u32[]{:S(2)}) %collective-permute-start.7) | collective-permute-done | bytes 262176 | tf_op jit(solution)/shard_map/ppermute | solution.py:904
  65.5 0.9 copy-done.1
  66.5 0.1 pack_table.1.refs_0_
  66.6 1.9 %collective-permute-start.9 = (s32[264,128]{1,0:T(8,128)S(1)}, s32[264,128]{1,0:T(8,128)S(1)}, u32[]{:S(2)}, u32[]{:S(2)}) collective-permute-start(s32[264,128]{1,0:T(8,128)S(1)} %pack_table.1.refs_0_), channel_id=1, source_target_pairs={{0,1},{1,0},{2,3},{3,2},{4,5},{5,4},{6,7},{7,6},{8,9},{9,8},{10,11... | collective-permute-start | bytes 405512 | tf_op jit(solution)/shard_map/ppermute | solution.py:760
  68.5 1.5 %collective-permute-start.16 = (s32[264,128]{1,0:T(8,128)S(1)}, s32[264,128]{1,0:T(8,128)S(1)}, u32[]{:S(2)}, u32[]{:S(2)}) collective-permute-start(s32[264,128]{1,0:T(8,128)S(1)} %pack_table.1.refs_0_), channel_id=1, source_target_pairs={{0,4},{1,5},{2,6},{3,7},{4,0},{5,1},{6,2},{7,3},{8,12},{9,13},{10,... | collective-permute-start | bytes 405512 | tf_op jit(solution)/shard_map/ppermute | solution.py:760
  70.0 2.4 %collective-permute-start.8 = (s32[264,128]{1,0:T(8,128)S(1)}, s32[264,128]{1,0:T(8,128)S(1)}, u32[]{:S(2)}, u32[]{:S(2)}) collective-permute-start(s32[264,128]{1,0:T(8,128)S(1)} %pack_table.1.refs_0_), channel_id=1, source_target_pairs={{0,8},{1,9},{2,10},{3,11},{4,12},{5,13},{6,14},{7,15},{8,0},{9,1},... | collective-permute-start | bytes 405512 | tf_op jit(solution)/shard_map/ppermute | solution.py:760
  72.3 2.5 %collective-permute-done.9.refs_1_ = s32[264,128]{1,0:T(8,128)S(1)} collective-permute-done((s32[264,128]{1,0:T(8,128)S(1)}, s32[264,128]{1,0:T(8,128)S(1)}, u32[]{:S(2)}, u32[]{:S(2)}) %collective-permute-start.9) | collective-permute-done | bytes 135200 | tf_op jit(solution)/shard_map/ppermute | solution.py:760
  74.9 1.4 %collective-permute-start.10 = (s32[264,128]{1,0:T(8,128)S(1)}, s32[264,128]{1,0:T(8,128)S(1)}, u32[]{:S(2)}, u32[]{:S(2)}) collective-permute-start(s32[264,128]{1,0:T(8,128)S(1)} %collective-permute-done.9.refs_1_), channel_id=1, source_target_pairs={{0,2},{1,3},{2,0},{3,1},{4,6},{5,7},{6,4},{7,5},{8,10},{9,11},{10,... | collective-permute-start | bytes 405512 | tf_op jit(solution)/shard_map/ppermute | solution.py:760
  76.3 0.6 collective-permute-start.15
  76.9 0.0 collective-permute-done.16.refs_4_
  76.9 1.4 %collective-permute-start.17 = (s32[264,128]{1,0:T(8,128)S(1)}, s32[264,128]{1,0:T(8,128)S(1)}, u32[]{:S(2)}, u32[]{:S(2)}) collective-permute-start(s32[264,128]{1,0:T(8,128)S(1)} %collective-permute-done.16.refs_4_), channel_id=1, source_target_pairs={{0,2},{1,3},{2,0},{3,1},{4,6},{5,7},{6,4},{7,5},{8,10},{9,11},{10,... | collective-permute-start | bytes 405512 | tf_op jit(solution)/shard_map/ppermute | solution.py:760
  78.3 4.1 %collective-permute-done.8.refs_8_ = s32[264,128]{1,0:T(8,128)S(1)} collective-permute-done((s32[264,128]{1,0:T(8,128)S(1)}, s32[264,128]{1,0:T(8,128)S(1)}, u32[]{:S(2)}, u32[]{:S(2)}) %collective-permute-start.8) | collective-permute-done | bytes 135200 | tf_op jit(solution)/shard_map/ppermute | solution.py:760
  82.4 0.0 collective-permute-done.10.refs_3_
  82.4 1.5 %collective-permute-start.20 = (s32[264,128]{1,0:T(8,128)S(1)}, s32[264,128]{1,0:T(8,128)S(1)}, u32[]{:S(2)}, u32[]{:S(2)}) collective-permute-start(s32[264,128]{1,0:T(8,128)S(1)} %collective-permute-done.8.refs_8_), channel_id=1, source_target_pairs={{0,1},{1,0},{2,3},{3,2},{4,5},{5,4},{6,7},{7,6},{8,9},{9,8},{10,11... | collective-permute-start | bytes 405512 | tf_op jit(solution)/shard_map/ppermute | solution.py:760
  83.9 0.0 collective-permute-start.11
  83.9 0.6 collective-permute-start.18
  84.5 0.0 collective-permute-done.15.refs_2_
  84.5 1.7 %collective-permute-start.21 = (s32[264,128]{1,0:T(8,128)S(1)}, s32[264,128]{1,0:T(8,128)}, u32[]{:S(2)}, u32[]{:S(2)}) collective-permute-start(s32[264,128]{1,0:T(8,128)S(1)} %collective-permute-done.8.refs_8_), channel_id=1, source_target_pairs={{0,2},{1,3},{2,0},{3,1},{4,6},{5,7},{6,4},{7,5},{8,10},{9,11},{10,... | collective-permute-start | bytes 405512 | tf_op jit(solution)/shard_map/ppermute | solution.py:760
  86.2 0.0 collective-permute-done.17.refs_5_
  86.2 2.2 %collective-permute-start.19 = (s32[264,128]{1,0:T(8,128)S(1)}, s32[264,128]{1,0:T(8,128)}, u32[]{:S(2)}, u32[]{:S(2)}) collective-permute-start(s32[264,128]{1,0:T(8,128)S(1)} %collective-permute-done.17.refs_5_), channel_id=1, source_target_pairs={{0,1},{1,0},{2,3},{3,2},{4,5},{5,4},{6,7},{7,6},{8,9},{9,8},{10,11... | collective-permute-start | bytes 405512 | tf_op jit(solution)/shard_map/ppermute | solution.py:760
  88.3 0.6 collective-permute-done.20.refs_9_
  89.0 1.7 %collective-permute-start.22 = (s32[264,128]{1,0:T(8,128)S(1)}, s32[264,128]{1,0:T(8,128)}, u32[]{:S(2)}, u32[]{:S(2)}) collective-permute-start(s32[264,128]{1,0:T(8,128)S(1)} %collective-permute-done.20.refs_9_), channel_id=1, source_target_pairs={{0,2},{1,3},{2,0},{3,1},{4,6},{5,7},{6,4},{7,5},{8,10},{9,11},{10,... | collective-permute-start | bytes 405512 | tf_op jit(solution)/shard_map/ppermute | solution.py:760
  90.6 0.0 collective-permute-done.11.refs_0_
  90.6 0.3 collective-permute-start.12
  91.0 0.0 all-to-all-done.1.held_ref
  91.0 2.5 %decode_mixer.1 = f32[2,16,128,128]{3,2,1,0:T(8,128)} custom-call(s32[16,136,128]{2,1,0:T(8,128)} %all-to-all-done.1.held_ref), custom_call_target="tpu_custom_call" | custom-call | flops 2000000000 | bytes 6000000 | tf_op jit(solution)/shard_map/decode_mixer/pallas_call | solution.py:378
  93.5 0.0 collective-permute-done.18.refs_6_
  93.5 1.5 %collective-permute-start.13 = (s32[264,128]{1,0:T(8,128)S(1)}, s32[264,128]{1,0:T(8,128)S(1)}, u32[]{:S(2)}, u32[]{:S(2)}) collective-permute-start(s32[264,128]{1,0:T(8,128)S(1)} %collective-permute-done.11.refs_0_), channel_id=1, source_target_pairs={{0,1},{1,0},{2,3},{3,2},{4,5},{5,4},{6,7},{7,6},{8,9},{9,8},{10,11... | collective-permute-start | bytes 405512 | tf_op jit(solution)/shard_map/ppermute | solution.py:760
  95.0 0.6 collective-permute-done.12.refs_1_
  95.7 1.5 %collective-permute-start.14 = (s32[264,128]{1,0:T(8,128)S(1)}, s32[264,128]{1,0:T(8,128)S(1)}, u32[]{:S(2)}, u32[]{:S(2)}) collective-permute-start(s32[264,128]{1,0:T(8,128)S(1)} %collective-permute-done.12.refs_1_), channel_id=1, source_target_pairs={{0,1},{1,0},{2,3},{3,2},{4,5},{5,4},{6,7},{7,6},{8,9},{9,8},{10,11... | collective-permute-start | bytes 405512 | tf_op jit(solution)/shard_map/ppermute | solution.py:760
  97.1 0.0 collective-permute-done.19.refs_7_
  97.1 0.0 collective-permute-done.21.refs_10_
  97.1 0.0 collective-permute-done.22.refs_11_
  97.1 2.9 %unpack_table.2.refs_4_ = f32[512,2048]{1,0:T(8,128)} custom-call(s32[1]{0:T(128)} %bitcast.place_ref, s32[264,128]{1,0:T(8,128)S(1)} %pack_table.1.refs_0_, s32[264,128]{1,0:T(8,128)S(1)} %collective-permute-done.9.refs_1_, s32[264,128]{1,0:T(8,128)S(1)} %collective-permute-done.15.refs_2_, s32[264,128]{1,0:T(8,128)S(1)} %collective-permute-done.10.refs_3_, ...), custom_call_target="tpu_custom_call" | custom-call | flops 2500000000 | bytes 7500000 | tf_op jit(solution)/shard_map/unpack_table/pallas_call | solution.py:432
  100.0 0.6 collective-permute-done.14.refs_3_
  100.7 1.0 %unpack_table.3 = f32[512,2048]{1,0:T(8,128)} custom-call(s32[1]{0:T(128)} %bitcast.place_ref, s32[264,128]{1,0:T(8,128)S(1)} %collective-permute-done.11.refs_0_, s32[264,128]{1,0:T(8,128)S(1)} %collective-permute-done.12.refs_1_, s32[264,128]{1,0:T(8,128)S(1)} %collective-permute-done.13.refs_2_, ...), custom_call_target="tpu_custom_call", output_to_operand_aliasing={{}: (5, {})} | custom-call | flops 1500000000 | bytes 4500000 | tf_op jit(solution)/shard_map/unpack_table/pallas_call | solution.py:432
  (16 shorter events, 0.1 us)
Async XLA Ops:
  0.6 5.7 %copy-start = (bf16[512,2048]{1,0:T(8,128)(2,1)S(1)}, bf16[512,2048]{1,0:T(8,128)(2,1)}, u32[]{:S(2)}) copy-start(bf16[512,2048]{1,0:T(8,128)(2,1)} %param.12) | copy-start | bytes 6291460
  0.6 15.6 %collective-permute-start.1 = (s32[1,128]{1,0:T(1,128)}, s32[1,128]{1,0:T(1,128)S(1)}, u32[]{:S(2)}, u32[]{:S(2)}) collective-permute-start(s32[1,128]{1,0:T(1,128)} %param.11), channel_id=1, source_target_pairs={{0,8},{1,9},{2,10},{3,11},{4,12},{5,13},{6,14},{7,15},{8,0},{9,1},... | collective-permute-start | bytes 1544 | tf_op jit(solution)/shard_map/ppermute | solution.py:752
  4.7 11.5 %collective-permute-start = (s32[1,128]{1,0:T(1,128)}, s32[1,128]{1,0:T(1,128)S(1)}, u32[]{:S(2)}, u32[]{:S(2)}) collective-permute-start(s32[1,128]{1,0:T(1,128)} %param.11), channel_id=1, source_target_pairs={{0,4},{1,5},{2,6},{3,7},{4,0},{5,1},{6,2},{7,3},{8,12},{9,13},{10,... | collective-permute-start | bytes 1544 | tf_op jit(solution)/shard_map/ppermute | solution.py:752
  6.3 10.0 %collective-permute-start.2 = (s32[1,128]{1,0:T(1,128)}, s32[1,128]{1,0:T(1,128)S(1)}, u32[]{:S(2)}, u32[]{:S(2)}) collective-permute-start(s32[1,128]{1,0:T(1,128)} %param.11), channel_id=1, source_target_pairs={{0,12},{1,13},{2,14},{3,15},{4,8},{5,9},{6,10},{7,11},{8,4},{9,5},... | collective-permute-start | bytes 1544 | tf_op jit(solution)/shard_map/ppermute | solution.py:752
  6.4 2.8 %copy-start.3 = (bf16[512,128]{1,0:T(8,128)(2,1)}, bf16[512,128]{1,0:T(8,128)(2,1)S(1)}, u32[]{:S(2)}) copy-start(bf16[512,128]{1,0:T(8,128)(2,1)S(1)} %constant_dynamic-slice_fusion.refs_4_) | copy-start | bytes 393220
  6.4 24.6 %collective-permute-start.6 = (bf16[512,128]{1,0:T(8,128)(2,1)S(1)}, bf16[512,128]{1,0:T(8,128)(2,1)S(1)}, u32[]{:S(2)}, u32[]{:S(2)}) collective-permute-start(bf16[512,128]{1,0:T(8,128)(2,1)S(1)} %constant_dynamic-slice_fusion.refs_4_), channel_id=1, source_target_pairs={{0,16},{16,0},{1,17},{17,1},{2,18},{18,2},{3,19},{19,3},{4,20},{20... | collective-permute-start | bytes 393224 | tf_op jit(solution)/shard_map/ppermute | solution.py:798
  9.2 7.2 %copy-start.5 = (s32[1,128]{1,0:T(1,128)S(1)}, s32[1,128]{1,0:T(1,128)}, u32[]{:S(2)}) copy-start(s32[1,128]{1,0:T(1,128)} %param.11) | copy-start | bytes 1540
  9.2 34.2 %all-to-all-start = ((s32[16,136,128]{2,1,0:T(8,128)}), s32[16,136,128]{2,1,0:T(8,128)S(1)}, u32[]{:S(2)}, u32[]{:S(2)}) async-start(s32[16,136,128]{2,1,0:T(8,128)} %encode_cotangent.1), calls=%async_computation | async-start | bytes 2228224 | tf_op jit(solution)/shard_map/all_to_all | solution.py:790
  16.3 14.6 %copy-start.4 = (s32[4,128]{1,0:T(4,128)}, s32[4,128]{1,0:T(4,128)S(1)}, u32[]{:S(2)}) copy-start(s32[4,128]{1,0:T(4,128)S(1)} %pad_add_fusion.refs_0_) | copy-start | bytes 6148
  16.4 14.6 %collective-permute-start.5 = (s32[4,128]{1,0:T(4,128)S(1)}, s32[4,128]{1,0:T(4,128)S(1)}, u32[]{:S(2)}, u32[]{:S(2)}) collective-permute-start(s32[4,128]{1,0:T(4,128)S(1)} %pad_add_fusion.refs_0_), channel_id=1, source_target_pairs={{0,3},{1,2},{2,1},{3,0},{4,7},{5,6},{6,5},{7,4},{8,11},{9,10},{10,... | collective-permute-start | bytes 6152 | tf_op jit(solution)/shard_map/ppermute | solution.py:752
  19.2 11.7 %collective-permute-start.4 = (s32[4,128]{1,0:T(4,128)S(1)}, s32[4,128]{1,0:T(4,128)S(1)}, u32[]{:S(2)}, u32[]{:S(2)}) collective-permute-start(s32[4,128]{1,0:T(4,128)S(1)} %pad_add_fusion.refs_0_), channel_id=1, source_target_pairs={{0,2},{1,3},{2,0},{3,1},{4,6},{5,7},{6,4},{7,5},{8,10},{9,11},{10,... | collective-permute-start | bytes 6152 | tf_op jit(solution)/shard_map/ppermute | solution.py:752
  19.8 11.2 %collective-permute-start.3 = (s32[4,128]{1,0:T(4,128)S(1)}, s32[4,128]{1,0:T(4,128)S(1)}, u32[]{:S(2)}, u32[]{:S(2)}) collective-permute-start(s32[4,128]{1,0:T(4,128)S(1)} %pad_add_fusion.refs_0_), channel_id=1, source_target_pairs={{0,1},{1,0},{2,3},{3,2},{4,5},{5,4},{6,7},{7,6},{8,9},{9,8},{10,11... | collective-permute-start | bytes 6152 | tf_op jit(solution)/shard_map/ppermute | solution.py:752
  30.9 0.6 copy-start.7
  31.0 0.6 copy-start.8
  31.0 0.6 copy-start.9
  31.0 0.7 copy-start.6
  43.3 7.0 %copy-start.2 = (s32[16,136,128]{2,1,0:T(8,128)}, s32[16,136,128]{2,1,0:T(8,128)S(1)}, u32[]{:S(2)}) copy-start(s32[16,136,128]{2,1,0:T(8,128)S(1)} %all-to-all-done.refs_4_) | copy-start | bytes 3342340
  43.4 47.6 %all-to-all-start.1 = ((s32[16,136,128]{2,1,0:T(8,128)}), s32[16,136,128]{2,1,0:T(8,128)}, u32[]{:S(2)}, u32[]{:S(2)}) async-start(s32[16,136,128]{2,1,0:T(8,128)} %get-tuple-element.23), calls=%async_computation.1 | async-start | bytes 2228224 | tf_op jit(solution)/shard_map/all_to_all | solution.py:790
  63.7 1.8 %collective-permute-start.7 = (f32[512,128]{1,0:T(8,128)}, f32[512,128]{1,0:T(8,128)S(1)}, u32[]{:S(2)}, u32[]{:S(2)}) collective-permute-start(f32[512,128]{1,0:T(8,128)} %get-tuple-element.21), channel_id=1, source_target_pairs={{0,16},{16,0},{1,17},{17,1},{2,18},{18,2},{3,19},{19,3},{4,20},{20... | collective-permute-start | bytes 786440 | tf_op jit(solution)/shard_map/ppermute | solution.py:904
  65.5 1.0 copy-start.1
  66.6 8.3 %collective-permute-start.9 = (s32[264,128]{1,0:T(8,128)S(1)}, s32[264,128]{1,0:T(8,128)S(1)}, u32[]{:S(2)}, u32[]{:S(2)}) collective-permute-start(s32[264,128]{1,0:T(8,128)S(1)} %pack_table.1.refs_0_), channel_id=1, source_target_pairs={{0,1},{1,0},{2,3},{3,2},{4,5},{5,4},{6,7},{7,6},{8,9},{9,8},{10,11... | collective-permute-start | bytes 405512 | tf_op jit(solution)/shard_map/ppermute | solution.py:760
  68.5 8.4 %collective-permute-start.16 = (s32[264,128]{1,0:T(8,128)S(1)}, s32[264,128]{1,0:T(8,128)S(1)}, u32[]{:S(2)}, u32[]{:S(2)}) collective-permute-start(s32[264,128]{1,0:T(8,128)S(1)} %pack_table.1.refs_0_), channel_id=1, source_target_pairs={{0,4},{1,5},{2,6},{3,7},{4,0},{5,1},{6,2},{7,3},{8,12},{9,13},{10,... | collective-permute-start | bytes 405512 | tf_op jit(solution)/shard_map/ppermute | solution.py:760
  70.0 12.5 %collective-permute-start.8 = (s32[264,128]{1,0:T(8,128)S(1)}, s32[264,128]{1,0:T(8,128)S(1)}, u32[]{:S(2)}, u32[]{:S(2)}) collective-permute-start(s32[264,128]{1,0:T(8,128)S(1)} %pack_table.1.refs_0_), channel_id=1, source_target_pairs={{0,8},{1,9},{2,10},{3,11},{4,12},{5,13},{6,14},{7,15},{8,0},{9,1},... | collective-permute-start | bytes 405512 | tf_op jit(solution)/shard_map/ppermute | solution.py:760
  74.9 7.6 %collective-permute-start.10 = (s32[264,128]{1,0:T(8,128)S(1)}, s32[264,128]{1,0:T(8,128)S(1)}, u32[]{:S(2)}, u32[]{:S(2)}) collective-permute-start(s32[264,128]{1,0:T(8,128)S(1)} %collective-permute-done.9.refs_1_), channel_id=1, source_target_pairs={{0,2},{1,3},{2,0},{3,1},{4,6},{5,7},{6,4},{7,5},{8,10},{9,11},{10,... | collective-permute-start | bytes 405512 | tf_op jit(solution)/shard_map/ppermute | solution.py:760
  76.3 8.2 %collective-permute-start.15 = (s32[264,128]{1,0:T(8,128)S(1)}, s32[264,128]{1,0:T(8,128)S(1)}, u32[]{:S(2)}, u32[]{:S(2)}) collective-permute-start(s32[264,128]{1,0:T(8,128)S(1)} %pack_table.1.refs_0_), channel_id=1, source_target_pairs={{0,2},{1,3},{2,0},{3,1},{4,6},{5,7},{6,4},{7,5},{8,10},{9,11},{10,... | collective-permute-start | bytes 405512 | tf_op jit(solution)/shard_map/ppermute | solution.py:760
  76.9 9.2 %collective-permute-start.17 = (s32[264,128]{1,0:T(8,128)S(1)}, s32[264,128]{1,0:T(8,128)S(1)}, u32[]{:S(2)}, u32[]{:S(2)}) collective-permute-start(s32[264,128]{1,0:T(8,128)S(1)} %collective-permute-done.16.refs_4_), channel_id=1, source_target_pairs={{0,2},{1,3},{2,0},{3,1},{4,6},{5,7},{6,4},{7,5},{8,10},{9,11},{10,... | collective-permute-start | bytes 405512 | tf_op jit(solution)/shard_map/ppermute | solution.py:760
  82.4 6.5 %collective-permute-start.20 = (s32[264,128]{1,0:T(8,128)S(1)}, s32[264,128]{1,0:T(8,128)S(1)}, u32[]{:S(2)}, u32[]{:S(2)}) collective-permute-start(s32[264,128]{1,0:T(8,128)S(1)} %collective-permute-done.8.refs_8_), channel_id=1, source_target_pairs={{0,1},{1,0},{2,3},{3,2},{4,5},{5,4},{6,7},{7,6},{8,9},{9,8},{10,11... | collective-permute-start | bytes 405512 | tf_op jit(solution)/shard_map/ppermute | solution.py:760
  83.9 6.7 %collective-permute-start.11 = (s32[264,128]{1,0:T(8,128)S(1)}, s32[264,128]{1,0:T(8,128)S(1)}, u32[]{:S(2)}, u32[]{:S(2)}) collective-permute-start(s32[264,128]{1,0:T(8,128)S(1)} %collective-permute-done.8.refs_8_), channel_id=1, source_target_pairs={{0,4},{1,5},{2,6},{3,7},{4,0},{5,1},{6,2},{7,3},{8,12},{9,13},{10,... | collective-permute-start | bytes 405512 | tf_op jit(solution)/shard_map/ppermute | solution.py:760
  83.9 9.6 %collective-permute-start.18 = (s32[264,128]{1,0:T(8,128)S(1)}, s32[264,128]{1,0:T(8,128)}, u32[]{:S(2)}, u32[]{:S(2)}) collective-permute-start(s32[264,128]{1,0:T(8,128)S(1)} %collective-permute-done.16.refs_4_), channel_id=1, source_target_pairs={{0,1},{1,0},{2,3},{3,2},{4,5},{5,4},{6,7},{7,6},{8,9},{9,8},{10,11... | collective-permute-start | bytes 405512 | tf_op jit(solution)/shard_map/ppermute | solution.py:760
  84.5 12.7 %collective-permute-start.21 = (s32[264,128]{1,0:T(8,128)S(1)}, s32[264,128]{1,0:T(8,128)}, u32[]{:S(2)}, u32[]{:S(2)}) collective-permute-start(s32[264,128]{1,0:T(8,128)S(1)} %collective-permute-done.8.refs_8_), channel_id=1, source_target_pairs={{0,2},{1,3},{2,0},{3,1},{4,6},{5,7},{6,4},{7,5},{8,10},{9,11},{10,... | collective-permute-start | bytes 405512 | tf_op jit(solution)/shard_map/ppermute | solution.py:760
  86.2 11.0 %collective-permute-start.19 = (s32[264,128]{1,0:T(8,128)S(1)}, s32[264,128]{1,0:T(8,128)}, u32[]{:S(2)}, u32[]{:S(2)}) collective-permute-start(s32[264,128]{1,0:T(8,128)S(1)} %collective-permute-done.17.refs_5_), channel_id=1, source_target_pairs={{0,1},{1,0},{2,3},{3,2},{4,5},{5,4},{6,7},{7,6},{8,9},{9,8},{10,11... | collective-permute-start | bytes 405512 | tf_op jit(solution)/shard_map/ppermute | solution.py:760
  89.0 8.2 %collective-permute-start.22 = (s32[264,128]{1,0:T(8,128)S(1)}, s32[264,128]{1,0:T(8,128)}, u32[]{:S(2)}, u32[]{:S(2)}) collective-permute-start(s32[264,128]{1,0:T(8,128)S(1)} %collective-permute-done.20.refs_9_), channel_id=1, source_target_pairs={{0,2},{1,3},{2,0},{3,1},{4,6},{5,7},{6,4},{7,5},{8,10},{9,11},{10,... | collective-permute-start | bytes 405512 | tf_op jit(solution)/shard_map/ppermute | solution.py:760
  90.6 5.0 %collective-permute-start.12 = (s32[264,128]{1,0:T(8,128)S(1)}, s32[264,128]{1,0:T(8,128)S(1)}, u32[]{:S(2)}, u32[]{:S(2)}) collective-permute-start(s32[264,128]{1,0:T(8,128)S(1)} %collective-permute-done.11.refs_0_), channel_id=1, source_target_pairs={{0,2},{1,3},{2,0},{3,1},{4,6},{5,7},{6,4},{7,5},{8,10},{9,11},{10,... | collective-permute-start | bytes 405512 | tf_op jit(solution)/shard_map/ppermute | solution.py:760
  93.5 6.5 %collective-permute-start.13 = (s32[264,128]{1,0:T(8,128)S(1)}, s32[264,128]{1,0:T(8,128)S(1)}, u32[]{:S(2)}, u32[]{:S(2)}) collective-permute-start(s32[264,128]{1,0:T(8,128)S(1)} %collective-permute-done.11.refs_0_), channel_id=1, source_target_pairs={{0,1},{1,0},{2,3},{3,2},{4,5},{5,4},{6,7},{7,6},{8,9},{9,8},{10,11... | collective-permute-start | bytes 405512 | tf_op jit(solution)/shard_map/ppermute | solution.py:760
  95.7 5.0 %collective-permute-start.14 = (s32[264,128]{1,0:T(8,128)S(1)}, s32[264,128]{1,0:T(8,128)S(1)}, u32[]{:S(2)}, u32[]{:S(2)}) collective-permute-start(s32[264,128]{1,0:T(8,128)S(1)} %collective-permute-done.12.refs_1_), channel_id=1, source_target_pairs={{0,1},{1,0},{2,3},{3,2},{4,5},{5,4},{6,7},{7,6},{8,9},{9,8},{10,11... | collective-permute-start | bytes 405512 | tf_op jit(solution)/shard_map/ppermute | solution.py:760
